TPU v7x, 256 devices: a whole 4x4x8 slice. The times are simulated.
256 devices in a mesh: group: 16 (over y, z_hi), inner: 16 (over z_lo, x, core).
Axes of the slice: x: 4, y: 4, z: 8 (z_hi: 4, z_lo: 2; z = z_hi * 2 + z_lo), core: 2. Of those that a mesh axis runs over, the one named last changes fastest.
Arguments:
- query_rows: bfloat16 [16, 2048, 2560], P('group', 'inner'), may hold values from -6 to 6
- key_rows: bfloat16 [16, 2048, 2560], P('group', 'inner'), may hold values from -6 to 6
- value_rows: bfloat16 [16, 2048, 2560], P('group', 'inner'), may hold values from -6 to 6
- out_rows: bfloat16 [16, 2048, 2560], P('group', 'inner'), may hold values from -6 to 6
- grad_out: bfloat16 [16, 2048, 2560], P('group', 'inner'), may hold values from -6 to 6
- log_sum_exp: float32 [16, 20, 2048], P('group', None, 'inner'), may hold values from 4 to 6
- far_frames: int32 [16, 32, 11], P('group', 'inner'), may hold values from 0 to 15, as said below
- far_blocks: int32 [16, 32, 11], P('group', 'inner'), may hold values from 0 to 7
Outputs:
- grad_query: bfloat16 [16, 2048, 2560], P('group', 'inner')
- grad_key: bfloat16 [16, 2048, 2560], P('group', 'inner')
- grad_value: bfloat16 [16, 2048, 2560], P('group', 'inner')
Inputs may be any that keep to these rules, and one draw needn't show every extreme that they name: `far_frames`: for every query tile the 11 listed frames are distinct and each lies 2 or more frames away from the tile's own frame.
All inputs are finite; a program needn't handle non-finite values.
Results may differ from a plain program's by a relative error of at most 0.0054.
Values may be sent and summed in bfloat16 or wider, within the bound.
No kernel may reach another device: no remote copies, remote signals or barrier semaphores. Data moves between devices by JAX's collectives and lax.ppermute only.
A program may use at most 128 MiB of HBM per device.

v0:
```python
import math

import jax
import jax.numpy as jnp
from jax import lax
from jax.sharding import PartitionSpec as P

TILE = 64
FBLOCK = 8


def extended(shard, sides, width):
    for axis, dim in sides:
        devices, length = (lax.axis_size(axis), shard.shape[dim])
        up = [(i, (i + 1) % devices) for i in range(devices - 1)]
        down = [(j, i) for i, j in up]
        last = lax.slice_in_dim(shard, length - width, length, axis=dim)
        first = lax.slice_in_dim(shard, 0, width, axis=dim)
        before = lax.ppermute(last, axis, up)
        after = lax.ppermute(first, axis, down)
        shard = jnp.concatenate([before, shard, after], axis=dim)
    return shard


def passed_along(block, axis, distance):
    devices = range(lax.axis_size(axis))
    route = [(i - distance, i) for i in devices if i - distance in devices]
    return lax.ppermute(block, axis, route)


def split_heads(row_data, head_count):
    return row_data.reshape(
        row_data.shape[0], row_data.shape[1], head_count, row_data.shape[2] // head_count
    )


def merge_heads(tensor):
    return tensor.reshape(tensor.shape[0], tensor.shape[1], tensor.shape[2] * tensor.shape[3])


def pair_terms(
    query_tiles, grad_tiles, log_tiles, delta_tiles, key_window, value_window, window_mask
):
    head_count = log_tiles.shape[1]
    head_size = query_tiles.shape[2] // head_count
    score_scale = 1.0 / math.sqrt(head_size)
    query_heads = split_heads(query_tiles, head_count)
    grad_heads = split_heads(grad_tiles, head_count)
    key_heads = split_heads(key_window, head_count)
    value_heads = split_heads(value_window, head_count)
    scores = jnp.einsum(
        "bqhd,bkhd->bhqk", query_heads, key_heads, preferred_element_type=jnp.float32
    )
    weights = jnp.exp(scores * score_scale - log_tiles[..., None]) * window_mask[:, None]
    grad_weights = jnp.einsum(
        "bqhd,bkhd->bhqk", grad_heads, value_heads, preferred_element_type=jnp.float32
    )
    grad_scores = (weights * (grad_weights - delta_tiles[..., None])).astype(jnp.bfloat16)
    query_part = None
    key_part = None
    value_part = None
    query_part = merge_heads(
        score_scale
        * jnp.einsum("bhqk,bkhd->bqhd", grad_scores, key_heads, preferred_element_type=jnp.float32)
    )
    weights_low = weights.astype(jnp.bfloat16)
    key_part = merge_heads(
        score_scale
        * jnp.einsum(
            "bhqk,bqhd->bkhd", grad_scores, query_heads, preferred_element_type=jnp.float32
        )
    )
    value_part = merge_heads(
        jnp.einsum("bhqk,bqhd->bkhd", weights_low, grad_heads, preferred_element_type=jnp.float32)
    )
    return (query_part, key_part, value_part)


def build_mask(tile_ids, tiles_total, has_prev, has_next, tile_rows):
    window_slots = jnp.arange(5 * tile_rows, dtype=jnp.int32)
    positions = jnp.arange(tile_rows, dtype=jnp.int32)
    tile_step = window_slots // tile_rows
    offsets = (tile_step - 1) * tile_rows + window_slots % tile_rows
    inside_band = jnp.abs(offsets[:, None] - positions[None, :]) <= tile_rows
    tile_at = tile_ids[:, None] + tile_step[None, :] - 1
    inside_grid = (tile_at >= 0) & (tile_at < tiles_total)
    same_part = (
        (window_slots < 3 * tile_rows)[None, :, None] & inside_band[None] & inside_grid[:, :, None]
    )
    earlier = (window_slots >= 3 * tile_rows) & (window_slots < 4 * tile_rows) & has_prev
    later_slots = (window_slots >= 4 * tile_rows) & has_next
    return (same_part | (earlier | later_slots)[None, :, None]).astype(jnp.float32)


def windows(padded, tile_count, join_axis):
    pieces = (
        padded[1, 0:tile_count],
        padded[1, 1 : tile_count + 1],
        padded[1, 2 : tile_count + 2],
        padded[0, 1 : tile_count + 1],
        padded[2, 1 : tile_count + 1],
    )
    return jnp.concatenate(pieces, axis=join_axis)


def body(query_rows, key_rows, value_rows, out_rows, grad_out, log_sum_exp, far_frames, far_blocks):
    spatial_dev = query_rows.shape[1]
    feature = query_rows.shape[2]
    head_count = log_sum_exp.shape[1]
    tiles_dev = spatial_dev // TILE
    sub_count = TILE // FBLOCK
    far_count = far_frames.shape[2]
    group_count = lax.axis_size("group")
    inner_count = lax.axis_size("inner")
    group_at = lax.axis_index("group")
    inner_at = lax.axis_index("inner")
    delta_rows = jnp.einsum(
        "bshd,bshd->bhs",
        split_heads(grad_out, head_count),
        split_heads(out_rows, head_count),
        preferred_element_type=jnp.float32,
    )
    query_tiles = query_rows.reshape(tiles_dev, TILE, feature)
    grad_tiles = grad_out.reshape(tiles_dev, TILE, feature)
    log_tiles = log_sum_exp.reshape(head_count, tiles_dev, TILE).transpose(1, 0, 2)
    delta_tiles = delta_rows.reshape(head_count, tiles_dev, TILE).transpose(1, 0, 2)
    key_value = jnp.concatenate([key_rows, value_rows], axis=2).reshape(
        1, tiles_dev, TILE, 2 * feature
    )
    tile_ids = inner_at * tiles_dev + jnp.arange(tiles_dev, dtype=jnp.int32)
    pair_mask = build_mask(
        tile_ids, tiles_dev * inner_count, group_at > 0, group_at < group_count - 1, TILE
    )
    key_halo = extended(key_value, (("group", 0), ("inner", 1)), 1)
    key_window = windows(key_halo, tiles_dev, 1)
    near_parts = pair_terms(
        query_tiles,
        grad_tiles,
        log_tiles,
        delta_tiles,
        key_window[..., :feature],
        key_window[..., feature:],
        jnp.transpose(pair_mask, (0, 2, 1)),
    )
    near_query = near_parts[0]
    grad_rows = jnp.concatenate([near_parts[1], near_parts[2]], axis=2)
    lower_part = grad_rows[:, 0:TILE]
    middle = grad_rows[:, TILE : 2 * TILE]
    upper_part = grad_rows[:, 2 * TILE : 3 * TILE]
    padded = (
        jnp.pad(lower_part, ((0, 2), (0, 0), (0, 0)))
        + jnp.pad(middle, ((1, 1), (0, 0), (0, 0)))
        + jnp.pad(upper_part, ((2, 0), (0, 0), (0, 0)))
    )
    own_sums = padded[1 : tiles_dev + 1]
    from_later = passed_along(grad_rows[:, 3 * TILE : 4 * TILE], "group", -1)
    from_earlier = passed_along(grad_rows[:, 4 * TILE :], "group", 1)
    from_right = passed_along(padded[0].astype(jnp.bfloat16), "inner", -1).astype(jnp.float32)
    from_left = passed_along(padded[tiles_dev + 1].astype(jnp.bfloat16), "inner", 1).astype(
        jnp.float32
    )
    own_sums = own_sums + from_later + from_earlier
    own_sums = own_sums.at[tiles_dev - 1].add(from_right).at[0].add(from_left)
    near_sums = own_sums.reshape(spatial_dev, 2 * feature)
    frames_here = far_frames[0]
    blocks_here = far_blocks[0]
    chosen = (frames_here[..., None] == jnp.arange(group_count, dtype=jnp.int32)).astype(jnp.int32)
    request = (jnp.sum(chosen * (blocks_here[..., None] + 1), axis=1) - 1).T
    asked_for = lax.all_to_all(request, "group", split_axis=0, concat_axis=0, tiled=True)
    pick_table = (asked_for[..., None] == jnp.arange(sub_count, dtype=jnp.int32)).astype(
        jnp.bfloat16
    )
    key_blocks = key_value.reshape(tiles_dev, sub_count, FBLOCK * 2 * feature)
    picked = jnp.einsum(
        "scb,cbr->scr", pick_table, key_blocks, preferred_element_type=jnp.float32
    ).astype(jnp.bfloat16)
    far_rows_in = lax.all_to_all(picked, "group", split_axis=0, concat_axis=0, tiled=True)
    choose_low = chosen.astype(jnp.bfloat16)
    far_keys = jnp.einsum(
        "ckd,dcr->ckr", choose_low, far_rows_in, preferred_element_type=jnp.float32
    ).astype(jnp.bfloat16)
    far_keys = far_keys.reshape(tiles_dev, far_count * FBLOCK, 2 * feature)
    all_ones = jnp.ones((tiles_dev, TILE, far_count * FBLOCK), jnp.float32)
    far_parts = pair_terms(
        query_tiles,
        grad_tiles,
        log_tiles,
        delta_tiles,
        far_keys[..., :feature],
        far_keys[..., feature:],
        all_ones,
    )
    far_back = jnp.concatenate([far_parts[1], far_parts[2]], axis=2).astype(jnp.bfloat16)
    far_back = far_back.reshape(tiles_dev, far_count, FBLOCK * 2 * feature)
    send_back = jnp.einsum(
        "ckd,ckr->dcr", choose_low, far_back, preferred_element_type=jnp.float32
    ).astype(jnp.bfloat16)
    returned = lax.all_to_all(send_back, "group", split_axis=0, concat_axis=0, tiled=True)
    far_sums = jnp.einsum("scb,scr->cbr", pick_table, returned, preferred_element_type=jnp.float32)
    total_sums = near_sums + far_sums.reshape(spatial_dev, 2 * feature)
    grad_query = (near_query + far_parts[0]).reshape(1, spatial_dev, feature).astype(jnp.bfloat16)
    grad_key = total_sums[:, :feature].reshape(1, spatial_dev, feature).astype(jnp.bfloat16)
    grad_value = total_sums[:, feature:].reshape(1, spatial_dev, feature).astype(jnp.bfloat16)
    return (grad_query, grad_key, grad_value)


def solution(mesh):
    return jax.shard_map(
        body,
        mesh=mesh,
        in_specs=(
            P("group", "inner", None),
            P("group", "inner", None),
            P("group", "inner", None),
            P("group", "inner", None),
            P("group", "inner", None),
            P("group", None, "inner"),
            P("group", "inner", None),
            P("group", "inner", None),
        ),
        out_specs=(P("group", "inner", None), P("group", "inner", None), P("group", "inner", None)),
        check_vma=False,
    )
```

profile of v0, /device:TPU:23, one launch (start us, length us, event | category | flops | bytes accessed | tf_op | source)
XLA Modules:
  0.0 368.3 jit_solution(8181670400790581247)
XLA Ops:
  3.0 7.8 %collective-permute-start.1 = (bf16[1,2,64,5120]{3,2,1,0:T(8,128)(2,1)S(1)}, bf16[1,2,64,5120]{3,2,1,0:T(8,128)(2,1)S(1)}, u32[]{:S(2)}, u32[]{:S(2)}) collective-permute-start(bf16[1,2,64,5120]{3,2,1,0:T(8,128)(2,1)S(1)} %bitcast.130), channel_id=1, source_target_pairs={{16,0},{32,16},{48,32},{64,48},{80,64},{96,80},{112,96},{128,112},... | collective-permute-start | bytes 3932168 | tf_op jit(solution)/shard_map/ppermute | solution.py:20
  10.8 1.9 collective-permute-start
  12.7 51.9 %collective-permute-done.1 = bf16[1,2,64,5120]{3,2,1,0:T(8,128)(2,1)S(1)} collective-permute-done((bf16[1,2,64,5120]{3,2,1,0:T(8,128)(2,1)S(1)}, bf16[1,2,64,5120]{3,2,1,0:T(8,128)(2,1)S(1)}, u32[]{:S(2)}, u32[]{:S(2)}) %collective-permute-start.1) | collective-permute-done | bytes 1310752 | tf_op jit(solution)/shard_map/ppermute | solution.py:20
  66.3 2.1 fusion.85
  68.4 12.8 %collective-permute-start.2 = (bf16[3,1,64,5120]{3,2,1,0:T(8,128)(2,1)}, bf16[3,1,64,5120]{3,2,1,0:T(8,128)(2,1)}, u32[]{:S(2)}, u32[]{:S(2)}) collective-permute-start(bf16[3,1,64,5120]{3,2,1,0:T(8,128)(2,1)} %get-tuple-element.37), channel_id=1, source_target_pairs={{0,1},{1,2},{2,3},{3,4},{4,5},{5,6},{6,7},{7,8},{8,9},{9,10},{10,1... | collective-permute-start | bytes 5898248 | tf_op jit(solution)/shard_map/ppermute | solution.py:19
  82.0 4.4 %all-to-all-start = ((s32[16,1,2]{2,1,0:T(1,128)}), s32[16,1,2]{2,1,0:T(1,128)S(1)}, u32[]{:S(2)}, u32[]{:S(2)}) async-start(s32[16,1,2]{2,1,0:T(1,128)} %copy.53), calls=%async_computation | async-start | bytes 16384 | tf_op jit(solution)/shard_map/all_to_all | solution.py:169
  86.4 2.2 copy.84
  89.6 1.5 fusion.45
  91.2 1.9 collective-permute-start.3
  93.2 1.3 reshape_reshape.12
  94.5 1.5 reshape_reshape.13
  96.3 1.3 reshape_reshape.11
  97.6 7.0 %all-to-all-done = s32[16,1,2]{2,1,0:T(1,128)S(1)} async-done(((s32[16,1,2]{2,1,0:T(1,128)}), s32[16,1,2]{2,1,0:T(1,128)S(1)}, u32[]{:S(2)}, u32[]{:S(2)}) %all-to-all-start) | async-done | bytes 160 | tf_op jit(solution)/shard_map/all_to_all | solution.py:169
  104.6 2.2 fusion
  106.9 4.2 %copy.55 = bf16[16,2,40960]{2,1,0:T(2,128)(2,1)} copy(bf16[16,2,40960]{2,0,1:T(8,128)(2,1)S(1)} %fusion) | data formatting | bytes 5242880 | tf_op jit(solution)/shard_map/convert_element_type | solution.py:176
  111.1 9.3 %all-to-all-start.1 = ((bf16[16,2,40960]{2,1,0:T(2,128)(2,1)}), bf16[16,2,40960]{2,1,0:T(2,128)(2,1)}, u32[]{:S(2)}, u32[]{:S(2)}) async-start(bf16[16,2,40960]{2,1,0:T(2,128)(2,1)} %copy.55), calls=%async_computation.1 | async-start | bytes 5242880 | tf_op jit(solution)/shard_map/all_to_all | solution.py:177
  121.7 19.4 %collective-permute-done.3 = bf16[3,1,64,5120]{3,2,1,0:T(8,128)(2,1)} collective-permute-done((bf16[3,1,64,5120]{3,2,1,0:T(8,128)(2,1)}, bf16[3,1,64,5120]{3,2,1,0:T(8,128)(2,1)}, u32[]{:S(2)}, u32[]{:S(2)}) %collective-permute-start.3) | collective-permute-done | bytes 1966112 | tf_op jit(solution)/shard_map/ppermute | solution.py:20
  143.6 1.2 fusion.6
  144.8 1.6 fusion.2
  146.5 1.2 copy-done.6
  148.8 1.9 convolution_bitcast_fusion
  150.7 3.6 bitcast_dynamic-update-slice_fusion.1
  154.3 3.6 bitcast_dynamic-update-slice_fusion
  158.0 9.8 %fusion.84 = (f32[2,64,5120]{2,1,0:T(8,128)}, f32[2,64,5120]{2,1,0:T(8,128)}, f32[2,64,5120]{2,1,0:T(8,128)}, f32[2,64,5120]{2,1,0:T(8,128)}, f32[2,64,5120]{2,1,0:T(8,128)}) fusion(f32[2,320,5120]{2,1,0:T(8,128)} %bitcast_dynamic-update-slice_fusion), kind=kLoop, calls=%fused_computation.134 | loop fusion | bytes 26214400 | tf_op jit(solution)/shard_map/slice | solution.py:147
  167.8 3.7 collective-permute-start.5
  171.5 6.9 %collective-permute-start.4 = (f32[2,64,5120]{2,1,0:T(8,128)}, f32[2,64,5120]{2,1,0:T(8,128)}, u32[]{:S(2)}, u32[]{:S(2)}) collective-permute-start(f32[2,64,5120]{2,1,0:T(8,128)} %get-tuple-element.31), channel_id=1, source_target_pairs={{16,0},{32,16},{48,32},{64,48},{80,64},{96,80},{112,96},{128,112},... | collective-permute-start | bytes 7864328 | tf_op jit(solution)/shard_map/ppermute | solution.py:28
  178.3 7.3 %fusion.83 = (bf16[4,64,5120]{2,1,0:T(8,128)(2,1)}, f32[4,64,5120]{2,1,0:T(8,128)}) fusion(f32[2,64,5120]{2,1,0:T(8,128)} %get-tuple-element.32, f32[2,64,5120]{2,1,0:T(8,128)} %get-tuple-element.33, f32[2,64,5120]{2,1,0:T(8,128)} %get-tuple-element.29), kind=kLoop, calls=%fused_computation.133 | loop fusion | flops 3932160 | bytes 15728640 | tf_op jit(solution)/shard_map/convert.11
  185.7 2.9 all-to-all-done.1
  188.5 6.3 %convolution_convert_fusion.1 = bf16[2,11,40960]{2,1,0:T(8,128)(2,1)} fusion(bf16[16,2,40960]{2,1,0:T(2,128)(2,1)} %all-to-all-done.1, s32[2,11]{1,0:T(2,128)S(1)} %bitcast.145), kind=kOutput, calls=%fused_computation.1 | convolution fusion | flops 29738016 | bytes 4423768 | tf_op jit(solution)/shard_map/ckd,dcr->ckr/dot_general | solution.py:179
  194.8 3.6 reshape.316
  198.4 1.7 slice_bitcast_fusion.2
  203.4 1.4 pad_maximum_fusion.1
  204.9 3.6 convert_element_type.101
  208.5 2.6 fusion.1
  211.0 4.2 %copy.73 = bf16[16,2,40960]{2,1,0:T(2,128)(2,1)} copy(bf16[16,2,40960]{2,0,1:T(8,128)(2,1)S(1)} %fusion.1) | data formatting | bytes 5242880 | tf_op jit(solution)/shard_map/convert_element_type | solution.py:197
  215.3 32.4 %all-to-all-start.2 = ((bf16[16,2,40960]{2,1,0:T(2,128)(2,1)}), bf16[16,2,40960]{2,1,0:T(2,128)(2,1)}, u32[]{:S(2)}, u32[]{:S(2)}) async-start(bf16[16,2,40960]{2,1,0:T(2,128)(2,1)} %copy.73), calls=%async_computation.2 | async-start | bytes 5242880 | tf_op jit(solution)/shard_map/all_to_all | solution.py:198
  247.7 2.7 slice_bitcast_fusion.6
  250.4 30.4 %collective-permute-start.7 = (bf16[64,5120]{1,0:T(8,128)(2,1)}, bf16[64,5120]{1,0:T(8,128)(2,1)}, u32[]{:S(2)}, u32[]{:S(2)}) collective-permute-start(bf16[64,5120]{1,0:T(8,128)(2,1)} %get-tuple-element.38), channel_id=1, source_target_pairs={{0,1},{1,2},{2,3},{3,4},{4,5},{5,6},{6,7},{7,8},{8,9},{9,10},{10,1... | collective-permute-start | bytes 1966088 | tf_op jit(solution)/shard_map/ppermute | solution.py:28
  280.8 2.2 collective-permute-start.6
  284.7 1.2 convert_element_type.96
  285.9 44.5 %collective-permute-done.4 = f32[2,64,5120]{2,1,0:T(8,128)} collective-permute-done((f32[2,64,5120]{2,1,0:T(8,128)}, f32[2,64,5120]{2,1,0:T(8,128)}, u32[]{:S(2)}, u32[]{:S(2)}) %collective-permute-start.4) | collective-permute-done | bytes 2621472 | tf_op jit(solution)/shard_map/ppermute | solution.py:28
  330.5 3.7 %fusion.13 = f32[2,64,5120]{2,1,0:T(8,128)S(1)} fusion(f32[2,64,5120]{2,1,0:T(8,128)} %collective-permute-done.5, f32[2,64,5120]{2,1,0:T(8,128)} %collective-permute-done.4, f32[4,64,5120]{2,1,0:T(8,128)} %get-tuple-element.28), kind=kLoop, calls=%fused_computation.27 | loop fusion | flops 1310720 | bytes 10485760 | tf_op jit(solution)/shard_map/add | solution.py:162
  334.2 19.0 %collective-permute-done.6 = bf16[64,5120]{1,0:T(8,128)(2,1)} collective-permute-done((bf16[64,5120]{1,0:T(8,128)(2,1)}, bf16[64,5120]{1,0:T(8,128)(2,1)}, u32[]{:S(2)}, u32[]{:S(2)}) %collective-permute-start.6) | collective-permute-done | bytes 655392 | tf_op jit(solution)/shard_map/ppermute | solution.py:28
  353.2 1.4 fusion.40
  354.6 1.4 fusion.39
  356.0 6.2 %fusion.15 = f32[2,8,40960]{2,1,0:T(8,128)} fusion(bf16[16,2,40960]{2,1,0:T(2,128)(2,1)} %all-to-all-done.2, s32[16,2]{0,1:T(2,128)S(1)} %bitcast.143), kind=kOutput, calls=%fused_computation.30 | convolution fusion | flops 20971776 | bytes 5243008 | tf_op jit(solution)/shard_map/scb,scr->cbr/dot_general | solution.py:199
  362.1 3.1 reshape.326
  365.2 2.0 fusion.14
  (76 shorter events, 17.3 us)
Async XLA Ops:
  0.6 12.1 %copy-start.16 = (s32[1,2,11]{2,1,0:T(2,128)S(1)}, s32[1,2,11]{2,1,0:T(2,128)}, u32[]{:S(2)}) copy-start(s32[1,2,11]{2,1,0:T(2,128)} %param.19) | copy-start | bytes 268
  3.0 61.7 %collective-permute-start.1 = (bf16[1,2,64,5120]{3,2,1,0:T(8,128)(2,1)S(1)}, bf16[1,2,64,5120]{3,2,1,0:T(8,128)(2,1)S(1)}, u32[]{:S(2)}, u32[]{:S(2)}) collective-permute-start(bf16[1,2,64,5120]{3,2,1,0:T(8,128)(2,1)S(1)} %bitcast.130), channel_id=1, source_target_pairs={{16,0},{32,16},{48,32},{64,48},{80,64},{96,80},{112,96},{128,112},... | collective-permute-start | bytes 3932168 | tf_op jit(solution)/shard_map/ppermute | solution.py:20
  10.8 53.8 %collective-permute-start = (bf16[1,2,64,5120]{3,2,1,0:T(8,128)(2,1)S(1)}, bf16[1,2,64,5120]{3,2,1,0:T(8,128)(2,1)S(1)}, u32[]{:S(2)}, u32[]{:S(2)}) collective-permute-start(bf16[1,2,64,5120]{3,2,1,0:T(8,128)(2,1)S(1)} %bitcast.131), channel_id=1, source_target_pairs={{0,16},{16,32},{32,48},{48,64},{64,80},{80,96},{96,112},{112,128},... | collective-permute-start | bytes 3932168 | tf_op jit(solution)/shard_map/ppermute | solution.py:19
  64.6 1.2 copy-start
  66.2 14.9 %copy-start.14 = (s32[1,2,11]{2,1,0:T(2,128)S(1)}, s32[1,2,11]{2,1,0:T(2,128)}, u32[]{:S(2)}) copy-start(s32[1,2,11]{2,1,0:T(2,128)} %param.18) | copy-start | bytes 268
  66.3 22.3 %copy-start.12 = (bf16[1,128,2560]{2,1,0:T(8,128)(2,1)S(1)}, bf16[1,128,2560]{2,1,0:T(8,128)(2,1)}, u32[]{:S(2)}) copy-start(bf16[1,128,2560]{2,1,0:T(8,128)(2,1)} %param.16) | copy-start | bytes 1966084
  68.4 52.0 %collective-permute-start.2 = (bf16[3,1,64,5120]{3,2,1,0:T(8,128)(2,1)}, bf16[3,1,64,5120]{3,2,1,0:T(8,128)(2,1)}, u32[]{:S(2)}, u32[]{:S(2)}) collective-permute-start(bf16[3,1,64,5120]{3,2,1,0:T(8,128)(2,1)} %get-tuple-element.37), channel_id=1, source_target_pairs={{0,1},{1,2},{2,3},{3,4},{4,5},{5,6},{6,7},{7,8},{8,9},{9,10},{10,1... | collective-permute-start | bytes 5898248 | tf_op jit(solution)/shard_map/ppermute | solution.py:19
  82.0 22.6 %all-to-all-start = ((s32[16,1,2]{2,1,0:T(1,128)}), s32[16,1,2]{2,1,0:T(1,128)S(1)}, u32[]{:S(2)}, u32[]{:S(2)}) async-start(s32[16,1,2]{2,1,0:T(1,128)} %copy.53), calls=%async_computation | async-start | bytes 16384 | tf_op jit(solution)/shard_map/all_to_all | solution.py:169
  89.6 6.3 %copy-start.15 = (f32[1,20,128]{2,0,1:T(1,128)S(1)}, f32[1,20,128]{2,0,1:T(1,128)}, u32[]{:S(2)}) copy-start(f32[1,20,128]{2,0,1:T(1,128)} %param.17) | copy-start | bytes 30724
  91.2 49.8 %collective-permute-start.3 = (bf16[3,1,64,5120]{3,2,1,0:T(8,128)(2,1)}, bf16[3,1,64,5120]{3,2,1,0:T(8,128)(2,1)}, u32[]{:S(2)}, u32[]{:S(2)}) collective-permute-start(bf16[3,1,64,5120]{3,2,1,0:T(8,128)(2,1)} %get-tuple-element.36), channel_id=1, source_target_pairs={{1,0},{2,1},{3,2},{4,3},{5,4},{6,5},{7,6},{8,7},{9,8},{10,9},{11,1... | collective-permute-start | bytes 5898248 | tf_op jit(solution)/shard_map/ppermute | solution.py:20
  94.5 1.8 copy-start.13
  111.1 77.5 %all-to-all-start.1 = ((bf16[16,2,40960]{2,1,0:T(2,128)(2,1)}), bf16[16,2,40960]{2,1,0:T(2,128)(2,1)}, u32[]{:S(2)}, u32[]{:S(2)}) async-start(bf16[16,2,40960]{2,1,0:T(2,128)(2,1)} %copy.55), calls=%async_computation.1 | async-start | bytes 5242880 | tf_op jit(solution)/shard_map/all_to_all | solution.py:177
  121.6 19.5 %copy-start.1 = (bf16[1,2,64,5120]{3,2,1,0:T(8,128)(2,1)S(1)}, bf16[1,2,64,5120]{3,2,1,0:T(8,128)(2,1)}, u32[]{:S(2)}) copy-start(bf16[1,2,64,5120]{3,2,1,0:T(8,128)(2,1)} %copy-done) | copy-start | bytes 3932164
  142.4 1.1 copy-start.4
  143.6 1.3 copy-start.2
  146.5 1.3 copy-start.6
  167.8 118.1 %collective-permute-start.5 = (f32[2,64,5120]{2,1,0:T(8,128)}, f32[2,64,5120]{2,1,0:T(8,128)}, u32[]{:S(2)}, u32[]{:S(2)}) collective-permute-start(f32[2,64,5120]{2,1,0:T(8,128)} %get-tuple-element.30), channel_id=1, source_target_pairs={{0,16},{16,32},{32,48},{48,64},{64,80},{80,96},{96,112},{112,128},... | collective-permute-start | bytes 7864328 | tf_op jit(solution)/shard_map/ppermute | solution.py:28
  171.5 159.0 %collective-permute-start.4 = (f32[2,64,5120]{2,1,0:T(8,128)}, f32[2,64,5120]{2,1,0:T(8,128)}, u32[]{:S(2)}, u32[]{:S(2)}) collective-permute-start(f32[2,64,5120]{2,1,0:T(8,128)} %get-tuple-element.31), channel_id=1, source_target_pairs={{16,0},{32,16},{48,32},{64,48},{80,64},{96,80},{112,96},{128,112},... | collective-permute-start | bytes 7864328 | tf_op jit(solution)/shard_map/ppermute | solution.py:28
  198.4 1.7 copy-start.5
  198.4 2.7 copy-start.3
  200.1 1.7 copy-start.10
  202.6 0.9 copy-start.8
  215.3 140.7 %all-to-all-start.2 = ((bf16[16,2,40960]{2,1,0:T(2,128)(2,1)}), bf16[16,2,40960]{2,1,0:T(2,128)(2,1)}, u32[]{:S(2)}, u32[]{:S(2)}) async-start(bf16[16,2,40960]{2,1,0:T(2,128)(2,1)} %copy.73), calls=%async_computation.2 | async-start | bytes 5242880 | tf_op jit(solution)/shard_map/all_to_all | solution.py:198
  247.7 35.3 %copy-start.9 = (bf16[2,20,88,64]{2,3,1,0:T(8,128)(2,1)S(1)}, bf16[2,20,88,64]{2,3,1,0:T(8,128)(2,1)}, u32[]{:S(2)}) copy-start(bf16[2,20,88,64]{2,3,1,0:T(8,128)(2,1)} %copy-done.8) | copy-start | bytes 1351684
  247.7 35.3 %copy-start.11 = (bf16[2,11,20,8,128]{4,3,2,1,0:T(8,128)(2,1)S(1)}, bf16[2,11,20,8,128]{4,3,2,1,0:T(8,128)(2,1)}, u32[]{:S(2)}) copy-start(bf16[2,11,20,8,128]{4,3,2,1,0:T(8,128)(2,1)} %copy-done.10) | copy-start | bytes 2703364
  247.7 35.7 %copy-start.7 = (bf16[2,20,64,320]{3,2,1,0:T(8,128)(2,1)S(1)}, bf16[2,20,64,320]{3,2,1,0:T(8,128)(2,1)}, u32[]{:S(2)}) copy-start(bf16[2,20,64,320]{3,2,1,0:T(8,128)(2,1)} %copy-done.6) | copy-start | bytes 4915204
  250.4 104.2 %collective-permute-start.7 = (bf16[64,5120]{1,0:T(8,128)(2,1)}, bf16[64,5120]{1,0:T(8,128)(2,1)}, u32[]{:S(2)}, u32[]{:S(2)}) collective-permute-start(bf16[64,5120]{1,0:T(8,128)(2,1)} %get-tuple-element.38), channel_id=1, source_target_pairs={{0,1},{1,2},{2,3},{3,4},{4,5},{5,6},{6,7},{7,8},{8,9},{9,10},{10,1... | collective-permute-start | bytes 1966088 | tf_op jit(solution)/shard_map/ppermute | solution.py:28
  280.8 72.4 %collective-permute-start.6 = (bf16[64,5120]{1,0:T(8,128)(2,1)}, bf16[64,5120]{1,0:T(8,128)(2,1)}, u32[]{:S(2)}, u32[]{:S(2)}) collective-permute-start(bf16[64,5120]{1,0:T(8,128)(2,1)} %get-tuple-element.39), channel_id=1, source_target_pairs={{1,0},{2,1},{3,2},{4,3},{5,4},{6,5},{7,6},{8,7},{9,8},{10,9},{11,1... | collective-permute-start | bytes 1966088 | tf_op jit(solution)/shard_map/ppermute | solution.py:28
where the time goes:
time: 372 us; the launch traced here: 368 us
  waiting for transfers between devices  145 us (39%)
  starting transfers between devices  114 us (31%)
  local copies, waits for them, and re-layouts  59.6 us (16%)
  matrix products  27.4 us (7%)
  other arithmetic  21.9 us (6%)
    ppermute x2, waiting for transfers between devices, extended(): after = lax.ppermute(first, axis, down)  71.3 us
    ppermute x4, waiting for transfers between devices, passed_along(): return lax.ppermute(block, axis, route)  63.5 us
    ppermute x4, starting transfers between devices, passed_along(): return lax.ppermute(block, axis, route)  43.1 us
    all_to_all x1, starting transfers between devices, body(): lax.all_to_all(send_back, 'group', split_axis=0, concat_axis=0, tiled=True)  32.4 us
    ppermute x2, starting transfers between devices, extended(): before = lax.ppermute(last, axis, up)  14.7 us
    unnamed x42, local copies, waits for them, and re-layouts  13.5 us
    slice x1, local copies, waits for them, and re-layouts, body(): lower_part = grad_rows[:, 0:TILE]  9.81 us
    ppermute x2, starting transfers between devices, extended(): after = lax.ppermute(first, axis, down)  9.73 us
  transfers between devices with their start and end apart: 11, of which 6 were waited for; matrix products, arithmetic and copies ran while one was open for 24% of the time, Pallas kernels for 0%

commit v1 on v0

v1 whole, which is shorter than its diff:
```python
import functools
import math

import jax
import jax.numpy as jnp
from jax import lax
from jax.experimental import pallas as pl
from jax.experimental.pallas import tpu as pltpu
from jax.sharding import PartitionSpec as P

BF = jnp.bfloat16
F32 = jnp.float32
HEAD = 128
TILE = 64
HALF = 32
BLOCK = 8
GROUP = 16
POS = 128
LOG2E = math.log2(math.e)
SCALE = 1.0 / math.sqrt(HEAD)
BIG = 1e30

Q0, K0, V0, G0 = 0, 128, 256, 384
EK0, EV0, EQ0, EG0 = 512, 576, 640, 672
ST0, ROWS_IN = 704, 720
RQ0, RK0, RV0, REK0, REV0, REQ0, ROWS_OUT = 0, 128, 256, 384, 448, 512, 544


def nt(a, b):
    return lax.dot_general(a, b, (((1,), (1,)), ((), ())), preferred_element_type=F32)


def nn(a, b):
    return jnp.dot(a, b, preferred_element_type=F32)


def cols(h):
    return pl.ds(h * HEAD, HEAD)


def three_terms(x):
    hi = x.astype(BF).astype(F32)
    mid = (x - hi).astype(BF).astype(F32)
    low = ((x - hi) - mid).astype(BF).astype(F32)
    return hi, mid, low


def pack_kernel(
    frame_ref, frames_ref, blocks_ref, q_ref, k_ref, v_ref, o_ref, g_ref, lse_ref,
    send_ref, delta_ref, low_ref, high_ref,
):
    heads = lse_ref.shape[0]
    far = frames_ref.shape[1]
    frame = frame_ref[0]
    ones = jnp.ones((8, HEAD), BF)
    for h in range(heads):
        prod = g_ref[:, cols(h)].astype(F32) * o_ref[:, cols(h)].astype(F32)
        hi = prod.astype(BF)
        lo = (prod - hi.astype(F32)).astype(BF)
        row = nt(ones, hi) + nt(ones, lo)
        delta_ref[h : h + 1, :] = row[0:1, :]
    code = lax.broadcasted_iota(jnp.int32, (1, HEAD), 1)
    code_frame = code // BLOCK
    masks = []
    for t in range(POS // TILE):
        hit = jnp.abs(code_frame - frame) == 1
        for j in range(far):
            hit = hit | (code == frames_ref[t, j] * BLOCK + blocks_ref[t, j])
        masks.append(hit.astype(F32))
    sub = lax.broadcasted_iota(jnp.int32, (16, HEAD), 0)
    lane = lax.broadcasted_iota(jnp.int32, (16, HEAD), 1)
    place = (frame % 4) * HALF
    for d in range(GROUP):
        he, te, half = GROUP + d // 4, (d // 2) % 2, d % 2
        send_ref[d, Q0 : Q0 + POS, :] = q_ref[:, cols(d)]
        send_ref[d, K0 : K0 + POS, :] = k_ref[:, cols(d)]
        send_ref[d, V0 : V0 + POS, :] = v_ref[:, cols(d)]
        send_ref[d, G0 : G0 + POS, :] = g_ref[:, cols(d)]
        rows = slice(te * TILE, te * TILE + TILE)
        part = slice(te * TILE + half * HALF, te * TILE + half * HALF + HALF)
        send_ref[d, EK0 : EK0 + TILE, :] = k_ref[rows, cols(he)]
        send_ref[d, EV0 : EV0 + TILE, :] = v_ref[rows, cols(he)]
        send_ref[d, EQ0 : EQ0 + HALF, :] = q_ref[part, cols(he)]
        send_ref[d, EG0 : EG0 + HALF, :] = g_ref[part, cols(he)]
        main = three_terms(lse_ref[d : d + 1, :]) + three_terms(delta_ref[d : d + 1, :])
        extra = three_terms(lse_ref[he : he + 1, :]) + three_terms(delta_ref[he : he + 1, :])
        mine = jnp.zeros((16, HEAD), F32)
        for i in range(6):
            mine = jnp.where(sub == i, main[i], mine)
        theirs = jnp.zeros((16, HEAD), F32)
        for i in range(6):
            theirs = jnp.where(sub == 6 + i, extra[i], theirs)
        start = te * TILE + half * HALF
        theirs = pltpu.roll(theirs, lax.rem(place + (HEAD - start), HEAD), 1)
        inside = (lane >= place) & (lane < place + HALF)
        both = jnp.where(inside, theirs, 0.0) + mine
        for t in range(2):
            both = jnp.where(sub == 12 + t, masks[t], both)
        send_ref[d, ST0:ROWS_IN, :] = both.astype(BF)
    low_ref[0] = k_ref[0:TILE, :]
    low_ref[1] = v_ref[0:TILE, :]
    high_ref[0] = k_ref[POS - TILE : POS, :]
    high_ref[1] = v_ref[POS - TILE : POS, :]


def own_kernel(
    side_ref, q_ref, k_ref, v_ref, g_ref, before_ref, after_ref, lse_ref, delta_ref,
    dq_ref, dk_ref, dv_ref, low_ref, high_ref,
):
    step = pl.program_id(0)
    per_step = q_ref.shape[1] // HEAD
    width = POS + 2 * TILE
    key = lax.broadcasted_iota(jnp.int32, (width, POS), 0)
    query = lax.broadcasted_iota(jnp.int32, (width, POS), 1)
    first = jnp.where(side_ref[0] > 0, 0, TILE)
    last = jnp.where(side_ref[0] < side_ref[1] - 1, width, width - TILE)
    inside = (key >= query) & (key <= query + 2 * TILE) & (key >= first) & (key < last)
    for j in range(per_step):
        h = step * per_step + j
        q = q_ref[:, cols(j)]
        g = g_ref[:, cols(j)]
        k = jnp.concatenate([before_ref[0, :, cols(j)], k_ref[:, cols(j)], after_ref[0, :, cols(j)]], 0)
        v = jnp.concatenate([before_ref[1, :, cols(j)], v_ref[:, cols(j)], after_ref[1, :, cols(j)]], 0)
        lse = lse_ref[pl.ds(h, 1), :]
        delta = delta_ref[pl.ds(h, 1), :]
        p = jnp.exp2(nt(k, q) * (SCALE * LOG2E) - lse * LOG2E)
        p = jnp.where(inside, p, 0.0)
        ds = (p * (nt(v, g) - delta)).astype(BF)
        dv = nn(p.astype(BF), g)
        dk = nn(ds, q) * SCALE
        dq = lax.dot_general(ds, k, (((0,), (0,)), ((), ())), preferred_element_type=F32)
        dq_ref[:, cols(j)] = dq * SCALE
        dk_ref[:, cols(j)] = dk[TILE : TILE + POS]
        dv_ref[:, cols(j)] = dv[TILE : TILE + POS]
        low_ref[0, :, cols(j)] = dk[0:TILE].astype(BF)
        low_ref[1, :, cols(j)] = dv[0:TILE].astype(BF)
        high_ref[0, :, cols(j)] = dk[TILE + POS :].astype(BF)
        high_ref[1, :, cols(j)] = dv[TILE + POS :].astype(BF)


def cross_kernel(in_ref, out_ref, kx_ref, kt_ref, dk_ref, dv_ref, row_ref):
    keys = GROUP * TILE
    chunk = 256
    stats = in_ref[:, ST0:ROWS_IN, :].astype(F32)
    lane = lax.broadcasted_iota(jnp.int32, (1, HEAD), 1)
    spread = (
        lax.broadcasted_iota(jnp.int32, (keys, HEAD), 0) // BLOCK
        == lax.broadcasted_iota(jnp.int32, (keys, HEAD), 1)
    ).astype(BF)
    for unit in range(3):
        main = unit < 2
        if main:
            span = TILE
            q_at, k_at = Q0 + unit * TILE, K0 + unit * TILE
            v_at, g_at = V0 + unit * TILE, G0 + unit * TILE
            dq_at, dk_at, dv_at = RQ0 + unit * TILE, RK0 + unit * TILE, RV0 + unit * TILE
            mask = in_ref[:, ST0 + 12 + unit, :]
        else:
            span = HALF
            q_at, k_at, v_at, g_at = EQ0, EK0, EV0, EG0
            dq_at, dk_at, dv_at = REQ0, REK0, REV0
            second = (lax.axis_index("group") // 2) % 2
            mask = jnp.where(second == 1, in_ref[:, ST0 + 13, :], in_ref[:, ST0 + 12, :])
        per = HEAD // span
        base = 0 if main else 6
        for s in range(2):
            at = base + 3 * s
            full = (stats[:, at, :] + stats[:, at + 1, :]) + stats[:, at + 2, :]
            if main:
                turned = pltpu.roll(full, TILE, 1)
                left, right = (full, turned) if unit == 0 else (turned, full)
                for i in range(GROUP // per):
                    row_ref[s, i : i + 1, :] = jnp.where(
                        lane < TILE, left[2 * i : 2 * i + 1], right[2 * i + 1 : 2 * i + 2]
                    )
            else:
                for i in range(GROUP // per):
                    row_ref[s, i : i + 1, :] = (full[4 * i : 4 * i + 1] + full[4 * i + 1 : 4 * i + 2]) + (
                        full[4 * i + 2 : 4 * i + 3] + full[4 * i + 3 : 4 * i + 4]
                    )
        k = in_ref[:, k_at : k_at + TILE, :].reshape(keys, HEAD)
        v = in_ref[:, v_at : v_at + TILE, :].reshape(keys, HEAD)
        padded = jnp.concatenate([mask.astype(F32), jnp.zeros((HEAD - GROUP, HEAD), F32)], 0)
        kx_ref[:, 0:HEAD] = k
        kx_ref[:, HEAD:] = ((nt(spread, padded.astype(BF)) - 1.0) * BIG).astype(BF)
        kt_ref[...] = k.astype(F32).T.astype(BF)
        dk_ref[...] = jnp.zeros_like(dk_ref)
        dv_ref[...] = jnp.zeros_like(dv_ref)
        count = chunk // span
        query = lax.broadcasted_iota(jnp.int32, (chunk, HEAD), 0) // span
        column = lax.broadcasted_iota(jnp.int32, (chunk, HEAD), 1)

        def one_chunk(c, carry):
            frames = pl.ds(c * count, count)
            q = in_ref[frames, q_at : q_at + span, :].reshape(chunk, HEAD)
            g = in_ref[frames, g_at : g_at + span, :].reshape(chunk, HEAD)
            choose = (column == query + c * count).astype(F32).astype(BF)
            qx = jnp.concatenate([q, choose], 1)
            lse = jnp.concatenate([row_ref[0, pl.ds(2 * c + i, 1), :] for i in range(2)], 1)
            delta = jnp.concatenate([row_ref[1, pl.ds(2 * c + i, 1), :] for i in range(2)], 1)
            p = jnp.exp2(nt(kx_ref[...], qx) * (SCALE * LOG2E) - lse * LOG2E)
            ds = (p * (nt(v, g) - delta)).astype(BF)
            dv_ref[...] += nn(p.astype(BF), g)
            dk_ref[...] += nn(ds, q)
            dq = (nn(kt_ref[...], ds) * SCALE).T.astype(BF)
            out_ref[frames, dq_at : dq_at + span, :] = dq.reshape(count, span, HEAD)
            return carry

        lax.fori_loop(0, GROUP * span // chunk, one_chunk, 0)
        out_ref[:, dk_at : dk_at + TILE, :] = (dk_ref[...] * SCALE).astype(BF).reshape(GROUP, TILE, HEAD)
        out_ref[:, dv_at : dv_at + TILE, :] = dv_ref[...].astype(BF).reshape(GROUP, TILE, HEAD)


def join_kernel(
    back_ref, dq_in, dk_in, dv_in, left_ref, right_ref, dq_ref, dk_ref, dv_ref
):
    step = pl.program_id(0)
    per_step = dq_ref.shape[1] // HEAD

    def finish(j, dq, dk, dv):
        dq_ref[:, cols(j)] = (dq_in[:, cols(j)] + dq).astype(BF)
        for i, (own, ref, more) in enumerate(((dk_in, dk_ref, dk), (dv_in, dv_ref, dv))):
            total = own[:, cols(j)] + more
            side = jnp.concatenate([left_ref[i, :, cols(j)], right_ref[i, :, cols(j)]], 0)
            ref[:, cols(j)] = (total + side.astype(F32)).astype(BF)

    @pl.when(step < 4)
    def _():
        for j in range(per_step):
            d = step * per_step + j
            finish(
                j,
                back_ref[d, RQ0 : RQ0 + POS, :].astype(F32),
                back_ref[d, RK0 : RK0 + POS, :].astype(F32),
                back_ref[d, RV0 : RV0 + POS, :].astype(F32),
            )

    @pl.when(step == 4)
    def _():
        for j in range(per_step):
            four = range(4 * j, 4 * j + 4)
            dq = jnp.concatenate([back_ref[d, REQ0:ROWS_OUT, :].astype(F32) for d in four], 0)
            sums = []
            for at in (REK0, REV0):
                part = [back_ref[d, at : at + TILE, :].astype(F32) for d in four]
                sums.append(jnp.concatenate([part[0] + part[1], part[2] + part[3]], 0))
            finish(j, dq, sums[0], sums[1])


VMEM = pl.BlockSpec(memory_space=pltpu.VMEM)
SMEM = pl.BlockSpec(memory_space=pltpu.SMEM)
ROOM = 48 * 1024 * 1024


def body(query_rows, key_rows, value_rows, out_rows, grad_out, log_sum_exp, far_frames, far_blocks):
    q, k, v, o, g = (a[0] for a in (query_rows, key_rows, value_rows, out_rows, grad_out))
    lse = log_sum_exp[0]
    feature = q.shape[1]
    heads = lse.shape[0]
    inner = lax.axis_size("inner")
    inner_at = lax.axis_index("inner")
    frame = lax.axis_index("group").reshape(1).astype(jnp.int32)
    sides = jnp.stack([inner_at, jnp.full((), inner, inner_at.dtype)]).astype(jnp.int32)
    halo = jax.ShapeDtypeStruct((2, TILE, feature), BF)

    send, delta, first_rows, last_rows = pl.pallas_call(
        pack_kernel,
        out_shape=(
            jax.ShapeDtypeStruct((GROUP, ROWS_IN, HEAD), BF),
            jax.ShapeDtypeStruct((heads, POS), F32),
            halo,
            halo,
        ),
        in_specs=[SMEM] * 3 + [VMEM] * 6,
        out_specs=[VMEM] * 4,
        compiler_params=pltpu.CompilerParams(vmem_limit_bytes=ROOM),
        name="pack",
    )(frame, far_frames[0], far_blocks[0], q, k, v, o, g, lse)

    arrived = lax.all_to_all(send, "group", 0, 0, tiled=True)

    up = [(i, i + 1) for i in range(inner - 1)]
    down = [(i + 1, i) for i in range(inner - 1)]
    before = lax.ppermute(last_rows, "inner", up)
    after = lax.ppermute(first_rows, "inner", down)

    wide = 4 * HEAD
    rows = pl.BlockSpec((POS, wide), lambda i: (0, i))
    edge = pl.BlockSpec((2, TILE, wide), lambda i: (0, 0, i))
    whole = pl.BlockSpec((heads, POS), lambda i: (0, 0))
    own_shape = jax.ShapeDtypeStruct((POS, feature), F32)
    dq_own, dk_own, dv_own, to_low, to_high = pl.pallas_call(
        own_kernel,
        grid=(feature // wide,),
        out_shape=(own_shape, own_shape, own_shape, halo, halo),
        in_specs=[SMEM, rows, rows, rows, rows, edge, edge, whole, whole],
        out_specs=[rows, rows, rows, edge, edge],
        compiler_params=pltpu.CompilerParams(vmem_limit_bytes=ROOM),
        name="own",
    )(sides, q, k, v, g, before, after, lse, delta)
    from_right = lax.ppermute(to_low, "inner", down)
    from_left = lax.ppermute(to_high, "inner", up)

    keys = GROUP * TILE
    back = pl.pallas_call(
        cross_kernel,
        out_shape=jax.ShapeDtypeStruct((GROUP, ROWS_OUT, HEAD), BF),
        in_specs=[VMEM],
        out_specs=VMEM,
        scratch_shapes=[
            pltpu.VMEM((keys, 2 * HEAD), BF),
            pltpu.VMEM((HEAD, keys), BF),
            pltpu.VMEM((keys, HEAD), F32),
            pltpu.VMEM((keys, HEAD), F32),
            pltpu.VMEM((2, 8, HEAD), F32),
        ],
        compiler_params=pltpu.CompilerParams(vmem_limit_bytes=ROOM),
        name="cross",
    )(arrived)
    returned = lax.all_to_all(back, "group", 0, 0, tiled=True)

    out_shape = jax.ShapeDtypeStruct((POS, feature), BF)
    outs = pl.pallas_call(
        join_kernel,
        grid=(feature // wide,),
        out_shape=(out_shape,) * 3,
        in_specs=[VMEM, rows, rows, rows, edge, edge],
        out_specs=[rows] * 3,
        compiler_params=pltpu.CompilerParams(vmem_limit_bytes=ROOM),
        name="join",
    )(returned, dq_own, dk_own, dv_own, from_left, from_right)
    return tuple(a[None] for a in outs)


def solution(mesh):
    shard = P("group", "inner", None)
    return jax.shard_map(
        body,
        mesh=mesh,
        in_specs=(shard,) * 5 + (P("group", None, "inner"), shard, shard),
        out_specs=(shard,) * 3,
        check_vma=False,
    )
```

time: 372 us -> 203 us (0.55)
  starting transfers between devices: 114 us -> 21.2 us
  waiting for transfers between devices: 145 us -> 62.5 us
  blocking collectives: 0 us -> 77 us
  local copies, waits for them, and re-layouts: 59.6 us -> 13.1 us
  matrix products: 27.4 us -> 0 us
  Pallas kernels: 0 us -> 27.1 us
  other arithmetic: 21.9 us -> 0.08 us
    all_to_all x0 -> x1, blocking collectives: none -> 77 us  [body(): arrived = lax.all_to_all(send, 'group', 0, 0, tiled=True)]
    ppermute x8 -> x4, waiting for transfers between devices: 135 us -> 62.5 us  [the longest x1 48.8 us: body(): before = lax.ppermute(last_rows, 'inner', up)]
    ppermute x8 -> x4, starting transfers between devices: 67.5 us -> 13.7 us  [the longest x1 4.78 us: body(): from_left = lax.ppermute(to_high, 'inner', up)]
    all_to_all x3 -> x1, starting transfers between devices: 46.1 us -> 7.47 us  [body(): returned = lax.all_to_all(back, 'group', 0, 0, tiled=True)]
    dot_general x14 -> x0, matrix products: 27.4 us -> none  [the longest x1 6.27 us: body(): jnp.einsum('ckd,dcr->ckr', choose_low, far_rows_in, preferred_element_typ...]
    pallas_call x0 -> x4, Pallas kernels: none -> 27.1 us  [the longest x1 11.3 us: body(): pl.pallas_call(cross_kernel, out_shape=jax.ShapeDtypeStruct((GROUP, ROWS_...]
    convert_element_type x7 -> x0, local copies, waits for them, and re-layouts: 17.5 us -> none  [the longest x1 4.22 us: body(): picked = jnp.einsum('scb,cbr->scr', pick_table, key_blocks, preferred_ele...]
    slice x2 -> x0, local copies, waits for them, and re-layouts: 11.9 us -> none  [the longest x1 9.81 us: body(): lower_part = grad_rows[:, 0:TILE]]
  transfers between devices with their start and end apart: 11 -> 5, of which waited for: 6 -> 4; matrix products, arithmetic and copies ran while one was open for 24% -> 0% of each run, Pallas kernels for 0% -> 4%
where the time goes in v1:
time: 203 us; the launch traced here: 202 us
  blocking collectives  77 us (38%)
  waiting for transfers between devices  62.5 us (31%)
  Pallas kernels  27.1 us (13%)
  starting transfers between devices  21.2 us (10%)
  local copies, waits for them, and re-layouts  13.1 us (6%)
    all_to_all x1, blocking collectives, body(): arrived = lax.all_to_all(send, 'group', 0, 0, tiled=True)  77 us
    ppermute x1, waiting for transfers between devices, body(): before = lax.ppermute(last_rows, 'inner', up)  48.8 us
    unnamed x33, local copies, waits for them, and re-layouts  13.1 us
    pallas_call x1, Pallas kernels, body(): pl.pallas_call(cross_kernel, out_shape=jax.ShapeDtypeStruct((GROUP, ROWS_...  11.3 us
    pallas_call x1, Pallas kernels, body(): pl.pallas_call(own_kernel, grid=(feature // wide,), out_shape=(own_shape,...  7.85 us
    all_to_all x1, starting transfers between devices, body(): returned = lax.all_to_all(back, 'group', 0, 0, tiled=True)  7.47 us
    ppermute x1, waiting for transfers between devices, body(): from_right = lax.ppermute(to_low, 'inner', down)  6.51 us
    ppermute x1, waiting for transfers between devices, body(): from_left = lax.ppermute(to_high, 'inner', up)  5.58 us
  transfers between devices with their start and end apart: 5, of which 4 were waited for; matrix products, arithmetic and copies ran while one was open for 0% of the time, Pallas kernels for 4%

profile of v1, /device:TPU:23, one launch (start us, length us, event | category | flops | bytes accessed | tf_op | source)
XLA Modules:
  0.0 201.8 jit_solution(3921248754254211970)
XLA Ops:
  0.6 0.7 copy.13
  1.3 0.0 copy-start
  1.3 1.1 copy-done
  2.4 0.0 copy-start.2
  2.4 1.1 copy-done.2
  3.5 0.0 copy-start.4
  3.5 1.1 copy-done.4
  4.6 0.0 copy-start.6
  4.6 1.1 copy-done.6
  5.7 0.0 copy-start.11
  5.7 1.1 copy-done.11
  6.8 0.0 copy-start.12
  6.8 0.7 copy-done.12
  7.5 0.0 copy-start.13
  7.5 0.7 copy-done.13
  8.1 3.5 %pack.1 = (bf16[16,720,128]{2,1,0:T(8,128)(2,1)}, f32[20,128]{1,0:T(8,128)S(1)}, bf16[2,64,2560]{2,1,0:T(8,128)(2,1)S(1)}, bf16[2,64,2560]{2,1,0:T(8,128)(2,1)S(1)}) custom-call(s32[1]{0:T(128)} %bitcast.frame_ref, s32[2,11]{1,0:T(2,128)S(1)} %bitcast.26, s32[2,11]{1,0:T(2,128)S(1)} %bitcast.27, bf16[128,2560]{1,0:T(8,128)(2,1)S(1)} %bitcast.15, ...), custom_call_target="tpu_custom_call" | custom-call | tf_op jit(solution)/shard_map/pack/pallas_call | solution.py:266
  11.7 0.0 copy-start.14
  11.7 0.8 copy-done.14
  12.5 0.0 copy-start.15
  12.5 0.8 copy-done.15
  13.3 77.0 %all_to_all.10.in_ref = bf16[16,720,128]{2,1,0:T(8,128)(2,1)S(1)} all-to-all(bf16[16,720,128]{2,1,0:T(8,128)(2,1)} %get-tuple-element.15), channel_id=1, replica_groups=mesh['group'=16,'inner'=16] {'group'}, dimensions={0} | all-to-all | bytes 5898240 | tf_op jit(solution)/shard_map/all_to_all | solution.py:280
  90.3 11.3 %cross.1 = bf16[16,544,128]{2,1,0:T(8,128)(2,1)} custom-call(bf16[16,720,128]{2,1,0:T(8,128)(2,1)S(1)} %all_to_all.10.in_ref), custom_call_target="tpu_custom_call" | custom-call | tf_op jit(solution)/shard_map/cross/pallas_call | solution.py:305
  101.6 0.0 copy-start.3
  101.6 0.0 copy-start.5
  101.6 0.0 copy-start.7
  101.6 7.5 %all-to-all-start.1 = ((bf16[16,544,128]{2,1,0:T(8,128)(2,1)}), bf16[16,544,128]{2,1,0:T(8,128)(2,1)}, u32[]{:S(2)}, u32[]{:S(2)}) async-start(bf16[16,544,128]{2,1,0:T(8,128)(2,1)} %cross.1), calls=%async_computation.1 | async-start | bytes 4456448 | tf_op jit(solution)/shard_map/all_to_all | solution.py:320
  109.1 4.6 %collective-permute-start = (bf16[2,64,2560]{2,1,0:T(8,128)(2,1)}, bf16[2,64,2560]{2,1,0:T(8,128)(2,1)S(1)}, u32[]{:S(2)}, u32[]{:S(2)}) collective-permute-start(bf16[2,64,2560]{2,1,0:T(8,128)(2,1)} %copy-done.15), channel_id=1, source_target_pairs={{0,1},{1,2},{2,3},{3,4},{4,5},{5,6},{6,7},{7,8},{8,9},{9,10},{10,1... | collective-permute-start | bytes 1966088 | tf_op jit(solution)/shard_map/ppermute | solution.py:284
  113.7 2.5 %collective-permute-start.1 = (bf16[2,64,2560]{2,1,0:T(8,128)(2,1)}, bf16[2,64,2560]{2,1,0:T(8,128)(2,1)}, u32[]{:S(2)}, u32[]{:S(2)}) collective-permute-start(bf16[2,64,2560]{2,1,0:T(8,128)(2,1)} %copy-done.14), channel_id=1, source_target_pairs={{1,0},{2,1},{3,2},{4,3},{5,4},{6,5},{7,6},{8,7},{9,8},{10,9},{11,1... | collective-permute-start | bytes 1966088 | tf_op jit(solution)/shard_map/ppermute | solution.py:285
  116.2 0.1 pad_add_fusion.side_ref
  116.2 48.8 %collective-permute-done.before_ref = bf16[2,64,2560]{2,1,0:T(8,128)(2,1)S(1)} collective-permute-done((bf16[2,64,2560]{2,1,0:T(8,128)(2,1)}, bf16[2,64,2560]{2,1,0:T(8,128)(2,1)S(1)}, u32[]{:S(2)}, u32[]{:S(2)}) %collective-permute-start) | collective-permute-done | bytes 655392 | tf_op jit(solution)/shard_map/ppermute | solution.py:284
  165.1 1.6 collective-permute-done.1.after_ref
  166.7 0.0 copy-done.1
  166.7 0.0 copy-done.3
  166.7 0.0 copy-done.5
  166.7 0.0 copy-done.7
  166.7 7.8 %own.1 = (f32[128,2560]{1,0:T(8,128)}, f32[128,2560]{1,0:T(8,128)}, f32[128,2560]{1,0:T(8,128)}, bf16[2,64,2560]{2,1,0:T(8,128)(2,1)S(1)}, bf16[2,64,2560]{2,1,0:T(8,128)(2,1)S(1)}) custom-call(s32[2]{0:T(128)S(1)} %pad_add_fusion.side_ref, bf16[128,2560]{1,0:T(8,128)(2,1)S(1)} %bitcast.16, bf16[128,2560]{1,0:T(8,128)(2,1)S(1)} %bitcast.18, ...), custom_call_target="tpu_custom_call" | custom-call | tf_op jit(solution)/shard_map/own/pallas_call | solution.py:292
  174.6 4.8 %collective-permute-start.2 = (bf16[2,64,2560]{2,1,0:T(8,128)(2,1)S(1)}, bf16[2,64,2560]{2,1,0:T(8,128)(2,1)S(1)}, u32[]{:S(2)}, u32[]{:S(2)}) collective-permute-start(bf16[2,64,2560]{2,1,0:T(8,128)(2,1)S(1)} %get-tuple-element.22), channel_id=1, source_target_pairs={{0,1},{1,2},{2,3},{3,4},{4,5},{5,6},{6,7},{7,8},{8,9},{9,10},{10,1... | collective-permute-start | bytes 1966088 | tf_op jit(solution)/shard_map/ppermute | solution.py:302
  179.4 1.9 collective-permute-start.3
  181.3 5.6 %collective-permute-done.2.left_ref = bf16[2,64,2560]{2,1,0:T(8,128)(2,1)S(1)} collective-permute-done((bf16[2,64,2560]{2,1,0:T(8,128)(2,1)S(1)}, bf16[2,64,2560]{2,1,0:T(8,128)(2,1)S(1)}, u32[]{:S(2)}, u32[]{:S(2)}) %collective-permute-start.2) | collective-permute-done | bytes 655392 | tf_op jit(solution)/shard_map/ppermute | solution.py:302
  186.9 6.5 %collective-permute-done.3.right_ref = bf16[2,64,2560]{2,1,0:T(8,128)(2,1)S(1)} collective-permute-done((bf16[2,64,2560]{2,1,0:T(8,128)(2,1)S(1)}, bf16[2,64,2560]{2,1,0:T(8,128)(2,1)S(1)}, u32[]{:S(2)}, u32[]{:S(2)}) %collective-permute-start.3) | collective-permute-done | bytes 655392 | tf_op jit(solution)/shard_map/ppermute | solution.py:301
  193.4 0.0 all-to-all-done.1.back_ref
  193.4 0.0 copy-start.8
  193.4 1.3 copy-done.8
  194.7 0.0 copy-start.9
  194.7 1.3 copy-done.9
  196.0 0.0 copy-start.10
  196.0 1.3 copy-done.10
  197.3 4.5 %join.1 = (bf16[128,2560]{1,0:T(8,128)(2,1)}, bf16[128,2560]{1,0:T(8,128)(2,1)}, bf16[128,2560]{1,0:T(8,128)(2,1)}) custom-call(bf16[16,544,128]{2,1,0:T(8,128)(2,1)} %all-to-all-done.1.back_ref, f32[128,2560]{1,0:T(8,128)S(1)} %copy-done.8, f32[128,2560]{1,0:T(8,128)S(1)} %copy-done.9, f32[128,2560]{1,0:T(8,128)S(1)} %copy-done.10, ...), custom_call_target="tpu_custom_call" | custom-call | tf_op jit(solution)/shard_map/join/pallas_call | solution.py:323
  (1 shorter events, 0.0 us)
Async XLA Ops:
  1.3 1.1 copy-start
  2.4 1.1 copy-start.2
  3.5 1.1 copy-start.4
  4.6 1.1 copy-start.6
  5.7 1.1 copy-start.11
  6.8 0.7 copy-start.12
  7.5 0.7 copy-start.13
  11.7 0.8 copy-start.14
  12.5 0.8 copy-start.15
  101.6 65.1 %copy-start.1 = (bf16[1,128,2560]{2,1,0:T(8,128)(2,1)S(1)}, bf16[1,128,2560]{2,1,0:T(8,128)(2,1)}, u32[]{:S(2)}) copy-start(bf16[1,128,2560]{2,1,0:T(8,128)(2,1)} %param.8) | copy-start | bytes 1966084
  101.6 65.1 %copy-start.3 = (bf16[1,128,2560]{2,1,0:T(8,128)(2,1)S(1)}, bf16[1,128,2560]{2,1,0:T(8,128)(2,1)}, u32[]{:S(2)}) copy-start(bf16[1,128,2560]{2,1,0:T(8,128)(2,1)} %param.9) | copy-start | bytes 1966084
  101.6 65.1 %copy-start.5 = (bf16[1,128,2560]{2,1,0:T(8,128)(2,1)S(1)}, bf16[1,128,2560]{2,1,0:T(8,128)(2,1)}, u32[]{:S(2)}) copy-start(bf16[1,128,2560]{2,1,0:T(8,128)(2,1)} %param.10) | copy-start | bytes 1966084
  101.6 65.1 %copy-start.7 = (bf16[1,128,2560]{2,1,0:T(8,128)(2,1)S(1)}, bf16[1,128,2560]{2,1,0:T(8,128)(2,1)}, u32[]{:S(2)}) copy-start(bf16[1,128,2560]{2,1,0:T(8,128)(2,1)} %param.12) | copy-start | bytes 1966084
  101.6 91.7 %all-to-all-start.1 = ((bf16[16,544,128]{2,1,0:T(8,128)(2,1)}), bf16[16,544,128]{2,1,0:T(8,128)(2,1)}, u32[]{:S(2)}, u32[]{:S(2)}) async-start(bf16[16,544,128]{2,1,0:T(8,128)(2,1)} %cross.1), calls=%async_computation.1 | async-start | bytes 4456448 | tf_op jit(solution)/shard_map/all_to_all | solution.py:320
  109.1 56.0 %collective-permute-start = (bf16[2,64,2560]{2,1,0:T(8,128)(2,1)}, bf16[2,64,2560]{2,1,0:T(8,128)(2,1)S(1)}, u32[]{:S(2)}, u32[]{:S(2)}) collective-permute-start(bf16[2,64,2560]{2,1,0:T(8,128)(2,1)} %copy-done.15), channel_id=1, source_target_pairs={{0,1},{1,2},{2,3},{3,4},{4,5},{5,6},{6,7},{7,8},{8,9},{9,10},{10,1... | collective-permute-start | bytes 1966088 | tf_op jit(solution)/shard_map/ppermute | solution.py:284
  113.7 53.0 %collective-permute-start.1 = (bf16[2,64,2560]{2,1,0:T(8,128)(2,1)}, bf16[2,64,2560]{2,1,0:T(8,128)(2,1)}, u32[]{:S(2)}, u32[]{:S(2)}) collective-permute-start(bf16[2,64,2560]{2,1,0:T(8,128)(2,1)} %copy-done.14), channel_id=1, source_target_pairs={{1,0},{2,1},{3,2},{4,3},{5,4},{6,5},{7,6},{8,7},{9,8},{10,9},{11,1... | collective-permute-start | bytes 1966088 | tf_op jit(solution)/shard_map/ppermute | solution.py:285
  174.6 12.3 %collective-permute-start.2 = (bf16[2,64,2560]{2,1,0:T(8,128)(2,1)S(1)}, bf16[2,64,2560]{2,1,0:T(8,128)(2,1)S(1)}, u32[]{:S(2)}, u32[]{:S(2)}) collective-permute-start(bf16[2,64,2560]{2,1,0:T(8,128)(2,1)S(1)} %get-tuple-element.22), channel_id=1, source_target_pairs={{0,1},{1,2},{2,3},{3,4},{4,5},{5,6},{6,7},{7,8},{8,9},{9,10},{10,1... | collective-permute-start | bytes 1966088 | tf_op jit(solution)/shard_map/ppermute | solution.py:302
  179.4 14.0 %collective-permute-start.3 = (bf16[2,64,2560]{2,1,0:T(8,128)(2,1)S(1)}, bf16[2,64,2560]{2,1,0:T(8,128)(2,1)S(1)}, u32[]{:S(2)}, u32[]{:S(2)}) collective-permute-start(bf16[2,64,2560]{2,1,0:T(8,128)(2,1)S(1)} %get-tuple-element.23), channel_id=1, source_target_pairs={{1,0},{2,1},{3,2},{4,3},{5,4},{6,5},{7,6},{8,7},{9,8},{10,9},{11,1... | collective-permute-start | bytes 1966088 | tf_op jit(solution)/shard_map/ppermute | solution.py:301
  193.4 1.3 copy-start.8
  194.7 1.3 copy-start.9
  196.0 1.3 copy-start.10

commit v2 on v1

v2 whole, which is shorter than its diff:
```python
import functools
import math

import jax
import jax.numpy as jnp
from jax import lax
from jax.experimental import pallas as pl
from jax.experimental.pallas import tpu as pltpu
from jax.sharding import PartitionSpec as P

BF = jnp.bfloat16
F32 = jnp.float32
HEAD = 128
TILE = 64
HALF = 32
BLOCK = 8
GROUP = 16
SIDE = 4
POS = 128
WIDE = SIDE * HEAD
LOG2E = math.log2(math.e)
SCALE = 1.0 / math.sqrt(HEAD)
BIG = 1e30

BQ, BK, BV, BG, BS, ROWS_B = 0, 128, 256, 384, 512, 528
BACK_B = 384
AK, AV, AQ, AG, AS, ROWS_A = 0, 64, 128, 160, 192, 208
RK, RV, RQ, ROWS_R = 0, 64, 128, 160


def nt(a, b):
    return lax.dot_general(a, b, (((1,), (1,)), ((), ())), preferred_element_type=F32)


def nn(a, b):
    return jnp.dot(a, b, preferred_element_type=F32)


def cols(h):
    return pl.ds(h * HEAD, HEAD)


def three_terms(x):
    hi = x.astype(BF).astype(F32)
    mid = (x - hi).astype(BF).astype(F32)
    low = ((x - hi) - mid).astype(BF).astype(F32)
    return hi, mid, low


class Copies:
    def __init__(self, sems):
        self.sems, self.used, self.open = sems, 0, {}

    def start(self, key, source, target):
        copy = pltpu.make_async_copy(source, target, self.sems.at[self.used])
        copy.start()
        self.used += 1
        self.open.setdefault(key, []).append(copy)

    def wait(self, key):
        for copy in self.open.pop(key, []):
            copy.wait()

    def wait_all(self):
        for key in list(self.open):
            self.wait(key)


class Copies:
    def __init__(self, sems):
        self.sems, self.used, self.open = sems, 0, {}

    def start(self, key, source, target):
        copy = pltpu.make_async_copy(source, target, self.sems.at[self.used])
        copy.start()
        self.used += 1
        self.open.setdefault(key, []).append(copy)

    def wait(self, key):
        for copy in self.open.pop(key, []):
            copy.wait()

    def wait_all(self):
        for key in list(self.open):
            self.wait(key)


def deltas(grads, outs):
    ones = jnp.ones((8, HEAD), BF)
    prod = jnp.concatenate([g.astype(F32) * o.astype(F32) for g, o in zip(grads, outs)], 0)
    hi = prod.astype(BF)
    lo = (prod - hi.astype(F32)).astype(BF)
    sums = nt(ones, hi) + nt(ones, lo)
    return [sums[0:1, j * HEAD : j * HEAD + HEAD] for j in range(len(grads))]


def pair_masks(frame, frames_ref, blocks_ref):
    code = lax.broadcasted_iota(jnp.int32, (1, HEAD), 1)
    masks = []
    for t in range(POS // TILE):
        hit = jnp.abs(code // BLOCK - frame) == 1
        for j in range(frames_ref.shape[1]):
            hit = hit | (code == frames_ref[t, j] * BLOCK + blocks_ref[t, j])
        masks.append(hit.astype(F32))
    return masks


def stat_rows(lse, delta, masks):
    sub = lax.broadcasted_iota(jnp.int32, (16, HEAD), 0)
    rows = jnp.zeros((16, HEAD), F32)
    for i, term in enumerate(list(three_terms(lse) + three_terms(delta)) + masks):
        rows = jnp.where(sub == i, term, rows)
    return rows


def pack_a_kernel(
    place_ref, frames_ref, blocks_ref, lse_ref, q_hbm, k_hbm, v_hbm, o_hbm, g_hbm,
    z0_hbm, z1_hbm, z2_hbm, z3_hbm, low_hbm, high_hbm,
    q_all, k_all, v_all, o_all, g_all, send_ref, edge_ref, sems,
):
    copies = Copies(sems)
    at = slice(SIDE * WIDE, SIDE * WIDE + WIDE)
    for source, target in zip((g_hbm, o_hbm, q_hbm, k_hbm, v_hbm), (g_all, o_all, q_all, k_all, v_all)):
        copies.start("in", source.at[:, at], target)
    for i, source in enumerate((k_hbm, v_hbm)):
        copies.start("edge", source.at[0:TILE, :], edge_ref.at[0, i])
        copies.start("edge", source.at[POS - TILE : POS, :], edge_ref.at[1, i])
    masks = pair_masks(place_ref[0] * SIDE + place_ref[1], frames_ref, blocks_ref)
    copies.wait("in")
    rows = deltas([g_all[:, cols(j)] for j in range(SIDE)], [o_all[:, cols(j)] for j in range(SIDE)])
    for j in range(SIDE):
        send_ref[j, BQ : BQ + POS, :] = q_all[:, cols(j)]
        send_ref[j, BK : BK + POS, :] = k_all[:, cols(j)]
        send_ref[j, BV : BV + POS, :] = v_all[:, cols(j)]
        send_ref[j, BG : BG + POS, :] = g_all[:, cols(j)]
        send_ref[j, BS:ROWS_B, :] = stat_rows(lse_ref[GROUP + j], rows[j], masks).astype(BF)
    for dz, out in enumerate((z0_hbm, z1_hbm, z2_hbm, z3_hbm)):
        copies.start("out", send_ref.at[lax.rem(place_ref[1] + dz, SIDE)], out)
    copies.wait("edge")
    copies.start("out", edge_ref.at[0], low_hbm)
    copies.start("out", edge_ref.at[1], high_hbm)
    copies.wait_all()


def pack_b_kernel(
    place_ref, frames_ref, blocks_ref, lse_ref, q_hbm, k_hbm, v_hbm, o_hbm, g_hbm, send_hbm,
    q_all, k_all, v_all, o_all, g_all, send_ref, sems,
):
    copies = Copies(sems)
    pairs = ((g_hbm, g_all), (o_hbm, o_all), (q_hbm, q_all), (k_hbm, k_all), (v_hbm, v_all))
    for block in range(SIDE):
        at = slice(block * WIDE, block * WIDE + WIDE)
        for source, target in pairs:
            copies.start(block, source.at[:, at], target.at[:, at])
    masks = pair_masks(place_ref[0] * SIDE + place_ref[1], frames_ref, blocks_ref)
    for block in range(SIDE):
        copies.wait(block)
        heads = [block * SIDE + j for j in range(SIDE)]
        rows = deltas([g_all[:, cols(h)] for h in heads], [o_all[:, cols(h)] for h in heads])
        for j, h in enumerate(heads):
            send_ref[h, BQ : BQ + POS, :] = q_all[:, cols(h)]
            send_ref[h, BK : BK + POS, :] = k_all[:, cols(h)]
            send_ref[h, BV : BV + POS, :] = v_all[:, cols(h)]
            send_ref[h, BG : BG + POS, :] = g_all[:, cols(h)]
            send_ref[h, BS:ROWS_B, :] = stat_rows(lse_ref[h], rows[j], masks).astype(BF)
        four = slice(block * SIDE, block * SIDE + SIDE)
        copies.start("out", send_ref.at[four], send_hbm.at[four])
    copies.wait_all()


def split_kernel(place_ref, *refs):
    ins, outs = refs[:SIDE], refs[SIDE:]
    lane = lax.broadcasted_iota(jnp.int32, (16, HEAD), 1)
    sub = lax.broadcasted_iota(jnp.int32, (16, HEAD), 0)
    for dz, got in enumerate(ins):
        stats = got[BS:ROWS_B, :].astype(F32)
        for dy, out in enumerate(outs):
            y = lax.rem(place_ref[0] + dy, SIDE)
            tile = pl.multiple_of((y // 2) * TILE, TILE)
            half = pl.multiple_of(y * HALF, HALF)
            out[dz, AK : AK + TILE, :] = got[pl.ds(BK + tile, TILE), :]
            out[dz, AV : AV + TILE, :] = got[pl.ds(BV + tile, TILE), :]
            out[dz, AQ : AQ + HALF, :] = got[pl.ds(BQ + half, HALF), :]
            out[dz, AG : AG + HALF, :] = got[pl.ds(BG + half, HALF), :]
            turned = pltpu.roll(stats, lax.rem(dz * HALF + HEAD - half, HEAD), 1)
            inside = (lane >= dz * HALF) & (lane < dz * HALF + HALF)
            kept = jnp.where(sub < 6, jnp.where(inside, turned, 0.0), stats)
            out[dz, AS:ROWS_A, :] = kept.astype(BF)


def own_kernel(
    side_ref, q_ref, k_ref, v_ref, o_ref, g_ref, before_ref, after_ref, lse_ref,
    sums_ref, low_ref, high_ref,
):
    step = pl.program_id(0)
    width = POS + 2 * TILE
    key = lax.broadcasted_iota(jnp.int32, (width, POS), 0)
    query = lax.broadcasted_iota(jnp.int32, (width, POS), 1)
    first = jnp.where(side_ref[0] > 0, 0, TILE)
    last = jnp.where(side_ref[0] < side_ref[1] - 1, width, width - TILE)
    inside = (key >= query) & (key <= query + 2 * TILE) & (key >= first) & (key < last)
    rows = deltas([g_ref[:, cols(j)] for j in range(SIDE)], [o_ref[:, cols(j)] for j in range(SIDE)])
    for j in range(SIDE):
        q = q_ref[:, cols(j)]
        g = g_ref[:, cols(j)]
        k = jnp.concatenate([before_ref[0, :, cols(j)], k_ref[:, cols(j)], after_ref[0, :, cols(j)]], 0)
        v = jnp.concatenate([before_ref[1, :, cols(j)], v_ref[:, cols(j)], after_ref[1, :, cols(j)]], 0)
        lse = lse_ref[step * SIDE + j]
        p = jnp.exp2(nt(k, q) * (SCALE * LOG2E) - lse * LOG2E)
        p = jnp.where(inside, p, 0.0)
        ds = (p * (nt(v, g) - rows[j])).astype(BF)
        dv = nn(p.astype(BF), g)
        dk = nn(ds, q) * SCALE
        dq = lax.dot_general(ds, k, (((0,), (0,)), ((), ())), preferred_element_type=F32)
        sums_ref[0, :, cols(j)] = dq * SCALE
        sums_ref[1, :, cols(j)] = dk[TILE : TILE + POS]
        sums_ref[2, :, cols(j)] = dv[TILE : TILE + POS]
        low_ref[0, :, cols(j)] = dk[0:TILE].astype(BF)
        low_ref[1, :, cols(j)] = dv[0:TILE].astype(BF)
        high_ref[0, :, cols(j)] = dk[TILE + POS :].astype(BF)
        high_ref[1, :, cols(j)] = dv[TILE + POS :].astype(BF)


CHUNK = 512
UNROLL = 2
KEYS = GROUP * TILE


def attend(span, queries, key_code, k, v, mask, rows, kx_ref, kt_ref, dk_ref, dv_ref, row_ref, put_dq):
    for s in range(2):
        row_ref[s] = rows[s]
    lane = lax.broadcasted_iota(jnp.int32, (KEYS, HEAD), 1)
    spread = (key_code == lane).astype(F32).astype(BF)
    padded = jnp.concatenate([mask.astype(F32), jnp.zeros((HEAD - GROUP, HEAD), F32)], 0)
    kx_ref[:, 0:HEAD] = k
    kx_ref[:, HEAD:] = ((nt(spread, padded.astype(BF)) - 1.0) * BIG).astype(BF)
    kt_ref[...] = k.astype(F32).T.astype(BF)
    dk_ref[...] = jnp.zeros_like(dk_ref)
    dv_ref[...] = jnp.zeros_like(dv_ref)
    count = CHUNK // span
    query = lax.broadcasted_iota(jnp.int32, (CHUNK, HEAD), 0) // span
    column = lax.broadcasted_iota(jnp.int32, (CHUNK, HEAD), 1)

    def one_chunk(c, carry):
        frames = pl.ds(c * count, count)
        q, g = queries(frames)
        choose = (column == query + c * count).astype(F32).astype(BF)
        qx = jnp.concatenate([q, choose], 1)
        lanes = CHUNK // HEAD
        lse, delta = (
            jnp.concatenate([row_ref[s, pl.ds(lanes * c + i, 1), :] for i in range(lanes)], 1) for s in range(2)
        )
        p = jnp.exp2(nt(kx_ref[...], qx) * (SCALE * LOG2E) - lse * LOG2E)
        ds = (p * (nt(v, g) - delta)).astype(BF)
        dv_ref[...] += nn(p.astype(BF), g)
        dk_ref[...] += nn(ds, q)
        put_dq(frames, (nn(kt_ref[...], ds) * SCALE).T.astype(BF).reshape(count, span, HEAD))
        return carry

    lax.fori_loop(0, GROUP * span // CHUNK, one_chunk, 0, unroll=UNROLL)


def added(stats, at):
    return (stats[:, at, :] + stats[:, at + 1, :]) + stats[:, at + 2, :]


def stacked(rows):
    rows = rows + [jnp.zeros((8 - len(rows), HEAD), F32)] if len(rows) < 8 else rows
    return jnp.concatenate(rows, 0)


def quarter_kernel(place_ref, *refs):
    ins, outs = refs[:SIDE], refs[SIDE : 2 * SIDE]
    q_ref, g_ref, kx_ref, kt_ref, dk_ref, dv_ref, row_ref = refs[2 * SIDE :]
    y, z = place_ref[0], place_ref[1]
    stats = jnp.concatenate([got[:, AS:ROWS_A, :] for got in ins], 0).astype(F32)
    rows = []
    for s in range(2):
        full = added(stats, 3 * s)
        rows.append(
            stacked(
                [
                    (full[i : i + 1] + full[i + 1 : i + 2]) + (full[i + 2 : i + 3] + full[i + 3 : i + 4])
                    for i in range(0, GROUP, SIDE)
                ]
            )
        )
    mask = jnp.where(y >= 2, stats[:, 7, :], stats[:, 6, :])
    k = jnp.concatenate([got[:, AK : AK + TILE, :] for got in ins], 0)
    v = jnp.concatenate([got[:, AV : AV + TILE, :] for got in ins], 0)
    for i, got in enumerate(ins):
        q_ref[SIDE * i : SIDE * i + SIDE] = got[:, AQ : AQ + HALF, :]
        g_ref[SIDE * i : SIDE * i + SIDE] = got[:, AG : AG + HALF, :]
    row = lax.broadcasted_iota(jnp.int32, (KEYS, HEAD), 0)
    source_y = (y + SIDE - row // (SIDE * TILE)) % SIDE
    source_z = (z + SIDE - (row // TILE) % SIDE) % SIDE
    key_code = (source_y * SIDE + source_z) * BLOCK + (row % TILE) // BLOCK

    def queries(frames):
        return q_ref[frames].reshape(CHUNK, HEAD), g_ref[frames].reshape(CHUNK, HEAD)

    def put_dq(frames, dq):
        q_ref[frames] = dq

    attend(
        HALF, queries, key_code, k.reshape(KEYS, HEAD), v.reshape(KEYS, HEAD), mask, rows,
        kx_ref, kt_ref, dk_ref, dv_ref, row_ref, put_dq,
    )
    span = SIDE * TILE
    for i, out in enumerate(outs):
        dk = (dk_ref[i * span : i * span + span] * SCALE).astype(BF)
        dv = dv_ref[i * span : i * span + span].astype(BF)
        out[:, RK : RK + TILE, :] = dk.reshape(SIDE, TILE, HEAD)
        out[:, RV : RV + TILE, :] = dv.reshape(SIDE, TILE, HEAD)
        out[:, RQ : RQ + HALF, :] = q_ref[SIDE * i : SIDE * i + SIDE]


def merge_kernel(place_ref, *refs):
    ins, outs, sum_ref = refs[:SIDE], refs[SIDE : 2 * SIDE], refs[2 * SIDE]
    sum_ref[...] = jnp.zeros_like(sum_ref)
    for dy, got in enumerate(ins):
        y = lax.rem(place_ref[0] + dy, SIDE)
        tile = pl.multiple_of((y // 2) * TILE, TILE)
        half = pl.multiple_of(y * HALF, HALF)
        for dz, out in enumerate(outs):
            out[pl.ds(BQ + half, HALF), :] = got[dz, RQ:ROWS_R, :]
            sum_ref[dz, 0, pl.ds(tile, TILE), :] += got[dz, RK : RK + TILE, :].astype(F32)
            sum_ref[dz, 1, pl.ds(tile, TILE), :] += got[dz, RV : RV + TILE, :].astype(F32)
    for dz, out in enumerate(outs):
        out[BK : BK + POS, :] = sum_ref[dz, 0].astype(BF)
        out[BV : BV + POS, :] = sum_ref[dz, 1].astype(BF)


def head_kernel(in_hbm, out_hbm, in_ref, out_ref, sems, *scratch):
    copies = Copies(sems)

    def fetch(key, first, count):
        copies.start(key, in_hbm.at[:, first : first + count, :], in_ref.at[:, first : first + count, :])

    fetch("stats", BS, ROWS_B - BS)
    for unit in range(2):
        for at in (BK, BV, BQ, BG):
            fetch(unit, at + unit * TILE, TILE)
    key_code = lax.broadcasted_iota(jnp.int32, (KEYS, HEAD), 0) // BLOCK
    lane = lax.broadcasted_iota(jnp.int32, (1, HEAD), 1)
    copies.wait("stats")
    stats = in_ref[:, BS:ROWS_B, :].astype(F32)
    for unit in range(2):
        at = unit * TILE
        rows = []
        for s in range(2):
            full = added(stats, 3 * s)
            turned = pltpu.roll(full, TILE, 1)
            left, right = (full, turned) if unit == 0 else (turned, full)
            rows.append(
                stacked(
                    [jnp.where(lane < TILE, left[i : i + 1], right[i + 1 : i + 2]) for i in range(0, GROUP, 2)]
                )
            )

        def queries(frames):
            q = in_ref[frames, BQ + at : BQ + at + TILE, :].reshape(CHUNK, HEAD)
            g = in_ref[frames, BG + at : BG + at + TILE, :].reshape(CHUNK, HEAD)
            return q, g

        def put_dq(frames, dq):
            out_ref[frames, BQ + at : BQ + at + TILE, :] = dq

        copies.wait(unit)
        attend(
            TILE, queries, key_code,
            in_ref[:, BK + at : BK + at + TILE, :].reshape(KEYS, HEAD),
            in_ref[:, BV + at : BV + at + TILE, :].reshape(KEYS, HEAD),
            stats[:, 6 + unit, :], rows, *scratch, put_dq,
        )
        dk_ref, dv_ref = scratch[2:4]
        dk = (dk_ref[...] * SCALE).astype(BF).reshape(GROUP, TILE, HEAD)
        out_ref[:, BK + at : BK + at + TILE, :] = dk
        out_ref[:, BV + at : BV + at + TILE, :] = dv_ref[...].astype(BF).reshape(GROUP, TILE, HEAD)
        for first in (BQ + at, BK + at, BV + at):
            part = slice(first, first + TILE)
            copies.start("out", out_ref.at[:, part, :], out_hbm.at[:, part, :])
    copies.wait_all()


def join_kernel(
    place_ref, z0_hbm, z1_hbm, z2_hbm, z3_hbm, b_hbm, sums_in, left_in, right_in, dq_out, dk_out, dv_out,
    a_ref, b_ref, sums_ref, left_ref, right_ref, low_ref, sems,
):
    copies = Copies(sems)
    sets = ((dq_out, BQ), (dk_out, BK), (dv_out, BV))
    order = [SIDE] + list(range(SIDE))
    for block in order:
        at = slice(block * WIDE, block * WIDE + WIDE)
        if block == SIDE:
            for dz, share in enumerate((z0_hbm, z1_hbm, z2_hbm, z3_hbm)):
                copies.start(block, share, a_ref.at[dz])
        else:
            four = slice(SIDE * block, SIDE * block + SIDE)
            copies.start(block, b_hbm.at[four], b_ref.at[four])
        copies.start(block, sums_in.at[:, :, at], sums_ref.at[:, :, at])
        copies.start(block, left_in.at[:, :, at], left_ref.at[:, :, at])
        copies.start(block, right_in.at[:, :, at], right_ref.at[:, :, at])
    for block in order:
        copies.wait(block)
        at = slice(block * WIDE, block * WIDE + WIDE)
        for which, (out, row) in enumerate(sets):
            for j in range(SIDE):
                h = SIDE * block + j
                if block < SIDE:
                    more = b_ref[h, row : row + POS, :].astype(F32)
                else:
                    dz = lax.rem(j + SIDE - place_ref[1], SIDE)
                    more = a_ref[dz, row : row + POS, :].astype(F32)
                if which:
                    edges = [left_ref[which - 1, :, cols(h)], right_ref[which - 1, :, cols(h)]]
                    more = more + jnp.concatenate(edges, 0).astype(F32)
                low_ref[which, :, cols(h)] = (sums_ref[which, :, cols(h)] + more).astype(BF)
            copies.start("out", low_ref.at[which, :, at], out.at[:, at])
    copies.wait_all()


VMEM = pl.BlockSpec(memory_space=pltpu.VMEM)
SMEM = pl.BlockSpec(memory_space=pltpu.SMEM)
ANY = pl.BlockSpec(memory_space=pl.ANY)
MIB = 1024 * 1024


def room(mib):
    return pltpu.CompilerParams(vmem_limit_bytes=mib * MIB)


SCRATCH = [
    pltpu.VMEM((KEYS, 2 * HEAD), BF),
    pltpu.VMEM((HEAD, KEYS), BF),
    pltpu.VMEM((KEYS, HEAD), F32),
    pltpu.VMEM((KEYS, HEAD), F32),
    pltpu.VMEM((2, 8, HEAD), F32),
]


def shape(*dims, dtype=BF):
    return jax.ShapeDtypeStruct(dims, dtype)


def cost(us):
    return pl.CostEstimate(flops=0, bytes_accessed=int(us * 3_000_000), transcendentals=0)


def cost(us):
    return pl.CostEstimate(flops=0, bytes_accessed=int(us * 3_000_000), transcendentals=0)


def pack_a_call(*args):
    halo = shape(2, TILE, args[4].shape[1])
    return pl.pallas_call(
        pack_a_kernel,
        out_shape=(shape(ROWS_B, HEAD),) * SIDE + (halo, halo),
        in_specs=[SMEM] * 3 + [VMEM] + [ANY] * 5,
        out_specs=[ANY] * (SIDE + 2),
        scratch_shapes=[pltpu.VMEM((POS, WIDE), BF)] * 5
        + [
            pltpu.VMEM((SIDE, ROWS_B, HEAD), BF),
            pltpu.VMEM((2, *halo.shape), BF),
            pltpu.SemaphoreType.DMA((15,)),
        ],
        compiler_params=room(60),
        cost_estimate=cost(3),
        name="pack_a",
    )(*args)


def pack_b_call(*args):
    q = args[4]
    return pl.pallas_call(
        pack_b_kernel,
        out_shape=shape(GROUP, ROWS_B, HEAD),
        in_specs=[SMEM] * 3 + [VMEM] + [ANY] * 5,
        out_specs=ANY,
        scratch_shapes=[pltpu.VMEM(q.shape, BF)] * 5
        + [pltpu.VMEM((GROUP, ROWS_B, HEAD), BF), pltpu.SemaphoreType.DMA((24,))],
        compiler_params=room(60),
        cost_estimate=cost(4),
        name="pack_b",
    )(*args)


def four_call(kernel, rows, scratch, us, name, place, shares):
    return pl.pallas_call(
        kernel,
        out_shape=(rows,) * SIDE,
        in_specs=[SMEM] + [VMEM] * SIDE,
        out_specs=[VMEM] * SIDE,
        scratch_shapes=scratch,
        compiler_params=room(32),
        cost_estimate=cost(us),
        name=name,
    )(place, *shares)


def head_call(arrived):
    return pl.pallas_call(
        head_kernel,
        out_shape=shape(GROUP, BACK_B, HEAD),
        in_specs=[ANY],
        out_specs=ANY,
        scratch_shapes=[
            pltpu.VMEM((GROUP, ROWS_B, HEAD), BF),
            pltpu.VMEM((GROUP, BACK_B, HEAD), BF),
            pltpu.SemaphoreType.DMA((15,)),
        ]
        + SCRATCH,
        compiler_params=room(60),
        cost_estimate=cost(8),
        name="head",
    )(arrived)


def join_call(place, shares, b, sums, left, right):
    out = shape(*sums.shape[1:])
    return pl.pallas_call(
        join_kernel,
        out_shape=(out,) * 3,
        in_specs=[SMEM] + [ANY] * (SIDE + 4),
        out_specs=[ANY] * 3,
        scratch_shapes=[pltpu.VMEM((SIDE, BACK_B, HEAD), BF)]
        + [pltpu.VMEM(x.shape, x.dtype) for x in (b, sums, left, right)]
        + [pltpu.VMEM(sums.shape, BF), pltpu.SemaphoreType.DMA((38,))],
        compiler_params=room(60),
        cost_estimate=cost(4),
        name="join",
    )(place, *shares, b, sums, left, right)


def own_call(sides, q, k, v, o, g, before, after, lse):
    feature = q.shape[1]
    rows = pl.BlockSpec((POS, WIDE), lambda i: (0, i))
    edge = pl.BlockSpec((2, TILE, WIDE), lambda i: (0, 0, i))
    whole = pl.BlockSpec(lse.shape, lambda i: (0, 0, 0))
    halo = shape(2, TILE, feature)
    return pl.pallas_call(
        own_kernel,
        grid=(feature // WIDE,),
        out_shape=(shape(3, POS, feature, dtype=F32), halo, halo),
        in_specs=[SMEM] + [rows] * 5 + [edge, edge, whole],
        out_specs=[pl.BlockSpec((3, POS, WIDE), lambda i: (0, 0, i)), edge, edge],
        compiler_params=room(63),
        cost_estimate=cost(9),
        name="own",
    )(sides, q, k, v, o, g, before, after, lse)


def around(axis_step, shares):
    def partner(i, step):
        y, z = i // SIDE, i % SIDE
        return (y + step[0]) % SIDE * SIDE + (z + step[1]) % SIDE

    out = [shares[0], None, None, None]
    for d in (2, 1, 3):
        step = (d * axis_step[0], d * axis_step[1])
        out[d] = lax.ppermute(shares[d], "group", [(i, partner(i, step)) for i in range(GROUP)])
    return out


def body(query_rows, key_rows, value_rows, out_rows, grad_out, log_sum_exp, far_frames, far_blocks):
    rows = tuple(a[0] for a in (query_rows, key_rows, value_rows, out_rows, grad_out))
    lse = jnp.transpose(log_sum_exp, (1, 0, 2))
    inner = lax.axis_size("inner")
    inner_at = lax.axis_index("inner").astype(jnp.int32)
    group_at = lax.axis_index("group").astype(jnp.int32)
    sides = jnp.stack([inner_at, jnp.full((), inner, jnp.int32)])
    up = [(i, i + 1) for i in range(inner - 1)]
    down = [(i + 1, i) for i in range(inner - 1)]
    place = jnp.stack([group_at // SIDE, group_at % SIDE])
    facts = (place, far_frames[0], far_blocks[0], lse)

    *sends_z, first_rows, last_rows = pack_a_call(*facts, *rows)
    got_z = around((0, 1), sends_z)
    before = lax.ppermute(last_rows, "inner", up)
    after = lax.ppermute(first_rows, "inner", down)
    send_b = pack_b_call(*facts, *rows)
    send_b, got_z, before, after = lax.optimization_barrier((send_b, got_z, before, after))
    got_b = lax.all_to_all(send_b, "group", 0, 0, tiled=True)

    sends_y = four_call(split_kernel, shape(SIDE, ROWS_A, HEAD), [], 3, "split", place, got_z)
    got_y = around((1, 0), sends_y)
    sums, to_low, to_high = own_call(sides, *rows, before, after, lse)
    got_y, to_low, to_high = lax.optimization_barrier((got_y, to_low, to_high))
    from_right = lax.ppermute(to_low, "inner", down)
    from_left = lax.ppermute(to_high, "inner", up)
    scratch = [pltpu.VMEM((GROUP, HALF, HEAD), BF)] * 2 + SCRATCH
    back_y = four_call(quarter_kernel, shape(SIDE, ROWS_R, HEAD), scratch, 3, "quarter", place, got_y)
    home_y = around((-1, 0), back_y)
    scratch = [pltpu.VMEM((SIDE, 2, POS, HEAD), F32)]
    back_z = four_call(merge_kernel, shape(BACK_B, HEAD), scratch, 3, "merge", place, home_y)

    got_b, back_z = lax.optimization_barrier((got_b, back_z))
    home_z = around((0, -1), back_z)
    back_b, from_left, from_right = lax.optimization_barrier((head_call(got_b), from_left, from_right))
    home_b = lax.all_to_all(back_b, "group", 0, 0, tiled=True)
    return tuple(a[None] for a in join_call(place, home_z, home_b, sums, from_left, from_right))


def solution(mesh):
    shard = P("group", "inner", None)
    return jax.shard_map(
        body,
        mesh=mesh,
        in_specs=(shard,) * 5 + (P("group", None, "inner"), shard, shard),
        out_specs=(shard,) * 3,
        check_vma=False,
    )
```

time: 203 us -> 165 us (0.81)
  blocking collectives: 77 us -> 0 us
  starting transfers between devices: 21.2 us -> 50.4 us
  local copies, waits for them, and re-layouts: 13.1 us -> 3.5 us
  waiting for transfers between devices: 62.5 us -> 71.7 us
  Pallas kernels: 27.1 us -> 34.5 us
    all_to_all x1 -> x0, blocking collectives: 77 us -> none  [body(): arrived = lax.all_to_all(send, 'group', 0, 0, tiled=True)]
    ppermute x0 -> x12, waiting for transfers between devices: none -> 71.7 us  [around(): lax.ppermute(shares[d], 'group', [(i, partner(i, step)) for i in range(GR...]
    ppermute x1, waiting for transfers between devices: 48.8 us -> 0.01 us  [body(): before = lax.ppermute(last_rows, 'inner', up)]
    ppermute x0 -> x12, starting transfers between devices: none -> 23.5 us  [around(): lax.ppermute(shares[d], 'group', [(i, partner(i, step)) for i in range(GR...]
    unnamed x33 -> x20, local copies, waits for them, and re-layouts: 13.1 us -> 3.5 us
    all_to_all x1 -> x2, starting transfers between devices: 7.47 us -> 15.6 us  [the longest x1 8.83 us: body(): home_b = lax.all_to_all(back_b, 'group', 0, 0, tiled=True)]
    pallas_call x4 -> x8, Pallas kernels: 27.1 us -> 34.5 us  [the longest x1 8.98 us: own_call(): pl.pallas_call(own_kernel, grid=(feature // WIDE,), out_shape=(shape(3, P...]
    ppermute x1, waiting for transfers between devices: 6.51 us -> 0.01 us  [body(): from_right = lax.ppermute(to_low, 'inner', down)]
  transfers between devices with their start and end apart: 5 -> 18, of which waited for: 4 -> 9; matrix products, arithmetic and copies ran while one was open for 0% -> 0% of each run, Pallas kernels for 4% -> 16%
where the time goes in v2:
time: 165 us; the launch traced here: 162 us
  waiting for transfers between devices  71.7 us (43%)
  starting transfers between devices  50.4 us (31%)
  Pallas kernels  34.5 us (21%)
  local copies, waits for them, and re-layouts  3.5 us (2%)
    ppermute x12, waiting for transfers between devices, around(): lax.ppermute(shares[d], 'group', [(i, partner(i, step)) for i in range(GR...  71.7 us
    ppermute x12, starting transfers between devices, around(): lax.ppermute(shares[d], 'group', [(i, partner(i, step)) for i in range(GR...  23.5 us
    pallas_call x1, Pallas kernels, own_call(): pl.pallas_call(own_kernel, grid=(feature // WIDE,), out_shape=(shape(3, P...  8.98 us
    all_to_all x1, starting transfers between devices, body(): home_b = lax.all_to_all(back_b, 'group', 0, 0, tiled=True)  8.83 us
    pallas_call x1, Pallas kernels, head_call(): pl.pallas_call(head_kernel, out_shape=shape(GROUP, BACK_B, HEAD), in_spec...  7.99 us
    all_to_all x1, starting transfers between devices, body(): got_b = lax.all_to_all(send_b, 'group', 0, 0, tiled=True)  6.77 us
    pallas_call x1, Pallas kernels, join_call(): pl.pallas_call(join_kernel, out_shape=(out,) * 3, in_specs=[SMEM] + [ANY]...  5.3 us
    pallas_call x3, Pallas kernels, four_call(): pl.pallas_call(kernel, out_shape=(rows,) * SIDE, in_specs=[SMEM] + [VMEM]...  4.94 us
  transfers between devices with their start and end apart: 18, of which 9 were waited for; matrix products, arithmetic and copies ran while one was open for 0% of the time, Pallas kernels for 16%

profile of v2, /device:TPU:23, one launch (start us, length us, event | category | flops | bytes accessed | tf_op | source)
XLA Modules:
  0.0 162.3 jit_solution(8572942558849975326)
XLA Ops:
  0.7 0.6 pad_add_fusion.place_ref
  1.3 3.5 %pack_a.1 = (bf16[528,128]{1,0:T(8,128)(2,1)}, bf16[528,128]{1,0:T(8,128)(2,1)}, bf16[528,128]{1,0:T(8,128)(2,1)}, bf16[528,128]{1,0:T(8,128)(2,1)}, bf16[2,64,2...) custom-call(s32[2]{0:T(128)} %pad_add_fusion.place_ref, s32[2,11]{1,0:T(2,128)} %bitcast.32, s32[2,11]{1,0:T(2,128)} %bitcast.34, ...), custom_call_target="tpu_custom_call" | custom-call | bytes 9000000 | tf_op jit(solution)/shard_map/pack_a/pallas_call | solution.py:456
  4.7 4.0 %collective-permute-start.3 = (bf16[2,64,2560]{2,1,0:T(8,128)(2,1)}, bf16[2,64,2560]{2,1,0:T(8,128)(2,1)S(1)}, u32[]{:S(2)}, u32[]{:S(2)}) collective-permute-start(bf16[2,64,2560]{2,1,0:T(8,128)(2,1)} %get-tuple-element.52), channel_id=1, source_target_pairs={{0,1},{1,2},{2,3},{3,4},{4,5},{5,6},{6,7},{7,8},{8,9},{9,10},{10,1... | collective-permute-start | bytes 1966088 | tf_op jit(solution)/shard_map/ppermute | solution.py:579
  8.8 1.9 %collective-permute-start.4 = (bf16[2,64,2560]{2,1,0:T(8,128)(2,1)}, bf16[2,64,2560]{2,1,0:T(8,128)(2,1)S(1)}, u32[]{:S(2)}, u32[]{:S(2)}) collective-permute-start(bf16[2,64,2560]{2,1,0:T(8,128)(2,1)} %get-tuple-element.53), channel_id=1, source_target_pairs={{1,0},{2,1},{3,2},{4,3},{5,4},{6,5},{7,6},{8,7},{9,8},{10,9},{11,1... | collective-permute-start | bytes 1966088 | tf_op jit(solution)/shard_map/ppermute | solution.py:580
  10.7 3.1 %collective-permute-start = (bf16[528,128]{1,0:T(8,128)(2,1)}, bf16[528,128]{1,0:T(8,128)(2,1)S(1)}, u32[]{:S(2)}, u32[]{:S(2)}) collective-permute-start(bf16[528,128]{1,0:T(8,128)(2,1)} %get-tuple-element.49), channel_id=1, source_target_pairs={{0,16},{16,32},{32,48},{48,0},{64,80},{80,96},{96,112},{112,64},{1... | collective-permute-start | bytes 405512 | tf_op jit(solution)/shard_map/ppermute | solution.py:561
  13.8 4.2 %collective-permute-start.1 = (bf16[528,128]{1,0:T(8,128)(2,1)}, bf16[528,128]{1,0:T(8,128)(2,1)S(1)}, u32[]{:S(2)}, u32[]{:S(2)}) collective-permute-start(bf16[528,128]{1,0:T(8,128)(2,1)} %get-tuple-element.50), channel_id=1, source_target_pairs={{0,32},{16,48},{32,0},{48,16},{64,96},{80,112},{96,64},{112,80},{1... | collective-permute-start | bytes 405512 | tf_op jit(solution)/shard_map/ppermute | solution.py:561
  18.0 2.4 %collective-permute-start.2 = (bf16[528,128]{1,0:T(8,128)(2,1)}, bf16[528,128]{1,0:T(8,128)(2,1)S(1)}, u32[]{:S(2)}, u32[]{:S(2)}) collective-permute-start(bf16[528,128]{1,0:T(8,128)(2,1)} %get-tuple-element.51), channel_id=1, source_target_pairs={{0,48},{16,0},{32,16},{48,32},{64,112},{80,64},{96,80},{112,96},{1... | collective-permute-start | bytes 405512 | tf_op jit(solution)/shard_map/ppermute | solution.py:561
  20.4 3.8 %pack_b.1 = bf16[16,528,128]{2,1,0:T(8,128)(2,1)} custom-call(s32[2]{0:T(128)} %pad_add_fusion.place_ref, s32[2,11]{1,0:T(2,128)} %bitcast.33, s32[2,11]{1,0:T(2,128)} %bitcast.35, f32[20,1,128]{2,1,0:T(1,128)} %bitcast.30, bf16[128,2560]{1,0:T(8,128)(2,1)} %bitcast.15, bf16[128,2560]{1,0:T(8,128)(2,1)} %bitcast.18, bf16[128,2560]{1,0:T(8,128)(2,1)} %bitcast.21, ...), custom_call_target="tpu_custom_call" | custom-call | bytes 12000000 | tf_op jit(solution)/shard_map/pack_b/pallas_call | solution.py:475
  24.2 6.6 %collective-permute-done.refs_1_ = bf16[528,128]{1,0:T(8,128)(2,1)S(1)} collective-permute-done((bf16[528,128]{1,0:T(8,128)(2,1)}, bf16[528,128]{1,0:T(8,128)(2,1)S(1)}, u32[]{:S(2)}, u32[]{:S(2)}) %collective-permute-start) | collective-permute-done | bytes 135200 | tf_op jit(solution)/shard_map/ppermute | solution.py:561
  30.8 2.4 %collective-permute-done.1.refs_2_ = bf16[528,128]{1,0:T(8,128)(2,1)S(1)} collective-permute-done((bf16[528,128]{1,0:T(8,128)(2,1)}, bf16[528,128]{1,0:T(8,128)(2,1)S(1)}, u32[]{:S(2)}, u32[]{:S(2)}) %collective-permute-start.1) | collective-permute-done | bytes 135200 | tf_op jit(solution)/shard_map/ppermute | solution.py:561
  33.2 0.0 collective-permute-done.2.refs_3_
  33.2 0.0 collective-permute-done.4.after_ref
  33.2 0.8 copy-done.5
  34.0 0.8 copy-done.6
  34.8 6.8 %all-to-all-start = ((bf16[16,528,128]{2,1,0:T(8,128)(2,1)}), bf16[16,528,128]{2,1,0:T(8,128)(2,1)}, u32[]{:S(2)}, u32[]{:S(2)}) async-start(bf16[16,528,128]{2,1,0:T(8,128)(2,1)} %pack_b.1), calls=%async_computation | async-start | bytes 4325376 | tf_op jit(solution)/shard_map/all_to_all | solution.py:583
  41.6 1.6 split.1
  43.2 0.9 collective-permute-start.5
  44.1 0.6 collective-permute-start.6
  44.7 0.8 collective-permute-start.7
  45.4 0.7 pad_add_fusion.1.side_ref
  46.1 9.0 %own.1 = (f32[3,128,2560]{2,1,0:T(8,128)}, bf16[2,64,2560]{2,1,0:T(8,128)(2,1)}, bf16[2,64,2560]{2,1,0:T(8,128)(2,1)}) custom-call(s32[2]{0:T(128)} %pad_add_fusion.1.side_ref, bf16[128,2560]{1,0:T(8,128)(2,1)} %bitcast.16, bf16[128,2560]{1,0:T(8,128)(2,1)} %bitcast.19, bf16[128,2560]{1,0:T(8,128)(2,1)} %bitcast.22, bf16[128,2560]{1,0:T(8,128)(2,1)} %bitcast.25, ...), custom_call_target="tpu_custom_call" | custom-call | bytes 27000000 | tf_op jit(solution)/shard_map/own/pallas_call | solution.py:541
  55.1 0.0 collective-permute-done.5.refs_1_
  55.1 6.6 %collective-permute-done.6.refs_2_ = bf16[4,208,128]{2,1,0:T(8,128)(2,1)S(1)} collective-permute-done((bf16[4,208,128]{2,1,0:T(8,128)(2,1)}, bf16[4,208,128]{2,1,0:T(8,128)(2,1)S(1)}, u32[]{:S(2)}, u32[]{:S(2)}) %collective-permute-start.6) | collective-permute-done | bytes 213024 | tf_op jit(solution)/shard_map/ppermute | solution.py:561
  61.7 2.5 %collective-permute-done.7.refs_3_ = bf16[4,208,128]{2,1,0:T(8,128)(2,1)S(1)} collective-permute-done((bf16[4,208,128]{2,1,0:T(8,128)(2,1)}, bf16[4,208,128]{2,1,0:T(8,128)(2,1)S(1)}, u32[]{:S(2)}, u32[]{:S(2)}) %collective-permute-start.7) | collective-permute-done | bytes 213024 | tf_op jit(solution)/shard_map/ppermute | solution.py:561
  64.1 2.6 %collective-permute-start.14 = (bf16[2,64,2560]{2,1,0:T(8,128)(2,1)}, bf16[2,64,2560]{2,1,0:T(8,128)(2,1)S(1)}, u32[]{:S(2)}, u32[]{:S(2)}) collective-permute-start(bf16[2,64,2560]{2,1,0:T(8,128)(2,1)} %get-tuple-element.84), channel_id=1, source_target_pairs={{0,1},{1,2},{2,3},{3,4},{4,5},{5,6},{6,7},{7,8},{8,9},{9,10},{10,1... | collective-permute-start | bytes 1966088 | tf_op jit(solution)/shard_map/ppermute | solution.py:590
  66.8 2.7 %collective-permute-start.15 = (bf16[2,64,2560]{2,1,0:T(8,128)(2,1)}, bf16[2,64,2560]{2,1,0:T(8,128)(2,1)}, u32[]{:S(2)}, u32[]{:S(2)}) collective-permute-start(bf16[2,64,2560]{2,1,0:T(8,128)(2,1)} %get-tuple-element.85), channel_id=1, source_target_pairs={{1,0},{2,1},{3,2},{4,3},{5,4},{6,5},{7,6},{8,7},{9,8},{10,9},{11,1... | collective-permute-start | bytes 1966088 | tf_op jit(solution)/shard_map/ppermute | solution.py:589
  69.5 2.7 %quarter.1 = (bf16[4,160,128]{2,1,0:T(8,128)(2,1)S(1)}, bf16[4,160,128]{2,1,0:T(8,128)(2,1)S(1)}, bf16[4,160,128]{2,1,0:T(8,128)(2,1)S(1)}, bf16[4,160,128]{2,1,0:T(8,128)(2,1)S(1)}) custom-call(s32[2]{0:T(128)S(1)} %copy-done.2, bf16[4,208,128]{2,1,0:T(8,128)(2,1)S(1)} %get-tuple-element.67.refs_0_, ...), custom_call_target="tpu_custom_call" | custom-call | bytes 9000000 | tf_op jit(solution)/shard_map/quarter/pallas_call | solution.py:489
  72.2 0.1 collective-permute-start.8
  72.3 2.1 %collective-permute-start.9 = (bf16[4,160,128]{2,1,0:T(8,128)(2,1)S(1)}, bf16[4,160,128]{2,1,0:T(8,128)(2,1)S(1)}, u32[]{:S(2)}, u32[]{:S(2)}) collective-permute-start(bf16[4,160,128]{2,1,0:T(8,128)(2,1)S(1)} %get-tuple-element.73), channel_id=1, source_target_pairs={{0,128},{16,144},{32,160},{48,176},{64,192},{80,208},{96,224},{112... | collective-permute-start | bytes 491528 | tf_op jit(solution)/shard_map/ppermute | solution.py:561
  74.4 2.0 %collective-permute-start.10 = (bf16[4,160,128]{2,1,0:T(8,128)(2,1)S(1)}, bf16[4,160,128]{2,1,0:T(8,128)(2,1)S(1)}, u32[]{:S(2)}, u32[]{:S(2)}) collective-permute-start(bf16[4,160,128]{2,1,0:T(8,128)(2,1)S(1)} %get-tuple-element.74), channel_id=1, source_target_pairs={{0,64},{16,80},{32,96},{48,112},{64,128},{80,144},{96,160},{112,17... | collective-permute-start | bytes 491528 | tf_op jit(solution)/shard_map/ppermute | solution.py:561
  76.3 8.3 %collective-permute-done.8.refs_1_ = bf16[4,160,128]{2,1,0:T(8,128)(2,1)S(1)} collective-permute-done((bf16[4,160,128]{2,1,0:T(8,128)(2,1)S(1)}, bf16[4,160,128]{2,1,0:T(8,128)(2,1)S(1)}, u32[]{:S(2)}, u32[]{:S(2)}) %collective-permute-start.8) | collective-permute-done | bytes 163872 | tf_op jit(solution)/shard_map/ppermute | solution.py:561
  84.6 0.8 collective-permute-done.9.refs_2_
  85.4 5.3 %collective-permute-done.10.refs_3_ = bf16[4,160,128]{2,1,0:T(8,128)(2,1)S(1)} collective-permute-done((bf16[4,160,128]{2,1,0:T(8,128)(2,1)S(1)}, bf16[4,160,128]{2,1,0:T(8,128)(2,1)S(1)}, u32[]{:S(2)}, u32[]{:S(2)}) %collective-permute-start.10) | collective-permute-done | bytes 163872 | tf_op jit(solution)/shard_map/ppermute | solution.py:561
  90.7 0.7 merge.1
  91.4 0.6 copy-done.1
  92.0 8.0 %head.1 = bf16[16,384,128]{2,1,0:T(8,128)(2,1)} custom-call(bf16[16,528,128]{2,1,0:T(8,128)(2,1)} %all-to-all-done.in_hbm), custom_call_target="tpu_custom_call" | custom-call | bytes 24000000 | tf_op jit(solution)/shard_map/head/pallas_call | solution.py:502
  100.0 0.0 collective-permute-done.15.right_in
  100.1 8.8 %all-to-all-start.1 = ((bf16[16,384,128]{2,1,0:T(8,128)(2,1)}), bf16[16,384,128]{2,1,0:T(8,128)(2,1)S(1)}, u32[]{:S(2)}, u32[]{:S(2)}) async-start(bf16[16,384,128]{2,1,0:T(8,128)(2,1)} %head.1), calls=%async_computation.1 | async-start | bytes 3145728 | tf_op jit(solution)/shard_map/all_to_all | solution.py:600
  108.9 3.3 %collective-permute-start.11 = (bf16[384,128]{1,0:T(8,128)(2,1)S(1)}, bf16[384,128]{1,0:T(8,128)(2,1)S(1)}, u32[]{:S(2)}, u32[]{:S(2)}) collective-permute-start(bf16[384,128]{1,0:T(8,128)(2,1)S(1)} %get-tuple-element.80), channel_id=1, source_target_pairs={{0,48},{16,0},{32,16},{48,32},{64,112},{80,64},{96,80},{112,96},{1... | collective-permute-start | bytes 294920 | tf_op jit(solution)/shard_map/ppermute | solution.py:561
  112.2 2.1 %collective-permute-start.12 = (bf16[384,128]{1,0:T(8,128)(2,1)S(1)}, bf16[384,128]{1,0:T(8,128)(2,1)S(1)}, u32[]{:S(2)}, u32[]{:S(2)}) collective-permute-start(bf16[384,128]{1,0:T(8,128)(2,1)S(1)} %get-tuple-element.81), channel_id=1, source_target_pairs={{0,32},{16,48},{32,0},{48,16},{64,96},{80,112},{96,64},{112,80},{1... | collective-permute-start | bytes 294920 | tf_op jit(solution)/shard_map/ppermute | solution.py:561
  114.3 2.1 %collective-permute-start.13 = (bf16[384,128]{1,0:T(8,128)(2,1)S(1)}, bf16[384,128]{1,0:T(8,128)(2,1)S(1)}, u32[]{:S(2)}, u32[]{:S(2)}) collective-permute-start(bf16[384,128]{1,0:T(8,128)(2,1)S(1)} %get-tuple-element.82), channel_id=1, source_target_pairs={{0,16},{16,32},{32,48},{48,0},{64,80},{80,96},{96,112},{112,64},{1... | collective-permute-start | bytes 294920 | tf_op jit(solution)/shard_map/ppermute | solution.py:561
  116.3 37.0 %collective-permute-done.11.z1_hbm = bf16[384,128]{1,0:T(8,128)(2,1)S(1)} collective-permute-done((bf16[384,128]{1,0:T(8,128)(2,1)S(1)}, bf16[384,128]{1,0:T(8,128)(2,1)S(1)}, u32[]{:S(2)}, u32[]{:S(2)}) %collective-permute-start.11) | collective-permute-done | bytes 98336 | tf_op jit(solution)/shard_map/ppermute | solution.py:561
  153.4 0.0 collective-permute-done.12.z2_hbm
  153.4 2.2 %collective-permute-done.13.z3_hbm = bf16[384,128]{1,0:T(8,128)(2,1)S(1)} collective-permute-done((bf16[384,128]{1,0:T(8,128)(2,1)S(1)}, bf16[384,128]{1,0:T(8,128)(2,1)S(1)}, u32[]{:S(2)}, u32[]{:S(2)}) %collective-permute-start.13) | collective-permute-done | bytes 98336 | tf_op jit(solution)/shard_map/ppermute | solution.py:561
  155.6 0.0 all-to-all-done.1.b_hbm
  155.7 0.6 copy-done.9
  156.3 0.6 copy-done.3
  156.9 5.3 %join.1 = (bf16[128,2560]{1,0:T(8,128)(2,1)}, bf16[128,2560]{1,0:T(8,128)(2,1)}, bf16[128,2560]{1,0:T(8,128)(2,1)}) custom-call(s32[2]{0:T(128)} %pad_add_fusion.place_ref, bf16[384,128]{1,0:T(8,128)(2,1)} %copy-done.1, bf16[384,128]{1,0:T(8,128)(2,1)} %copy-done.7, bf16[384,128]{1,0:T(8,128)(2,1)} %copy-done.8, bf16[384,128]{1,0:T(8,128)(2,1)} %copy-done.9, ...), custom_call_target="tpu_custom_call" | custom-call | bytes 12000000 | tf_op jit(solution)/shard_map/join/pallas_call | solution.py:521
  (18 shorter events, 0.0 us)
Async XLA Ops:
  4.7 28.4 %collective-permute-start.3 = (bf16[2,64,2560]{2,1,0:T(8,128)(2,1)}, bf16[2,64,2560]{2,1,0:T(8,128)(2,1)S(1)}, u32[]{:S(2)}, u32[]{:S(2)}) collective-permute-start(bf16[2,64,2560]{2,1,0:T(8,128)(2,1)} %get-tuple-element.52), channel_id=1, source_target_pairs={{0,1},{1,2},{2,3},{3,4},{4,5},{5,6},{6,7},{7,8},{8,9},{9,10},{10,1... | collective-permute-start | bytes 1966088 | tf_op jit(solution)/shard_map/ppermute | solution.py:579
  8.8 24.4 %collective-permute-start.4 = (bf16[2,64,2560]{2,1,0:T(8,128)(2,1)}, bf16[2,64,2560]{2,1,0:T(8,128)(2,1)S(1)}, u32[]{:S(2)}, u32[]{:S(2)}) collective-permute-start(bf16[2,64,2560]{2,1,0:T(8,128)(2,1)} %get-tuple-element.53), channel_id=1, source_target_pairs={{1,0},{2,1},{3,2},{4,3},{5,4},{6,5},{7,6},{8,7},{9,8},{10,9},{11,1... | collective-permute-start | bytes 1966088 | tf_op jit(solution)/shard_map/ppermute | solution.py:580
  10.7 20.1 %collective-permute-start = (bf16[528,128]{1,0:T(8,128)(2,1)}, bf16[528,128]{1,0:T(8,128)(2,1)S(1)}, u32[]{:S(2)}, u32[]{:S(2)}) collective-permute-start(bf16[528,128]{1,0:T(8,128)(2,1)} %get-tuple-element.49), channel_id=1, source_target_pairs={{0,16},{16,32},{32,48},{48,0},{64,80},{80,96},{96,112},{112,64},{1... | collective-permute-start | bytes 405512 | tf_op jit(solution)/shard_map/ppermute | solution.py:561
  13.8 19.4 %collective-permute-start.1 = (bf16[528,128]{1,0:T(8,128)(2,1)}, bf16[528,128]{1,0:T(8,128)(2,1)S(1)}, u32[]{:S(2)}, u32[]{:S(2)}) collective-permute-start(bf16[528,128]{1,0:T(8,128)(2,1)} %get-tuple-element.50), channel_id=1, source_target_pairs={{0,32},{16,48},{32,0},{48,16},{64,96},{80,112},{96,64},{112,80},{1... | collective-permute-start | bytes 405512 | tf_op jit(solution)/shard_map/ppermute | solution.py:561
  18.0 15.2 %collective-permute-start.2 = (bf16[528,128]{1,0:T(8,128)(2,1)}, bf16[528,128]{1,0:T(8,128)(2,1)S(1)}, u32[]{:S(2)}, u32[]{:S(2)}) collective-permute-start(bf16[528,128]{1,0:T(8,128)(2,1)} %get-tuple-element.51), channel_id=1, source_target_pairs={{0,48},{16,0},{32,16},{48,32},{64,112},{80,64},{96,80},{112,96},{1... | collective-permute-start | bytes 405512 | tf_op jit(solution)/shard_map/ppermute | solution.py:561
  33.2 0.8 copy-start.5
  34.0 0.8 copy-start.6
  34.0 7.6 %copy-start = (bf16[528,128]{1,0:T(8,128)(2,1)S(1)}, bf16[528,128]{1,0:T(8,128)(2,1)}, u32[]{:S(2)}) copy-start(bf16[528,128]{1,0:T(8,128)(2,1)} %get-tuple-element.55.refs_0_) | copy-start | bytes 405508
  34.0 7.6 %copy-start.2 = (s32[2]{0:T(128)S(1)}, s32[2]{0:T(128)}, u32[]{:S(2)}) copy-start(s32[2]{0:T(128)} %pad_add_fusion.place_ref) | copy-start | bytes 28
  34.8 57.2 %all-to-all-start = ((bf16[16,528,128]{2,1,0:T(8,128)(2,1)}), bf16[16,528,128]{2,1,0:T(8,128)(2,1)}, u32[]{:S(2)}, u32[]{:S(2)}) async-start(bf16[16,528,128]{2,1,0:T(8,128)(2,1)} %pack_b.1), calls=%async_computation | async-start | bytes 4325376 | tf_op jit(solution)/shard_map/all_to_all | solution.py:583
  43.2 11.9 %collective-permute-start.5 = (bf16[4,208,128]{2,1,0:T(8,128)(2,1)}, bf16[4,208,128]{2,1,0:T(8,128)(2,1)S(1)}, u32[]{:S(2)}, u32[]{:S(2)}) collective-permute-start(bf16[4,208,128]{2,1,0:T(8,128)(2,1)} %get-tuple-element.60), channel_id=1, source_target_pairs={{0,64},{16,80},{32,96},{48,112},{64,128},{80,144},{96,160},{112,17... | collective-permute-start | bytes 638984 | tf_op jit(solution)/shard_map/ppermute | solution.py:561
  44.1 17.6 %collective-permute-start.6 = (bf16[4,208,128]{2,1,0:T(8,128)(2,1)}, bf16[4,208,128]{2,1,0:T(8,128)(2,1)S(1)}, u32[]{:S(2)}, u32[]{:S(2)}) collective-permute-start(bf16[4,208,128]{2,1,0:T(8,128)(2,1)} %get-tuple-element.61), channel_id=1, source_target_pairs={{0,128},{16,144},{32,160},{48,176},{64,192},{80,208},{96,224},{112... | collective-permute-start | bytes 638984 | tf_op jit(solution)/shard_map/ppermute | solution.py:561
  44.7 19.5 %collective-permute-start.7 = (bf16[4,208,128]{2,1,0:T(8,128)(2,1)}, bf16[4,208,128]{2,1,0:T(8,128)(2,1)S(1)}, u32[]{:S(2)}, u32[]{:S(2)}) collective-permute-start(bf16[4,208,128]{2,1,0:T(8,128)(2,1)} %get-tuple-element.62), channel_id=1, source_target_pairs={{0,192},{16,208},{32,224},{48,240},{64,0},{80,16},{96,32},{112,48}... | collective-permute-start | bytes 638984 | tf_op jit(solution)/shard_map/ppermute | solution.py:561
  64.1 35.9 %collective-permute-start.14 = (bf16[2,64,2560]{2,1,0:T(8,128)(2,1)}, bf16[2,64,2560]{2,1,0:T(8,128)(2,1)S(1)}, u32[]{:S(2)}, u32[]{:S(2)}) collective-permute-start(bf16[2,64,2560]{2,1,0:T(8,128)(2,1)} %get-tuple-element.84), channel_id=1, source_target_pairs={{0,1},{1,2},{2,3},{3,4},{4,5},{5,6},{6,7},{7,8},{8,9},{9,10},{10,1... | collective-permute-start | bytes 1966088 | tf_op jit(solution)/shard_map/ppermute | solution.py:590
  66.8 33.3 %collective-permute-start.15 = (bf16[2,64,2560]{2,1,0:T(8,128)(2,1)}, bf16[2,64,2560]{2,1,0:T(8,128)(2,1)}, u32[]{:S(2)}, u32[]{:S(2)}) collective-permute-start(bf16[2,64,2560]{2,1,0:T(8,128)(2,1)} %get-tuple-element.85), channel_id=1, source_target_pairs={{1,0},{2,1},{3,2},{4,3},{5,4},{6,5},{7,6},{8,7},{9,8},{10,9},{11,1... | collective-permute-start | bytes 1966088 | tf_op jit(solution)/shard_map/ppermute | solution.py:589
  72.2 12.4 %collective-permute-start.8 = (bf16[4,160,128]{2,1,0:T(8,128)(2,1)S(1)}, bf16[4,160,128]{2,1,0:T(8,128)(2,1)S(1)}, u32[]{:S(2)}, u32[]{:S(2)}) collective-permute-start(bf16[4,160,128]{2,1,0:T(8,128)(2,1)S(1)} %get-tuple-element.72), channel_id=1, source_target_pairs={{0,192},{16,208},{32,224},{48,240},{64,0},{80,16},{96,32},{112,48}... | collective-permute-start | bytes 491528 | tf_op jit(solution)/shard_map/ppermute | solution.py:561
  72.3 13.2 %collective-permute-start.9 = (bf16[4,160,128]{2,1,0:T(8,128)(2,1)S(1)}, bf16[4,160,128]{2,1,0:T(8,128)(2,1)S(1)}, u32[]{:S(2)}, u32[]{:S(2)}) collective-permute-start(bf16[4,160,128]{2,1,0:T(8,128)(2,1)S(1)} %get-tuple-element.73), channel_id=1, source_target_pairs={{0,128},{16,144},{32,160},{48,176},{64,192},{80,208},{96,224},{112... | collective-permute-start | bytes 491528 | tf_op jit(solution)/shard_map/ppermute | solution.py:561
  74.4 16.3 %collective-permute-start.10 = (bf16[4,160,128]{2,1,0:T(8,128)(2,1)S(1)}, bf16[4,160,128]{2,1,0:T(8,128)(2,1)S(1)}, u32[]{:S(2)}, u32[]{:S(2)}) collective-permute-start(bf16[4,160,128]{2,1,0:T(8,128)(2,1)S(1)} %get-tuple-element.74), channel_id=1, source_target_pairs={{0,64},{16,80},{32,96},{48,112},{64,128},{80,144},{96,160},{112,17... | collective-permute-start | bytes 491528 | tf_op jit(solution)/shard_map/ppermute | solution.py:561
  91.4 0.6 copy-start.1
  100.0 55.6 %copy-start.4 = (bf16[2,64,2560]{2,1,0:T(8,128)(2,1)}, bf16[2,64,2560]{2,1,0:T(8,128)(2,1)S(1)}, u32[]{:S(2)}) copy-start(bf16[2,64,2560]{2,1,0:T(8,128)(2,1)S(1)} %collective-permute-done.14.left_in) | copy-start | bytes 1966084
  100.1 55.6 %all-to-all-start.1 = ((bf16[16,384,128]{2,1,0:T(8,128)(2,1)}), bf16[16,384,128]{2,1,0:T(8,128)(2,1)S(1)}, u32[]{:S(2)}, u32[]{:S(2)}) async-start(bf16[16,384,128]{2,1,0:T(8,128)(2,1)} %head.1), calls=%async_computation.1 | async-start | bytes 3145728 | tf_op jit(solution)/shard_map/all_to_all | solution.py:600
  108.9 44.5 %collective-permute-start.11 = (bf16[384,128]{1,0:T(8,128)(2,1)S(1)}, bf16[384,128]{1,0:T(8,128)(2,1)S(1)}, u32[]{:S(2)}, u32[]{:S(2)}) collective-permute-start(bf16[384,128]{1,0:T(8,128)(2,1)S(1)} %get-tuple-element.80), channel_id=1, source_target_pairs={{0,48},{16,0},{32,16},{48,32},{64,112},{80,64},{96,80},{112,96},{1... | collective-permute-start | bytes 294920 | tf_op jit(solution)/shard_map/ppermute | solution.py:561
  112.2 41.2 %collective-permute-start.12 = (bf16[384,128]{1,0:T(8,128)(2,1)S(1)}, bf16[384,128]{1,0:T(8,128)(2,1)S(1)}, u32[]{:S(2)}, u32[]{:S(2)}) collective-permute-start(bf16[384,128]{1,0:T(8,128)(2,1)S(1)} %get-tuple-element.81), channel_id=1, source_target_pairs={{0,32},{16,48},{32,0},{48,16},{64,96},{80,112},{96,64},{112,80},{1... | collective-permute-start | bytes 294920 | tf_op jit(solution)/shard_map/ppermute | solution.py:561
  114.3 41.4 %collective-permute-start.13 = (bf16[384,128]{1,0:T(8,128)(2,1)S(1)}, bf16[384,128]{1,0:T(8,128)(2,1)S(1)}, u32[]{:S(2)}, u32[]{:S(2)}) collective-permute-start(bf16[384,128]{1,0:T(8,128)(2,1)S(1)} %get-tuple-element.82), channel_id=1, source_target_pairs={{0,16},{16,32},{32,48},{48,0},{64,80},{80,96},{96,112},{112,64},{1... | collective-permute-start | bytes 294920 | tf_op jit(solution)/shard_map/ppermute | solution.py:561
  153.4 2.3 %copy-start.7 = (bf16[384,128]{1,0:T(8,128)(2,1)}, bf16[384,128]{1,0:T(8,128)(2,1)S(1)}, u32[]{:S(2)}) copy-start(bf16[384,128]{1,0:T(8,128)(2,1)S(1)} %collective-permute-done.11.z1_hbm) | copy-start | bytes 294916
  153.4 2.3 %copy-start.8 = (bf16[384,128]{1,0:T(8,128)(2,1)}, bf16[384,128]{1,0:T(8,128)(2,1)S(1)}, u32[]{:S(2)}) copy-start(bf16[384,128]{1,0:T(8,128)(2,1)S(1)} %collective-permute-done.12.z2_hbm) | copy-start | bytes 294916
  155.6 0.6 copy-start.9
  155.6 1.2 copy-start.3

commit v3 on v2

--- a/solution.py
+++ b/solution.py
@@ -114,7 +114,7 @@
 
 
 def pack_a_kernel(
-    place_ref, frames_ref, blocks_ref, lse_ref, q_hbm, k_hbm, v_hbm, o_hbm, g_hbm,
+    group_ref, frames_ref, blocks_ref, lse_ref, q_hbm, k_hbm, v_hbm, o_hbm, g_hbm,
     z0_hbm, z1_hbm, z2_hbm, z3_hbm, low_hbm, high_hbm,
     q_all, k_all, v_all, o_all, g_all, send_ref, edge_ref, sems,
 ):
@@ -125,7 +125,7 @@
     for i, source in enumerate((k_hbm, v_hbm)):
         copies.start("edge", source.at[0:TILE, :], edge_ref.at[0, i])
         copies.start("edge", source.at[POS - TILE : POS, :], edge_ref.at[1, i])
-    masks = pair_masks(place_ref[0] * SIDE + place_ref[1], frames_ref, blocks_ref)
+    masks = pair_masks(group_ref[0], frames_ref, blocks_ref)
     copies.wait("in")
     rows = deltas([g_all[:, cols(j)] for j in range(SIDE)], [o_all[:, cols(j)] for j in range(SIDE)])
     for j in range(SIDE):
@@ -135,7 +135,7 @@
         send_ref[j, BG : BG + POS, :] = g_all[:, cols(j)]
         send_ref[j, BS:ROWS_B, :] = stat_rows(lse_ref[GROUP + j], rows[j], masks).astype(BF)
     for dz, out in enumerate((z0_hbm, z1_hbm, z2_hbm, z3_hbm)):
-        copies.start("out", send_ref.at[lax.rem(place_ref[1] + dz, SIDE)], out)
+        copies.start("out", send_ref.at[lax.rem(group_ref[0] + dz, SIDE)], out)
     copies.wait("edge")
     copies.start("out", edge_ref.at[0], low_hbm)
     copies.start("out", edge_ref.at[1], high_hbm)
@@ -143,7 +143,7 @@
 
 
 def pack_b_kernel(
-    place_ref, frames_ref, blocks_ref, lse_ref, q_hbm, k_hbm, v_hbm, o_hbm, g_hbm, send_hbm,
+    group_ref, frames_ref, blocks_ref, lse_ref, q_hbm, k_hbm, v_hbm, o_hbm, g_hbm, send_hbm,
     q_all, k_all, v_all, o_all, g_all, send_ref, sems,
 ):
     copies = Copies(sems)
@@ -152,7 +152,7 @@
         at = slice(block * WIDE, block * WIDE + WIDE)
         for source, target in pairs:
             copies.start(block, source.at[:, at], target.at[:, at])
-    masks = pair_masks(place_ref[0] * SIDE + place_ref[1], frames_ref, blocks_ref)
+    masks = pair_masks(group_ref[0], frames_ref, blocks_ref)
     for block in range(SIDE):
         copies.wait(block)
         heads = [block * SIDE + j for j in range(SIDE)]
@@ -168,14 +168,14 @@
     copies.wait_all()
 
 
-def split_kernel(place_ref, *refs):
+def split_kernel(group_ref, *refs):
     ins, outs = refs[:SIDE], refs[SIDE:]
     lane = lax.broadcasted_iota(jnp.int32, (16, HEAD), 1)
     sub = lax.broadcasted_iota(jnp.int32, (16, HEAD), 0)
     for dz, got in enumerate(ins):
         stats = got[BS:ROWS_B, :].astype(F32)
         for dy, out in enumerate(outs):
-            y = lax.rem(place_ref[0] + dy, SIDE)
+            y = lax.rem(group_ref[0] // SIDE + dy, SIDE)
             tile = pl.multiple_of((y // 2) * TILE, TILE)
             half = pl.multiple_of(y * HALF, HALF)
             out[dz, AK : AK + TILE, :] = got[pl.ds(BK + tile, TILE), :]
@@ -269,10 +269,10 @@
     return jnp.concatenate(rows, 0)
 
 
-def quarter_kernel(place_ref, *refs):
+def quarter_kernel(group_ref, *refs):
     ins, outs = refs[:SIDE], refs[SIDE : 2 * SIDE]
     q_ref, g_ref, kx_ref, kt_ref, dk_ref, dv_ref, row_ref = refs[2 * SIDE :]
-    y, z = place_ref[0], place_ref[1]
+    y, z = group_ref[0] // SIDE, lax.rem(group_ref[0], SIDE)
     stats = jnp.concatenate([got[:, AS:ROWS_A, :] for got in ins], 0).astype(F32)
     rows = []
     for s in range(2):
@@ -315,11 +315,11 @@
         out[:, RQ : RQ + HALF, :] = q_ref[SIDE * i : SIDE * i + SIDE]
 
 
-def merge_kernel(place_ref, *refs):
+def merge_kernel(group_ref, *refs):
     ins, outs, sum_ref = refs[:SIDE], refs[SIDE : 2 * SIDE], refs[2 * SIDE]
     sum_ref[...] = jnp.zeros_like(sum_ref)
     for dy, got in enumerate(ins):
-        y = lax.rem(place_ref[0] + dy, SIDE)
+        y = lax.rem(group_ref[0] // SIDE + dy, SIDE)
         tile = pl.multiple_of((y // 2) * TILE, TILE)
         half = pl.multiple_of(y * HALF, HALF)
         for dz, out in enumerate(outs):
@@ -383,11 +383,19 @@
     copies.wait_all()
 
 
+def settle_kernel(sums_ref, left_ref, right_ref, out_ref):
+    out_ref[0] = sums_ref[0].astype(BF)
+    for i in range(2):
+        edges = jnp.concatenate([left_ref[i], right_ref[i]], 0).astype(F32)
+        out_ref[1 + i] = (sums_ref[1 + i] + edges).astype(BF)
+
+
 def join_kernel(
-    place_ref, z0_hbm, z1_hbm, z2_hbm, z3_hbm, b_hbm, sums_in, left_in, right_in, dq_out, dk_out, dv_out,
-    a_ref, b_ref, sums_ref, left_ref, right_ref, low_ref, sems,
+    group_ref, z0_hbm, z1_hbm, z2_hbm, z3_hbm, b_hbm, base_in, dq_out, dk_out, dv_out,
+    a_ref, b_ref, base_ref, low_ref, sems,
 ):
     copies = Copies(sems)
+    z = lax.rem(group_ref[0], SIDE)
     sets = ((dq_out, BQ), (dk_out, BK), (dv_out, BV))
     order = [SIDE] + list(range(SIDE))
     for block in order:
@@ -398,9 +406,7 @@
         else:
             four = slice(SIDE * block, SIDE * block + SIDE)
             copies.start(block, b_hbm.at[four], b_ref.at[four])
-        copies.start(block, sums_in.at[:, :, at], sums_ref.at[:, :, at])
-        copies.start(block, left_in.at[:, :, at], left_ref.at[:, :, at])
-        copies.start(block, right_in.at[:, :, at], right_ref.at[:, :, at])
+        copies.start(block, base_in.at[:, :, at], base_ref.at[:, :, at])
     for block in order:
         copies.wait(block)
         at = slice(block * WIDE, block * WIDE + WIDE)
@@ -408,14 +414,11 @@
             for j in range(SIDE):
                 h = SIDE * block + j
                 if block < SIDE:
-                    more = b_ref[h, row : row + POS, :].astype(F32)
+                    more = b_ref[h, row : row + POS, :]
                 else:
-                    dz = lax.rem(j + SIDE - place_ref[1], SIDE)
-                    more = a_ref[dz, row : row + POS, :].astype(F32)
-                if which:
-                    edges = [left_ref[which - 1, :, cols(h)], right_ref[which - 1, :, cols(h)]]
-                    more = more + jnp.concatenate(edges, 0).astype(F32)
-                low_ref[which, :, cols(h)] = (sums_ref[which, :, cols(h)] + more).astype(BF)
+                    more = a_ref[lax.rem(j + SIDE - z, SIDE), row : row + POS, :]
+                total = base_ref[which, :, cols(h)].astype(F32) + more.astype(F32)
+                low_ref[which, :, cols(h)] = total.astype(BF)
             copies.start("out", low_ref.at[which, :, at], out.at[:, at])
     copies.wait_all()
 
@@ -516,20 +519,35 @@
     )(arrived)
 
 
-def join_call(place, shares, b, sums, left, right):
-    out = shape(*sums.shape[1:])
+def settle_call(sums, left, right):
+    edge = pl.BlockSpec((2, TILE, WIDE), lambda i: (0, 0, i))
+    rows = pl.BlockSpec((3, POS, WIDE), lambda i: (0, 0, i))
+    return pl.pallas_call(
+        settle_kernel,
+        grid=(sums.shape[2] // WIDE,),
+        out_shape=shape(*sums.shape),
+        in_specs=[rows, edge, edge],
+        out_specs=rows,
+        compiler_params=room(60),
+        cost_estimate=cost(4),
+        name="settle",
+    )(sums, left, right)
+
+
+def join_call(group, shares, b, base):
+    out = shape(*base.shape[1:])
     return pl.pallas_call(
         join_kernel,
         out_shape=(out,) * 3,
-        in_specs=[SMEM] + [ANY] * (SIDE + 4),
+        in_specs=[SMEM] + [ANY] * (SIDE + 2),
         out_specs=[ANY] * 3,
         scratch_shapes=[pltpu.VMEM((SIDE, BACK_B, HEAD), BF)]
-        + [pltpu.VMEM(x.shape, x.dtype) for x in (b, sums, left, right)]
-        + [pltpu.VMEM(sums.shape, BF), pltpu.SemaphoreType.DMA((38,))],
+        + [pltpu.VMEM(x.shape, x.dtype) for x in (b, base, base)]
+        + [pltpu.SemaphoreType.DMA((28,))],
         compiler_params=room(60),
         cost_estimate=cost(4),
         name="join",
-    )(place, *shares, b, sums, left, right)
+    )(group, *shares, b, base)
 
 
 def own_call(sides, q, k, v, o, g, before, after, lse):
@@ -571,8 +589,8 @@
     sides = jnp.stack([inner_at, jnp.full((), inner, jnp.int32)])
     up = [(i, i + 1) for i in range(inner - 1)]
     down = [(i + 1, i) for i in range(inner - 1)]
-    place = jnp.stack([group_at // SIDE, group_at % SIDE])
-    facts = (place, far_frames[0], far_blocks[0], lse)
+    group = group_at.reshape(1)
+    facts = (group, far_frames[0], far_blocks[0], lse)
 
     *sends_z, first_rows, last_rows = pack_a_call(*facts, *rows)
     got_z = around((0, 1), sends_z)
@@ -582,23 +600,25 @@
     send_b, got_z, before, after = lax.optimization_barrier((send_b, got_z, before, after))
     got_b = lax.all_to_all(send_b, "group", 0, 0, tiled=True)
 
-    sends_y = four_call(split_kernel, shape(SIDE, ROWS_A, HEAD), [], 3, "split", place, got_z)
+    sends_y = four_call(split_kernel, shape(SIDE, ROWS_A, HEAD), [], 3, "split", group, got_z)
     got_y = around((1, 0), sends_y)
     sums, to_low, to_high = own_call(sides, *rows, before, after, lse)
     got_y, to_low, to_high = lax.optimization_barrier((got_y, to_low, to_high))
+    scratch = [pltpu.VMEM((GROUP, HALF, HEAD), BF)] * 2 + SCRATCH
+    back_y = four_call(quarter_kernel, shape(SIDE, ROWS_R, HEAD), scratch, 3, "quarter", group, got_y)
+    back_y, to_low, to_high = lax.optimization_barrier((back_y, to_low, to_high))
+    home_y = around((-1, 0), back_y)
     from_right = lax.ppermute(to_low, "inner", down)
     from_left = lax.ppermute(to_high, "inner", up)
-    scratch = [pltpu.VMEM((GROUP, HALF, HEAD), BF)] * 2 + SCRATCH
-    back_y = four_call(quarter_kernel, shape(SIDE, ROWS_R, HEAD), scratch, 3, "quarter", place, got_y)
-    home_y = around((-1, 0), back_y)
     scratch = [pltpu.VMEM((SIDE, 2, POS, HEAD), F32)]
-    back_z = four_call(merge_kernel, shape(BACK_B, HEAD), scratch, 3, "merge", place, home_y)
+    back_z = four_call(merge_kernel, shape(BACK_B, HEAD), scratch, 3, "merge", group, home_y)
 
     got_b, back_z = lax.optimization_barrier((got_b, back_z))
     home_z = around((0, -1), back_z)
     back_b, from_left, from_right = lax.optimization_barrier((head_call(got_b), from_left, from_right))
     home_b = lax.all_to_all(back_b, "group", 0, 0, tiled=True)
-    return tuple(a[None] for a in join_call(place, home_z, home_b, sums, from_left, from_right))
+    base = settle_call(sums, from_left, from_right)
+    return tuple(a[None] for a in join_call(group, home_z, home_b, base))
 
 
 def solution(mesh):

time: 165 us -> 163 us (0.988)
  the two profiles are of different devices: /device:TPU:23 before, /device:TPU:3 now
where the time goes in v3:
time: 163 us; the launch traced here: 162 us
  waiting for transfers between devices  66.5 us (41%)
  starting transfers between devices  53.6 us (33%)
  Pallas kernels  36 us (22%)
  local copies, waits for them, and re-layouts  4.12 us (3%)
    ppermute x12, waiting for transfers between devices, around(): lax.ppermute(shares[d], 'group', [(i, partner(i, step)) for i in range(GR...  64.8 us
    ppermute x12, starting transfers between devices, around(): lax.ppermute(shares[d], 'group', [(i, partner(i, step)) for i in range(GR...  24.6 us
    all_to_all x1, starting transfers between devices, body(): home_b = lax.all_to_all(back_b, 'group', 0, 0, tiled=True)  9.29 us
    pallas_call x1, Pallas kernels, own_call(): pl.pallas_call(own_kernel, grid=(feature // WIDE,), out_shape=(shape(3, P...  8.98 us
    pallas_call x1, Pallas kernels, head_call(): pl.pallas_call(head_kernel, out_shape=shape(GROUP, BACK_B, HEAD), in_spec...  8.04 us
    all_to_all x1, starting transfers between devices, body(): got_b = lax.all_to_all(send_b, 'group', 0, 0, tiled=True)  7.51 us
    pallas_call x1, Pallas kernels, settle_call(): pl.pallas_call(settle_kernel, grid=(sums.shape[2] // WIDE,), out_shape=sh...  5.16 us
    ppermute x1, starting transfers between devices, body(): from_left = lax.ppermute(to_high, 'inner', up)  4.48 us
  transfers between devices with their start and end apart: 18, of which 9 were waited for; matrix products, arithmetic and copies ran while one was open for 0% of the time, Pallas kernels for 18%

profile of v3, /device:TPU:3, one launch (start us, length us, event | category | flops | bytes accessed | tf_op | source)
XLA Modules:
  0.0 161.9 jit_solution(13349267548029526639)
XLA Ops:
  0.6 3.5 %pack_a.1 = (bf16[528,128]{1,0:T(8,128)(2,1)}, bf16[528,128]{1,0:T(8,128)(2,1)}, bf16[528,128]{1,0:T(8,128)(2,1)}, bf16[528,128]{1,0:T(8,128)(2,1)}, bf16[2,64,2...) custom-call(s32[1]{0:T(128)} %bitcast.group_ref, s32[2,11]{1,0:T(2,128)} %bitcast.31, s32[2,11]{1,0:T(2,128)} %bitcast.33, ...), custom_call_target="tpu_custom_call" | custom-call | bytes 9000000 | tf_op jit(solution)/shard_map/pack_a/pallas_call | solution.py:459
  4.1 3.7 %collective-permute-start.3 = (bf16[2,64,2560]{2,1,0:T(8,128)(2,1)}, bf16[2,64,2560]{2,1,0:T(8,128)(2,1)S(1)}, u32[]{:S(2)}, u32[]{:S(2)}) collective-permute-start(bf16[2,64,2560]{2,1,0:T(8,128)(2,1)} %get-tuple-element.58), channel_id=1, source_target_pairs={{0,1},{1,2},{2,3},{3,4},{4,5},{5,6},{6,7},{7,8},{8,9},{9,10},{10,1... | collective-permute-start | bytes 1966088 | tf_op jit(solution)/shard_map/ppermute | solution.py:597
  7.8 1.9 %collective-permute-start.4 = (bf16[2,64,2560]{2,1,0:T(8,128)(2,1)}, bf16[2,64,2560]{2,1,0:T(8,128)(2,1)S(1)}, u32[]{:S(2)}, u32[]{:S(2)}) collective-permute-start(bf16[2,64,2560]{2,1,0:T(8,128)(2,1)} %get-tuple-element.59), channel_id=1, source_target_pairs={{1,0},{2,1},{3,2},{4,3},{5,4},{6,5},{7,6},{8,7},{9,8},{10,9},{11,1... | collective-permute-start | bytes 1966088 | tf_op jit(solution)/shard_map/ppermute | solution.py:598
  9.7 3.1 %collective-permute-start = (bf16[528,128]{1,0:T(8,128)(2,1)}, bf16[528,128]{1,0:T(8,128)(2,1)S(1)}, u32[]{:S(2)}, u32[]{:S(2)}) collective-permute-start(bf16[528,128]{1,0:T(8,128)(2,1)} %get-tuple-element.55), channel_id=1, source_target_pairs={{0,16},{16,32},{32,48},{48,0},{64,80},{80,96},{96,112},{112,64},{1... | collective-permute-start | bytes 405512 | tf_op jit(solution)/shard_map/ppermute | solution.py:579
  12.8 5.1 %collective-permute-start.1 = (bf16[528,128]{1,0:T(8,128)(2,1)}, bf16[528,128]{1,0:T(8,128)(2,1)S(1)}, u32[]{:S(2)}, u32[]{:S(2)}) collective-permute-start(bf16[528,128]{1,0:T(8,128)(2,1)} %get-tuple-element.56), channel_id=1, source_target_pairs={{0,32},{16,48},{32,0},{48,16},{64,96},{80,112},{96,64},{112,80},{1... | collective-permute-start | bytes 405512 | tf_op jit(solution)/shard_map/ppermute | solution.py:579
  17.9 2.4 %collective-permute-start.2 = (bf16[528,128]{1,0:T(8,128)(2,1)}, bf16[528,128]{1,0:T(8,128)(2,1)S(1)}, u32[]{:S(2)}, u32[]{:S(2)}) collective-permute-start(bf16[528,128]{1,0:T(8,128)(2,1)} %get-tuple-element.57), channel_id=1, source_target_pairs={{0,48},{16,0},{32,16},{48,32},{64,112},{80,64},{96,80},{112,96},{1... | collective-permute-start | bytes 405512 | tf_op jit(solution)/shard_map/ppermute | solution.py:579
  20.3 3.8 %pack_b.1 = bf16[16,528,128]{2,1,0:T(8,128)(2,1)} custom-call(s32[1]{0:T(128)} %bitcast.group_ref, s32[2,11]{1,0:T(2,128)} %bitcast.32, s32[2,11]{1,0:T(2,128)} %bitcast.34, f32[20,1,128]{2,1,0:T(1,128)} %bitcast.29, bf16[128,2560]{1,0:T(8,128)(2,1)} %bitcast.14, bf16[128,2560]{1,0:T(8,128)(2,1)} %bitcast.17, bf16[128,2560]{1,0:T(8,128)(2,1)} %bitcast.20, ...), custom_call_target="tpu_custom_call" | custom-call | bytes 12000000 | tf_op jit(solution)/shard_map/pack_b/pallas_call | solution.py:478
  24.1 0.0 collective-permute-done.refs_1_
  24.1 2.9 %collective-permute-done.1.refs_2_ = bf16[528,128]{1,0:T(8,128)(2,1)S(1)} collective-permute-done((bf16[528,128]{1,0:T(8,128)(2,1)}, bf16[528,128]{1,0:T(8,128)(2,1)S(1)}, u32[]{:S(2)}, u32[]{:S(2)}) %collective-permute-start.1) | collective-permute-done | bytes 135200 | tf_op jit(solution)/shard_map/ppermute | solution.py:579
  27.0 4.4 %collective-permute-done.2.refs_3_ = bf16[528,128]{1,0:T(8,128)(2,1)S(1)} collective-permute-done((bf16[528,128]{1,0:T(8,128)(2,1)}, bf16[528,128]{1,0:T(8,128)(2,1)S(1)}, u32[]{:S(2)}, u32[]{:S(2)}) %collective-permute-start.2) | collective-permute-done | bytes 135200 | tf_op jit(solution)/shard_map/ppermute | solution.py:579
  31.4 0.0 collective-permute-done.3.before_ref
  31.4 0.0 collective-permute-done.4.after_ref
  31.4 0.8 copy-done.3
  32.3 0.8 copy-done.4
  33.1 7.5 %all-to-all-start = ((bf16[16,528,128]{2,1,0:T(8,128)(2,1)}), bf16[16,528,128]{2,1,0:T(8,128)(2,1)}, u32[]{:S(2)}, u32[]{:S(2)}) async-start(bf16[16,528,128]{2,1,0:T(8,128)(2,1)} %pack_b.1), calls=%async_computation | async-start | bytes 4325376 | tf_op jit(solution)/shard_map/all_to_all | solution.py:601
  40.6 1.0 split.1
  41.7 1.3 collective-permute-start.5
  43.0 2.4 %collective-permute-start.6 = (bf16[4,208,128]{2,1,0:T(8,128)(2,1)}, bf16[4,208,128]{2,1,0:T(8,128)(2,1)S(1)}, u32[]{:S(2)}, u32[]{:S(2)}) collective-permute-start(bf16[4,208,128]{2,1,0:T(8,128)(2,1)} %get-tuple-element.67), channel_id=1, source_target_pairs={{0,128},{16,144},{32,160},{48,176},{64,192},{80,208},{96,224},{112... | collective-permute-start | bytes 638984 | tf_op jit(solution)/shard_map/ppermute | solution.py:579
  45.4 1.2 collective-permute-start.7
  46.6 0.6 pad_add_fusion.side_ref
  47.2 9.0 %own.1 = (f32[3,128,2560]{2,1,0:T(8,128)}, bf16[2,64,2560]{2,1,0:T(8,128)(2,1)}, bf16[2,64,2560]{2,1,0:T(8,128)(2,1)}) custom-call(s32[2]{0:T(128)} %pad_add_fusion.side_ref, bf16[128,2560]{1,0:T(8,128)(2,1)} %bitcast.15, bf16[128,2560]{1,0:T(8,128)(2,1)} %bitcast.18, bf16[128,2560]{1,0:T(8,128)(2,1)} %bitcast.21, bf16[128,2560]{1,0:T(8,128)(2,1)} %bitcast.24, ...), custom_call_target="tpu_custom_call" | custom-call | bytes 27000000 | tf_op jit(solution)/shard_map/own/pallas_call | solution.py:559
  56.1 0.0 collective-permute-done.5.refs_1_
  56.2 4.1 %collective-permute-done.6.refs_2_ = bf16[4,208,128]{2,1,0:T(8,128)(2,1)S(1)} collective-permute-done((bf16[4,208,128]{2,1,0:T(8,128)(2,1)}, bf16[4,208,128]{2,1,0:T(8,128)(2,1)S(1)}, u32[]{:S(2)}, u32[]{:S(2)}) %collective-permute-start.6) | collective-permute-done | bytes 213024 | tf_op jit(solution)/shard_map/ppermute | solution.py:579
  60.2 2.1 %quarter.1 = (bf16[4,160,128]{2,1,0:T(8,128)(2,1)S(1)}, bf16[4,160,128]{2,1,0:T(8,128)(2,1)S(1)}, bf16[4,160,128]{2,1,0:T(8,128)(2,1)S(1)}, bf16[4,160,128]{2,1,0:T(8,128)(2,1)S(1)}) custom-call(s32[1]{0:T(128)} %bitcast.group_ref, bf16[4,208,128]{2,1,0:T(8,128)(2,1)S(1)} %get-tuple-element.73.refs_0_, ...), custom_call_target="tpu_custom_call" | custom-call | bytes 9000000 | tf_op jit(solution)/shard_map/quarter/pallas_call | solution.py:492
  62.3 4.5 %collective-permute-start.14 = (bf16[2,64,2560]{2,1,0:T(8,128)(2,1)}, bf16[2,64,2560]{2,1,0:T(8,128)(2,1)S(1)}, u32[]{:S(2)}, u32[]{:S(2)}) collective-permute-start(bf16[2,64,2560]{2,1,0:T(8,128)(2,1)} %get-tuple-element.96), channel_id=1, source_target_pairs={{0,1},{1,2},{2,3},{3,4},{4,5},{5,6},{6,7},{7,8},{8,9},{9,10},{10,1... | collective-permute-start | bytes 1966088 | tf_op jit(solution)/shard_map/ppermute | solution.py:612
  66.8 2.1 %collective-permute-start.15 = (bf16[2,64,2560]{2,1,0:T(8,128)(2,1)}, bf16[2,64,2560]{2,1,0:T(8,128)(2,1)S(1)}, u32[]{:S(2)}, u32[]{:S(2)}) collective-permute-start(bf16[2,64,2560]{2,1,0:T(8,128)(2,1)} %get-tuple-element.97), channel_id=1, source_target_pairs={{1,0},{2,1},{3,2},{4,3},{5,4},{6,5},{7,6},{8,7},{9,8},{10,9},{11,1... | collective-permute-start | bytes 1966088 | tf_op jit(solution)/shard_map/ppermute | solution.py:611
  69.0 0.1 collective-permute-start.8
  69.1 0.6 collective-permute-start.9
  69.6 0.9 collective-permute-start.10
  70.5 3.2 %collective-permute-done.8.refs_1_ = bf16[4,160,128]{2,1,0:T(8,128)(2,1)S(1)} collective-permute-done((bf16[4,160,128]{2,1,0:T(8,128)(2,1)S(1)}, bf16[4,160,128]{2,1,0:T(8,128)(2,1)S(1)}, u32[]{:S(2)}, u32[]{:S(2)}) %collective-permute-start.8) | collective-permute-done | bytes 163872 | tf_op jit(solution)/shard_map/ppermute | solution.py:579
  73.7 9.8 %collective-permute-done.9.refs_2_ = bf16[4,160,128]{2,1,0:T(8,128)(2,1)S(1)} collective-permute-done((bf16[4,160,128]{2,1,0:T(8,128)(2,1)S(1)}, bf16[4,160,128]{2,1,0:T(8,128)(2,1)S(1)}, u32[]{:S(2)}, u32[]{:S(2)}) %collective-permute-start.9) | collective-permute-done | bytes 163872 | tf_op jit(solution)/shard_map/ppermute | solution.py:579
  83.5 6.4 %collective-permute-done.10.refs_3_ = bf16[4,160,128]{2,1,0:T(8,128)(2,1)S(1)} collective-permute-done((bf16[4,160,128]{2,1,0:T(8,128)(2,1)S(1)}, bf16[4,160,128]{2,1,0:T(8,128)(2,1)S(1)}, u32[]{:S(2)}, u32[]{:S(2)}) %collective-permute-start.10) | collective-permute-done | bytes 163872 | tf_op jit(solution)/shard_map/ppermute | solution.py:579
  89.8 0.2 merge.1
  90.0 0.6 copy-done.1
  90.7 1.7 %all-to-all-done.in_hbm = bf16[16,528,128]{2,1,0:T(8,128)(2,1)} async-done(((bf16[16,528,128]{2,1,0:T(8,128)(2,1)}), bf16[16,528,128]{2,1,0:T(8,128)(2,1)}, u32[]{:S(2)}, u32[]{:S(2)}) %all-to-all-start) | async-done | bytes 2162720 | tf_op jit(solution)/shard_map/all_to_all | solution.py:601
  92.3 8.0 %head.1 = bf16[16,384,128]{2,1,0:T(8,128)(2,1)} custom-call(bf16[16,528,128]{2,1,0:T(8,128)(2,1)} %all-to-all-done.in_hbm), custom_call_target="tpu_custom_call" | custom-call | bytes 24000000 | tf_op jit(solution)/shard_map/head/pallas_call | solution.py:505
  100.4 0.0 copy-start.5
  100.4 0.0 copy-start.6
  100.4 9.3 %all-to-all-start.1 = ((bf16[16,384,128]{2,1,0:T(8,128)(2,1)}), bf16[16,384,128]{2,1,0:T(8,128)(2,1)S(1)}, u32[]{:S(2)}, u32[]{:S(2)}) async-start(bf16[16,384,128]{2,1,0:T(8,128)(2,1)} %head.1), calls=%async_computation.1 | async-start | bytes 3145728 | tf_op jit(solution)/shard_map/all_to_all | solution.py:619
  109.7 3.5 %collective-permute-start.11 = (bf16[384,128]{1,0:T(8,128)(2,1)S(1)}, bf16[384,128]{1,0:T(8,128)(2,1)S(1)}, u32[]{:S(2)}, u32[]{:S(2)}) collective-permute-start(bf16[384,128]{1,0:T(8,128)(2,1)S(1)} %get-tuple-element.92), channel_id=1, source_target_pairs={{0,48},{16,0},{32,16},{48,32},{64,112},{80,64},{96,80},{112,96},{1... | collective-permute-start | bytes 294920 | tf_op jit(solution)/shard_map/ppermute | solution.py:579
  113.2 2.1 %collective-permute-start.12 = (bf16[384,128]{1,0:T(8,128)(2,1)S(1)}, bf16[384,128]{1,0:T(8,128)(2,1)S(1)}, u32[]{:S(2)}, u32[]{:S(2)}) collective-permute-start(bf16[384,128]{1,0:T(8,128)(2,1)S(1)} %get-tuple-element.93), channel_id=1, source_target_pairs={{0,32},{16,48},{32,0},{48,16},{64,96},{80,112},{96,64},{112,80},{1... | collective-permute-start | bytes 294920 | tf_op jit(solution)/shard_map/ppermute | solution.py:579
  115.3 2.1 %collective-permute-start.13 = (bf16[384,128]{1,0:T(8,128)(2,1)S(1)}, bf16[384,128]{1,0:T(8,128)(2,1)S(1)}, u32[]{:S(2)}, u32[]{:S(2)}) collective-permute-start(bf16[384,128]{1,0:T(8,128)(2,1)S(1)} %get-tuple-element.94), channel_id=1, source_target_pairs={{0,16},{16,32},{32,48},{48,0},{64,80},{80,96},{96,112},{112,64},{1... | collective-permute-start | bytes 294920 | tf_op jit(solution)/shard_map/ppermute | solution.py:579
  117.4 5.2 %settle.1.base_in = bf16[3,128,2560]{2,1,0:T(8,128)(2,1)} custom-call(f32[3,128,2560]{2,1,0:T(8,128)} %get-tuple-element.99.sums_ref, bf16[2,64,2560]{2,1,0:T(8,128)(2,1)} %copy-done.5, bf16[2,64,2560]{2,1,0:T(8,128)(2,1)} %copy-done.6), custom_call_target="tpu_custom_call" | custom-call | bytes 12000000 | tf_op jit(solution)/shard_map/settle/pallas_call | solution.py:525
  122.5 31.9 %collective-permute-done.11.z1_hbm = bf16[384,128]{1,0:T(8,128)(2,1)S(1)} collective-permute-done((bf16[384,128]{1,0:T(8,128)(2,1)S(1)}, bf16[384,128]{1,0:T(8,128)(2,1)S(1)}, u32[]{:S(2)}, u32[]{:S(2)}) %collective-permute-start.11) | collective-permute-done | bytes 98336 | tf_op jit(solution)/shard_map/ppermute | solution.py:579
  154.4 2.3 %collective-permute-done.13.z3_hbm = bf16[384,128]{1,0:T(8,128)(2,1)S(1)} collective-permute-done((bf16[384,128]{1,0:T(8,128)(2,1)S(1)}, bf16[384,128]{1,0:T(8,128)(2,1)S(1)}, u32[]{:S(2)}, u32[]{:S(2)}) %collective-permute-start.13) | collective-permute-done | bytes 98336 | tf_op jit(solution)/shard_map/ppermute | solution.py:579
  156.7 0.6 copy-done.9
  157.3 1.2 copy-done.2
  158.5 3.2 %join.1 = (bf16[128,2560]{1,0:T(8,128)(2,1)}, bf16[128,2560]{1,0:T(8,128)(2,1)}, bf16[128,2560]{1,0:T(8,128)(2,1)}) custom-call(s32[1]{0:T(128)} %bitcast.group_ref, bf16[384,128]{1,0:T(8,128)(2,1)} %copy-done.1, bf16[384,128]{1,0:T(8,128)(2,1)} %copy-done.7, bf16[384,128]{1,0:T(8,128)(2,1)} %copy-done.8, bf16[384,128]{1,0:T(8,128)(2,1)} %copy-done.9, ...), custom_call_target="tpu_custom_call" | custom-call | bytes 12000000 | tf_op jit(solution)/shard_map/join/pallas_call | solution.py:539
  (18 shorter events, 0.0 us)
Async XLA Ops:
  4.1 27.3 %collective-permute-start.3 = (bf16[2,64,2560]{2,1,0:T(8,128)(2,1)}, bf16[2,64,2560]{2,1,0:T(8,128)(2,1)S(1)}, u32[]{:S(2)}, u32[]{:S(2)}) collective-permute-start(bf16[2,64,2560]{2,1,0:T(8,128)(2,1)} %get-tuple-element.58), channel_id=1, source_target_pairs={{0,1},{1,2},{2,3},{3,4},{4,5},{5,6},{6,7},{7,8},{8,9},{9,10},{10,1... | collective-permute-start | bytes 1966088 | tf_op jit(solution)/shard_map/ppermute | solution.py:597
  7.8 23.6 %collective-permute-start.4 = (bf16[2,64,2560]{2,1,0:T(8,128)(2,1)}, bf16[2,64,2560]{2,1,0:T(8,128)(2,1)S(1)}, u32[]{:S(2)}, u32[]{:S(2)}) collective-permute-start(bf16[2,64,2560]{2,1,0:T(8,128)(2,1)} %get-tuple-element.59), channel_id=1, source_target_pairs={{1,0},{2,1},{3,2},{4,3},{5,4},{6,5},{7,6},{8,7},{9,8},{10,9},{11,1... | collective-permute-start | bytes 1966088 | tf_op jit(solution)/shard_map/ppermute | solution.py:598
  9.7 14.4 %collective-permute-start = (bf16[528,128]{1,0:T(8,128)(2,1)}, bf16[528,128]{1,0:T(8,128)(2,1)S(1)}, u32[]{:S(2)}, u32[]{:S(2)}) collective-permute-start(bf16[528,128]{1,0:T(8,128)(2,1)} %get-tuple-element.55), channel_id=1, source_target_pairs={{0,16},{16,32},{32,48},{48,0},{64,80},{80,96},{96,112},{112,64},{1... | collective-permute-start | bytes 405512 | tf_op jit(solution)/shard_map/ppermute | solution.py:579
  12.8 14.2 %collective-permute-start.1 = (bf16[528,128]{1,0:T(8,128)(2,1)}, bf16[528,128]{1,0:T(8,128)(2,1)S(1)}, u32[]{:S(2)}, u32[]{:S(2)}) collective-permute-start(bf16[528,128]{1,0:T(8,128)(2,1)} %get-tuple-element.56), channel_id=1, source_target_pairs={{0,32},{16,48},{32,0},{48,16},{64,96},{80,112},{96,64},{112,80},{1... | collective-permute-start | bytes 405512 | tf_op jit(solution)/shard_map/ppermute | solution.py:579
  17.9 13.5 %collective-permute-start.2 = (bf16[528,128]{1,0:T(8,128)(2,1)}, bf16[528,128]{1,0:T(8,128)(2,1)S(1)}, u32[]{:S(2)}, u32[]{:S(2)}) collective-permute-start(bf16[528,128]{1,0:T(8,128)(2,1)} %get-tuple-element.57), channel_id=1, source_target_pairs={{0,48},{16,0},{32,16},{48,32},{64,112},{80,64},{96,80},{112,96},{1... | collective-permute-start | bytes 405512 | tf_op jit(solution)/shard_map/ppermute | solution.py:579
  31.4 0.8 copy-start.3
  32.2 0.8 copy-start.4
  32.3 8.4 %copy-start = (bf16[528,128]{1,0:T(8,128)(2,1)S(1)}, bf16[528,128]{1,0:T(8,128)(2,1)}, u32[]{:S(2)}) copy-start(bf16[528,128]{1,0:T(8,128)(2,1)} %get-tuple-element.61.refs_0_) | copy-start | bytes 405508
  33.1 59.2 %all-to-all-start = ((bf16[16,528,128]{2,1,0:T(8,128)(2,1)}), bf16[16,528,128]{2,1,0:T(8,128)(2,1)}, u32[]{:S(2)}, u32[]{:S(2)}) async-start(bf16[16,528,128]{2,1,0:T(8,128)(2,1)} %pack_b.1), calls=%async_computation | async-start | bytes 4325376 | tf_op jit(solution)/shard_map/all_to_all | solution.py:601
  41.7 14.5 %collective-permute-start.5 = (bf16[4,208,128]{2,1,0:T(8,128)(2,1)}, bf16[4,208,128]{2,1,0:T(8,128)(2,1)S(1)}, u32[]{:S(2)}, u32[]{:S(2)}) collective-permute-start(bf16[4,208,128]{2,1,0:T(8,128)(2,1)} %get-tuple-element.66), channel_id=1, source_target_pairs={{0,64},{16,80},{32,96},{48,112},{64,128},{80,144},{96,160},{112,17... | collective-permute-start | bytes 638984 | tf_op jit(solution)/shard_map/ppermute | solution.py:579
  43.0 17.2 %collective-permute-start.6 = (bf16[4,208,128]{2,1,0:T(8,128)(2,1)}, bf16[4,208,128]{2,1,0:T(8,128)(2,1)S(1)}, u32[]{:S(2)}, u32[]{:S(2)}) collective-permute-start(bf16[4,208,128]{2,1,0:T(8,128)(2,1)} %get-tuple-element.67), channel_id=1, source_target_pairs={{0,128},{16,144},{32,160},{48,176},{64,192},{80,208},{96,224},{112... | collective-permute-start | bytes 638984 | tf_op jit(solution)/shard_map/ppermute | solution.py:579
  45.4 14.8 %collective-permute-start.7 = (bf16[4,208,128]{2,1,0:T(8,128)(2,1)}, bf16[4,208,128]{2,1,0:T(8,128)(2,1)S(1)}, u32[]{:S(2)}, u32[]{:S(2)}) collective-permute-start(bf16[4,208,128]{2,1,0:T(8,128)(2,1)} %get-tuple-element.68), channel_id=1, source_target_pairs={{0,192},{16,208},{32,224},{48,240},{64,0},{80,16},{96,32},{112,48}... | collective-permute-start | bytes 638984 | tf_op jit(solution)/shard_map/ppermute | solution.py:579
  62.3 38.0 %collective-permute-start.14 = (bf16[2,64,2560]{2,1,0:T(8,128)(2,1)}, bf16[2,64,2560]{2,1,0:T(8,128)(2,1)S(1)}, u32[]{:S(2)}, u32[]{:S(2)}) collective-permute-start(bf16[2,64,2560]{2,1,0:T(8,128)(2,1)} %get-tuple-element.96), channel_id=1, source_target_pairs={{0,1},{1,2},{2,3},{3,4},{4,5},{5,6},{6,7},{7,8},{8,9},{9,10},{10,1... | collective-permute-start | bytes 1966088 | tf_op jit(solution)/shard_map/ppermute | solution.py:612
  66.8 33.6 %collective-permute-start.15 = (bf16[2,64,2560]{2,1,0:T(8,128)(2,1)}, bf16[2,64,2560]{2,1,0:T(8,128)(2,1)S(1)}, u32[]{:S(2)}, u32[]{:S(2)}) collective-permute-start(bf16[2,64,2560]{2,1,0:T(8,128)(2,1)} %get-tuple-element.97), channel_id=1, source_target_pairs={{1,0},{2,1},{3,2},{4,3},{5,4},{6,5},{7,6},{8,7},{9,8},{10,9},{11,1... | collective-permute-start | bytes 1966088 | tf_op jit(solution)/shard_map/ppermute | solution.py:611
  69.0 4.8 %collective-permute-start.8 = (bf16[4,160,128]{2,1,0:T(8,128)(2,1)S(1)}, bf16[4,160,128]{2,1,0:T(8,128)(2,1)S(1)}, u32[]{:S(2)}, u32[]{:S(2)}) collective-permute-start(bf16[4,160,128]{2,1,0:T(8,128)(2,1)S(1)} %get-tuple-element.84), channel_id=1, source_target_pairs={{0,192},{16,208},{32,224},{48,240},{64,0},{80,16},{96,32},{112,48}... | collective-permute-start | bytes 491528 | tf_op jit(solution)/shard_map/ppermute | solution.py:579
  69.1 14.4 %collective-permute-start.9 = (bf16[4,160,128]{2,1,0:T(8,128)(2,1)S(1)}, bf16[4,160,128]{2,1,0:T(8,128)(2,1)S(1)}, u32[]{:S(2)}, u32[]{:S(2)}) collective-permute-start(bf16[4,160,128]{2,1,0:T(8,128)(2,1)S(1)} %get-tuple-element.85), channel_id=1, source_target_pairs={{0,128},{16,144},{32,160},{48,176},{64,192},{80,208},{96,224},{112... | collective-permute-start | bytes 491528 | tf_op jit(solution)/shard_map/ppermute | solution.py:579
  69.6 20.2 %collective-permute-start.10 = (bf16[4,160,128]{2,1,0:T(8,128)(2,1)S(1)}, bf16[4,160,128]{2,1,0:T(8,128)(2,1)S(1)}, u32[]{:S(2)}, u32[]{:S(2)}) collective-permute-start(bf16[4,160,128]{2,1,0:T(8,128)(2,1)S(1)} %get-tuple-element.86), channel_id=1, source_target_pairs={{0,64},{16,80},{32,96},{48,112},{64,128},{80,144},{96,160},{112,17... | collective-permute-start | bytes 491528 | tf_op jit(solution)/shard_map/ppermute | solution.py:579
  90.0 0.6 copy-start.1
  100.4 17.0 %copy-start.5 = (bf16[2,64,2560]{2,1,0:T(8,128)(2,1)}, bf16[2,64,2560]{2,1,0:T(8,128)(2,1)S(1)}, u32[]{:S(2)}) copy-start(bf16[2,64,2560]{2,1,0:T(8,128)(2,1)S(1)} %collective-permute-done.14.left_ref) | copy-start | bytes 1966084
  100.4 17.0 %copy-start.6 = (bf16[2,64,2560]{2,1,0:T(8,128)(2,1)}, bf16[2,64,2560]{2,1,0:T(8,128)(2,1)S(1)}, u32[]{:S(2)}) copy-start(bf16[2,64,2560]{2,1,0:T(8,128)(2,1)S(1)} %collective-permute-done.15.right_ref) | copy-start | bytes 1966084
  100.4 56.3 %all-to-all-start.1 = ((bf16[16,384,128]{2,1,0:T(8,128)(2,1)}), bf16[16,384,128]{2,1,0:T(8,128)(2,1)S(1)}, u32[]{:S(2)}, u32[]{:S(2)}) async-start(bf16[16,384,128]{2,1,0:T(8,128)(2,1)} %head.1), calls=%async_computation.1 | async-start | bytes 3145728 | tf_op jit(solution)/shard_map/all_to_all | solution.py:619
  109.7 44.7 %collective-permute-start.11 = (bf16[384,128]{1,0:T(8,128)(2,1)S(1)}, bf16[384,128]{1,0:T(8,128)(2,1)S(1)}, u32[]{:S(2)}, u32[]{:S(2)}) collective-permute-start(bf16[384,128]{1,0:T(8,128)(2,1)S(1)} %get-tuple-element.92), channel_id=1, source_target_pairs={{0,48},{16,0},{32,16},{48,32},{64,112},{80,64},{96,80},{112,96},{1... | collective-permute-start | bytes 294920 | tf_op jit(solution)/shard_map/ppermute | solution.py:579
  113.2 41.2 %collective-permute-start.12 = (bf16[384,128]{1,0:T(8,128)(2,1)S(1)}, bf16[384,128]{1,0:T(8,128)(2,1)S(1)}, u32[]{:S(2)}, u32[]{:S(2)}) collective-permute-start(bf16[384,128]{1,0:T(8,128)(2,1)S(1)} %get-tuple-element.93), channel_id=1, source_target_pairs={{0,32},{16,48},{32,0},{48,16},{64,96},{80,112},{96,64},{112,80},{1... | collective-permute-start | bytes 294920 | tf_op jit(solution)/shard_map/ppermute | solution.py:579
  115.3 41.4 %collective-permute-start.13 = (bf16[384,128]{1,0:T(8,128)(2,1)S(1)}, bf16[384,128]{1,0:T(8,128)(2,1)S(1)}, u32[]{:S(2)}, u32[]{:S(2)}) collective-permute-start(bf16[384,128]{1,0:T(8,128)(2,1)S(1)} %get-tuple-element.94), channel_id=1, source_target_pairs={{0,16},{16,32},{32,48},{48,0},{64,80},{80,96},{96,112},{112,64},{1... | collective-permute-start | bytes 294920 | tf_op jit(solution)/shard_map/ppermute | solution.py:579
  154.4 2.3 %copy-start.7 = (bf16[384,128]{1,0:T(8,128)(2,1)}, bf16[384,128]{1,0:T(8,128)(2,1)S(1)}, u32[]{:S(2)}) copy-start(bf16[384,128]{1,0:T(8,128)(2,1)S(1)} %collective-permute-done.11.z1_hbm) | copy-start | bytes 294916
  154.4 2.3 %copy-start.8 = (bf16[384,128]{1,0:T(8,128)(2,1)}, bf16[384,128]{1,0:T(8,128)(2,1)S(1)}, u32[]{:S(2)}) copy-start(bf16[384,128]{1,0:T(8,128)(2,1)S(1)} %collective-permute-done.12.z2_hbm) | copy-start | bytes 294916
  156.7 0.6 copy-start.9
  157.3 1.2 copy-start.2

commit v4 on v3

--- a/solution.py
+++ b/solution.py
@@ -189,15 +189,15 @@
 
 
 def own_kernel(
-    side_ref, q_ref, k_ref, v_ref, o_ref, g_ref, before_ref, after_ref, lse_ref,
+    inner, at_ref, q_ref, k_ref, v_ref, o_ref, g_ref, before_ref, after_ref, lse_ref,
     sums_ref, low_ref, high_ref,
 ):
     step = pl.program_id(0)
     width = POS + 2 * TILE
     key = lax.broadcasted_iota(jnp.int32, (width, POS), 0)
     query = lax.broadcasted_iota(jnp.int32, (width, POS), 1)
-    first = jnp.where(side_ref[0] > 0, 0, TILE)
-    last = jnp.where(side_ref[0] < side_ref[1] - 1, width, width - TILE)
+    first = jnp.where(at_ref[0] > 0, 0, TILE)
+    last = jnp.where(at_ref[0] < inner - 1, width, width - TILE)
     inside = (key >= query) & (key <= query + 2 * TILE) & (key >= first) & (key < last)
     rows = deltas([g_ref[:, cols(j)] for j in range(SIDE)], [o_ref[:, cols(j)] for j in range(SIDE)])
     for j in range(SIDE):
@@ -482,7 +482,7 @@
         out_specs=ANY,
         scratch_shapes=[pltpu.VMEM(q.shape, BF)] * 5
         + [pltpu.VMEM((GROUP, ROWS_B, HEAD), BF), pltpu.SemaphoreType.DMA((24,))],
-        compiler_params=room(60),
+        compiler_params=room(63),
         cost_estimate=cost(4),
         name="pack_b",
     )(*args)
@@ -528,7 +528,7 @@
         out_shape=shape(*sums.shape),
         in_specs=[rows, edge, edge],
         out_specs=rows,
-        compiler_params=room(60),
+        compiler_params=room(63),
         cost_estimate=cost(4),
         name="settle",
     )(sums, left, right)
@@ -550,14 +550,14 @@
     )(group, *shares, b, base)
 
 
-def own_call(sides, q, k, v, o, g, before, after, lse):
+def own_call(inner, inner_at, q, k, v, o, g, before, after, lse):
     feature = q.shape[1]
     rows = pl.BlockSpec((POS, WIDE), lambda i: (0, i))
     edge = pl.BlockSpec((2, TILE, WIDE), lambda i: (0, 0, i))
     whole = pl.BlockSpec(lse.shape, lambda i: (0, 0, 0))
     halo = shape(2, TILE, feature)
     return pl.pallas_call(
-        own_kernel,
+        functools.partial(own_kernel, inner),
         grid=(feature // WIDE,),
         out_shape=(shape(3, POS, feature, dtype=F32), halo, halo),
         in_specs=[SMEM] + [rows] * 5 + [edge, edge, whole],
@@ -565,7 +565,7 @@
         compiler_params=room(63),
         cost_estimate=cost(9),
         name="own",
-    )(sides, q, k, v, o, g, before, after, lse)
+    )(inner_at, q, k, v, o, g, before, after, lse)
 
 
 def around(axis_step, shares):
@@ -586,7 +586,6 @@
     inner = lax.axis_size("inner")
     inner_at = lax.axis_index("inner").astype(jnp.int32)
     group_at = lax.axis_index("group").astype(jnp.int32)
-    sides = jnp.stack([inner_at, jnp.full((), inner, jnp.int32)])
     up = [(i, i + 1) for i in range(inner - 1)]
     down = [(i + 1, i) for i in range(inner - 1)]
     group = group_at.reshape(1)
@@ -602,7 +601,7 @@
 
     sends_y = four_call(split_kernel, shape(SIDE, ROWS_A, HEAD), [], 3, "split", group, got_z)
     got_y = around((1, 0), sends_y)
-    sums, to_low, to_high = own_call(sides, *rows, before, after, lse)
+    sums, to_low, to_high = own_call(inner, inner_at.reshape(1), *rows, before, after, lse)
     got_y, to_low, to_high = lax.optimization_barrier((got_y, to_low, to_high))
     scratch = [pltpu.VMEM((GROUP, HALF, HEAD), BF)] * 2 + SCRATCH
     back_y = four_call(quarter_kernel, shape(SIDE, ROWS_R, HEAD), scratch, 3, "quarter", group, got_y)

time: 163 us -> 161 us (0.988)
  the two profiles are of different devices: /device:TPU:3 before, /device:TPU:23 now
where the time goes in v4:
time: 161 us; the launch traced here: 158 us
  waiting for transfers between devices  64.5 us (40%)
  starting transfers between devices  56.1 us (35%)
  Pallas kernels  35.9 us (22%)
    ppermute x12, waiting for transfers between devices, around(): lax.ppermute(shares[d], 'group', [(i, partner(i, step)) for i in range(GR...  63.2 us
    ppermute x12, starting transfers between devices, around(): lax.ppermute(shares[d], 'group', [(i, partner(i, step)) for i in range(GR...  25.2 us
    all_to_all x1, starting transfers between devices, body(): home_b = lax.all_to_all(back_b, 'group', 0, 0, tiled=True)  10.6 us
    pallas_call x1, Pallas kernels, own_call(): pl.pallas_call(functools.partial(own_kernel, inner), grid=(feature // WID...  8.91 us
    pallas_call x1, Pallas kernels, head_call(): pl.pallas_call(head_kernel, out_shape=shape(GROUP, BACK_B, HEAD), in_spec...  8.05 us
    all_to_all x1, starting transfers between devices, body(): got_b = lax.all_to_all(send_b, 'group', 0, 0, tiled=True)  7.82 us
    pallas_call x1, Pallas kernels, settle_call(): pl.pallas_call(settle_kernel, grid=(sums.shape[2] // WIDE,), out_shape=sh...  5.18 us
    ppermute x1, starting transfers between devices, body(): from_left = lax.ppermute(to_high, 'inner', up)  4.67 us
  transfers between devices with their start and end apart: 18, of which 11 were waited for; matrix products, arithmetic and copies ran while one was open for 0% of the time, Pallas kernels for 18%

profile of v4, /device:TPU:23, one launch (start us, length us, event | category | flops | bytes accessed | tf_op | source)
XLA Modules:
  0.0 158.1 jit_solution(720482079783583148)
XLA Ops:
  0.6 3.5 %pack_a.1 = (bf16[528,128]{1,0:T(8,128)(2,1)}, bf16[528,128]{1,0:T(8,128)(2,1)}, bf16[528,128]{1,0:T(8,128)(2,1)}, bf16[528,128]{1,0:T(8,128)(2,1)}, bf16[2,64,2...) custom-call(s32[1]{0:T(128)} %bitcast.group_ref, s32[2,11]{1,0:T(2,128)} %bitcast.31, s32[2,11]{1,0:T(2,128)} %bitcast.33, ...), custom_call_target="tpu_custom_call" | custom-call | bytes 9000000 | tf_op jit(solution)/shard_map/pack_a/pallas_call | solution.py:459
  4.1 4.0 %collective-permute-start.3 = (bf16[2,64,2560]{2,1,0:T(8,128)(2,1)}, bf16[2,64,2560]{2,1,0:T(8,128)(2,1)}, u32[]{:S(2)}, u32[]{:S(2)}) collective-permute-start(bf16[2,64,2560]{2,1,0:T(8,128)(2,1)} %get-tuple-element.58), channel_id=1, source_target_pairs={{0,1},{1,2},{2,3},{3,4},{4,5},{5,6},{6,7},{7,8},{8,9},{9,10},{10,1... | collective-permute-start | bytes 1966088 | tf_op jit(solution)/shard_map/ppermute | solution.py:596
  8.1 1.9 %collective-permute-start.4 = (bf16[2,64,2560]{2,1,0:T(8,128)(2,1)}, bf16[2,64,2560]{2,1,0:T(8,128)(2,1)}, u32[]{:S(2)}, u32[]{:S(2)}) collective-permute-start(bf16[2,64,2560]{2,1,0:T(8,128)(2,1)} %get-tuple-element.59), channel_id=1, source_target_pairs={{1,0},{2,1},{3,2},{4,3},{5,4},{6,5},{7,6},{8,7},{9,8},{10,9},{11,1... | collective-permute-start | bytes 1966088 | tf_op jit(solution)/shard_map/ppermute | solution.py:597
  10.1 3.1 %collective-permute-start = (bf16[528,128]{1,0:T(8,128)(2,1)}, bf16[528,128]{1,0:T(8,128)(2,1)S(1)}, u32[]{:S(2)}, u32[]{:S(2)}) collective-permute-start(bf16[528,128]{1,0:T(8,128)(2,1)} %get-tuple-element.55), channel_id=1, source_target_pairs={{0,16},{16,32},{32,48},{48,0},{64,80},{80,96},{96,112},{112,64},{1... | collective-permute-start | bytes 405512 | tf_op jit(solution)/shard_map/ppermute | solution.py:579
  13.1 4.2 %collective-permute-start.1 = (bf16[528,128]{1,0:T(8,128)(2,1)}, bf16[528,128]{1,0:T(8,128)(2,1)S(1)}, u32[]{:S(2)}, u32[]{:S(2)}) collective-permute-start(bf16[528,128]{1,0:T(8,128)(2,1)} %get-tuple-element.56), channel_id=1, source_target_pairs={{0,32},{16,48},{32,0},{48,16},{64,96},{80,112},{96,64},{112,80},{1... | collective-permute-start | bytes 405512 | tf_op jit(solution)/shard_map/ppermute | solution.py:579
  17.4 2.4 %collective-permute-start.2 = (bf16[528,128]{1,0:T(8,128)(2,1)}, bf16[528,128]{1,0:T(8,128)(2,1)S(1)}, u32[]{:S(2)}, u32[]{:S(2)}) collective-permute-start(bf16[528,128]{1,0:T(8,128)(2,1)} %get-tuple-element.57), channel_id=1, source_target_pairs={{0,48},{16,0},{32,16},{48,32},{64,112},{80,64},{96,80},{112,96},{1... | collective-permute-start | bytes 405512 | tf_op jit(solution)/shard_map/ppermute | solution.py:579
  19.7 3.8 %pack_b.1 = bf16[16,528,128]{2,1,0:T(8,128)(2,1)} custom-call(s32[1]{0:T(128)} %bitcast.group_ref, s32[2,11]{1,0:T(2,128)} %bitcast.32, s32[2,11]{1,0:T(2,128)} %bitcast.34, f32[20,1,128]{2,1,0:T(1,128)} %bitcast.29, bf16[128,2560]{1,0:T(8,128)(2,1)} %bitcast.14, bf16[128,2560]{1,0:T(8,128)(2,1)} %bitcast.17, bf16[128,2560]{1,0:T(8,128)(2,1)} %bitcast.20, ...), custom_call_target="tpu_custom_call" | custom-call | bytes 12000000 | tf_op jit(solution)/shard_map/pack_b/pallas_call | solution.py:478
  23.6 6.8 %collective-permute-done.refs_1_ = bf16[528,128]{1,0:T(8,128)(2,1)S(1)} collective-permute-done((bf16[528,128]{1,0:T(8,128)(2,1)}, bf16[528,128]{1,0:T(8,128)(2,1)S(1)}, u32[]{:S(2)}, u32[]{:S(2)}) %collective-permute-start) | collective-permute-done | bytes 135200 | tf_op jit(solution)/shard_map/ppermute | solution.py:579
  30.4 2.2 %collective-permute-done.1.refs_2_ = bf16[528,128]{1,0:T(8,128)(2,1)S(1)} collective-permute-done((bf16[528,128]{1,0:T(8,128)(2,1)}, bf16[528,128]{1,0:T(8,128)(2,1)S(1)}, u32[]{:S(2)}, u32[]{:S(2)}) %collective-permute-start.1) | collective-permute-done | bytes 135200 | tf_op jit(solution)/shard_map/ppermute | solution.py:579
  32.6 0.0 collective-permute-done.2.refs_3_
  32.6 0.0 collective-permute-done.3.before_ref
  32.6 0.0 collective-permute-done.4.after_ref
  32.6 0.0 copy-start
  32.6 7.8 %all-to-all-start = ((bf16[16,528,128]{2,1,0:T(8,128)(2,1)}), bf16[16,528,128]{2,1,0:T(8,128)(2,1)}, u32[]{:S(2)}, u32[]{:S(2)}) async-start(bf16[16,528,128]{2,1,0:T(8,128)(2,1)} %pack_b.1), calls=%async_computation | async-start | bytes 4325376 | tf_op jit(solution)/shard_map/all_to_all | solution.py:600
  40.4 0.9 split.1
  41.4 0.9 collective-permute-start.5
  42.2 0.6 collective-permute-start.6
  42.8 0.8 collective-permute-start.7
  43.6 8.9 %own.1 = (f32[3,128,2560]{2,1,0:T(8,128)}, bf16[2,64,2560]{2,1,0:T(8,128)(2,1)}, bf16[2,64,2560]{2,1,0:T(8,128)(2,1)}) custom-call(s32[1]{0:T(128)} %bitcast.9.at_ref, bf16[128,2560]{1,0:T(8,128)(2,1)} %bitcast.15, bf16[128,2560]{1,0:T(8,128)(2,1)} %bitcast.18, bf16[128,2560]{1,0:T(8,128)(2,1)} %bitcast.21, bf16[128,2560]{1,0:T(8,128)(2,1)} %bitcast.24, ...), custom_call_target="tpu_custom_call" | custom-call | bytes 27000000 | tf_op jit(solution)/shard_map/own/pallas_call | solution.py:559
  52.5 6.5 %collective-permute-done.5.refs_1_ = bf16[4,208,128]{2,1,0:T(8,128)(2,1)S(1)} collective-permute-done((bf16[4,208,128]{2,1,0:T(8,128)(2,1)}, bf16[4,208,128]{2,1,0:T(8,128)(2,1)S(1)}, u32[]{:S(2)}, u32[]{:S(2)}) %collective-permute-start.5) | collective-permute-done | bytes 213024 | tf_op jit(solution)/shard_map/ppermute | solution.py:579
  59.0 0.0 collective-permute-done.6.refs_2_
  59.0 0.3 collective-permute-done.7.refs_3_
  59.3 2.1 %quarter.1 = (bf16[4,160,128]{2,1,0:T(8,128)(2,1)S(1)}, bf16[4,160,128]{2,1,0:T(8,128)(2,1)S(1)}, bf16[4,160,128]{2,1,0:T(8,128)(2,1)S(1)}, bf16[4,160,128]{2,1,0:T(8,128)(2,1)S(1)}) custom-call(s32[1]{0:T(128)} %bitcast.group_ref, bf16[4,208,128]{2,1,0:T(8,128)(2,1)S(1)} %get-tuple-element.73.refs_0_, ...), custom_call_target="tpu_custom_call" | custom-call | bytes 9000000 | tf_op jit(solution)/shard_map/quarter/pallas_call | solution.py:492
  61.4 4.7 %collective-permute-start.14 = (bf16[2,64,2560]{2,1,0:T(8,128)(2,1)}, bf16[2,64,2560]{2,1,0:T(8,128)(2,1)S(1)}, u32[]{:S(2)}, u32[]{:S(2)}) collective-permute-start(bf16[2,64,2560]{2,1,0:T(8,128)(2,1)} %get-tuple-element.96), channel_id=1, source_target_pairs={{0,1},{1,2},{2,3},{3,4},{4,5},{5,6},{6,7},{7,8},{8,9},{9,10},{10,1... | collective-permute-start | bytes 1966088 | tf_op jit(solution)/shard_map/ppermute | solution.py:611
  66.1 1.9 %collective-permute-start.15 = (bf16[2,64,2560]{2,1,0:T(8,128)(2,1)}, bf16[2,64,2560]{2,1,0:T(8,128)(2,1)S(1)}, u32[]{:S(2)}, u32[]{:S(2)}) collective-permute-start(bf16[2,64,2560]{2,1,0:T(8,128)(2,1)} %get-tuple-element.97), channel_id=1, source_target_pairs={{1,0},{2,1},{3,2},{4,3},{5,4},{6,5},{7,6},{8,7},{9,8},{10,9},{11,1... | collective-permute-start | bytes 1966088 | tf_op jit(solution)/shard_map/ppermute | solution.py:610
  68.0 0.1 collective-permute-start.8
  68.1 3.8 %collective-permute-start.9 = (bf16[4,160,128]{2,1,0:T(8,128)(2,1)S(1)}, bf16[4,160,128]{2,1,0:T(8,128)(2,1)S(1)}, u32[]{:S(2)}, u32[]{:S(2)}) collective-permute-start(bf16[4,160,128]{2,1,0:T(8,128)(2,1)S(1)} %get-tuple-element.85), channel_id=1, source_target_pairs={{0,128},{16,144},{32,160},{48,176},{64,192},{80,208},{96,224},{112... | collective-permute-start | bytes 491528 | tf_op jit(solution)/shard_map/ppermute | solution.py:579
  71.9 2.0 %collective-permute-start.10 = (bf16[4,160,128]{2,1,0:T(8,128)(2,1)S(1)}, bf16[4,160,128]{2,1,0:T(8,128)(2,1)S(1)}, u32[]{:S(2)}, u32[]{:S(2)}) collective-permute-start(bf16[4,160,128]{2,1,0:T(8,128)(2,1)S(1)} %get-tuple-element.86), channel_id=1, source_target_pairs={{0,64},{16,80},{32,96},{48,112},{64,128},{80,144},{96,160},{112,17... | collective-permute-start | bytes 491528 | tf_op jit(solution)/shard_map/ppermute | solution.py:579
  73.9 0.5 collective-permute-done.8.refs_1_
  74.4 10.2 %collective-permute-done.9.refs_2_ = bf16[4,160,128]{2,1,0:T(8,128)(2,1)S(1)} collective-permute-done((bf16[4,160,128]{2,1,0:T(8,128)(2,1)S(1)}, bf16[4,160,128]{2,1,0:T(8,128)(2,1)S(1)}, u32[]{:S(2)}, u32[]{:S(2)}) %collective-permute-start.9) | collective-permute-done | bytes 163872 | tf_op jit(solution)/shard_map/ppermute | solution.py:579
  84.6 3.2 %collective-permute-done.10.refs_3_ = bf16[4,160,128]{2,1,0:T(8,128)(2,1)S(1)} collective-permute-done((bf16[4,160,128]{2,1,0:T(8,128)(2,1)S(1)}, bf16[4,160,128]{2,1,0:T(8,128)(2,1)S(1)}, u32[]{:S(2)}, u32[]{:S(2)}) %collective-permute-start.10) | collective-permute-done | bytes 163872 | tf_op jit(solution)/shard_map/ppermute | solution.py:579
  87.8 0.2 merge.1
  87.9 0.6 copy-done.1
  88.6 1.3 all-to-all-done.in_hbm
  89.8 8.0 %head.1 = bf16[16,384,128]{2,1,0:T(8,128)(2,1)} custom-call(bf16[16,528,128]{2,1,0:T(8,128)(2,1)} %all-to-all-done.in_hbm), custom_call_target="tpu_custom_call" | custom-call | bytes 24000000 | tf_op jit(solution)/shard_map/head/pallas_call | solution.py:505
  97.9 0.0 collective-permute-done.14.left_ref
  97.9 0.0 copy-start.2
  97.9 0.0 collective-permute-done.15.right_ref
  97.9 0.0 copy-start.3
  98.0 10.6 %all-to-all-start.1 = ((bf16[16,384,128]{2,1,0:T(8,128)(2,1)}), bf16[16,384,128]{2,1,0:T(8,128)(2,1)}, u32[]{:S(2)}, u32[]{:S(2)}) async-start(bf16[16,384,128]{2,1,0:T(8,128)(2,1)} %head.1), calls=%async_computation.1 | async-start | bytes 3145728 | tf_op jit(solution)/shard_map/all_to_all | solution.py:618
  108.5 3.3 %collective-permute-start.11 = (bf16[384,128]{1,0:T(8,128)(2,1)S(1)}, bf16[384,128]{1,0:T(8,128)(2,1)}, u32[]{:S(2)}, u32[]{:S(2)}) collective-permute-start(bf16[384,128]{1,0:T(8,128)(2,1)S(1)} %get-tuple-element.92), channel_id=1, source_target_pairs={{0,48},{16,0},{32,16},{48,32},{64,112},{80,64},{96,80},{112,96},{1... | collective-permute-start | bytes 294920 | tf_op jit(solution)/shard_map/ppermute | solution.py:579
  111.8 2.1 %collective-permute-start.12 = (bf16[384,128]{1,0:T(8,128)(2,1)S(1)}, bf16[384,128]{1,0:T(8,128)(2,1)}, u32[]{:S(2)}, u32[]{:S(2)}) collective-permute-start(bf16[384,128]{1,0:T(8,128)(2,1)S(1)} %get-tuple-element.93), channel_id=1, source_target_pairs={{0,32},{16,48},{32,0},{48,16},{64,96},{80,112},{96,64},{112,80},{1... | collective-permute-start | bytes 294920 | tf_op jit(solution)/shard_map/ppermute | solution.py:579
  113.9 2.1 %collective-permute-start.13 = (bf16[384,128]{1,0:T(8,128)(2,1)S(1)}, bf16[384,128]{1,0:T(8,128)(2,1)}, u32[]{:S(2)}, u32[]{:S(2)}) collective-permute-start(bf16[384,128]{1,0:T(8,128)(2,1)S(1)} %get-tuple-element.94), channel_id=1, source_target_pairs={{0,16},{16,32},{32,48},{48,0},{64,80},{80,96},{96,112},{112,64},{1... | collective-permute-start | bytes 294920 | tf_op jit(solution)/shard_map/ppermute | solution.py:579
  116.0 5.2 %settle.1.base_in = bf16[3,128,2560]{2,1,0:T(8,128)(2,1)} custom-call(f32[3,128,2560]{2,1,0:T(8,128)} %get-tuple-element.99.sums_ref, bf16[2,64,2560]{2,1,0:T(8,128)(2,1)} %copy-done.2, bf16[2,64,2560]{2,1,0:T(8,128)(2,1)} %copy-done.3), custom_call_target="tpu_custom_call" | custom-call | bytes 12000000 | tf_op jit(solution)/shard_map/settle/pallas_call | solution.py:525
  121.2 31.3 %collective-permute-done.11.z1_hbm = bf16[384,128]{1,0:T(8,128)(2,1)} collective-permute-done((bf16[384,128]{1,0:T(8,128)(2,1)S(1)}, bf16[384,128]{1,0:T(8,128)(2,1)}, u32[]{:S(2)}, u32[]{:S(2)}) %collective-permute-start.11) | collective-permute-done | bytes 98336 | tf_op jit(solution)/shard_map/ppermute | solution.py:579
  152.5 0.2 collective-permute-done.12.z2_hbm
  152.7 2.0 %collective-permute-done.13.z3_hbm = bf16[384,128]{1,0:T(8,128)(2,1)} collective-permute-done((bf16[384,128]{1,0:T(8,128)(2,1)S(1)}, bf16[384,128]{1,0:T(8,128)(2,1)}, u32[]{:S(2)}, u32[]{:S(2)}) %collective-permute-start.13) | collective-permute-done | bytes 98336 | tf_op jit(solution)/shard_map/ppermute | solution.py:579
  154.7 3.2 %join.1 = (bf16[128,2560]{1,0:T(8,128)(2,1)}, bf16[128,2560]{1,0:T(8,128)(2,1)}, bf16[128,2560]{1,0:T(8,128)(2,1)}) custom-call(s32[1]{0:T(128)} %bitcast.group_ref, bf16[384,128]{1,0:T(8,128)(2,1)} %copy-done.1, bf16[384,128]{1,0:T(8,128)(2,1)} %collective-permute-done.11.z1_hbm, bf16[384,128]{1,0:T(8,128)(2,1)} %collective-permute-done.12.z2_hbm, ...), custom_call_target="tpu_custom_call" | custom-call | bytes 12000000 | tf_op jit(solution)/shard_map/join/pallas_call | solution.py:539
  (5 shorter events, 0.0 us)
Async XLA Ops:
  4.1 28.4 %collective-permute-start.3 = (bf16[2,64,2560]{2,1,0:T(8,128)(2,1)}, bf16[2,64,2560]{2,1,0:T(8,128)(2,1)}, u32[]{:S(2)}, u32[]{:S(2)}) collective-permute-start(bf16[2,64,2560]{2,1,0:T(8,128)(2,1)} %get-tuple-element.58), channel_id=1, source_target_pairs={{0,1},{1,2},{2,3},{3,4},{4,5},{5,6},{6,7},{7,8},{8,9},{9,10},{10,1... | collective-permute-start | bytes 1966088 | tf_op jit(solution)/shard_map/ppermute | solution.py:596
  8.1 24.4 %collective-permute-start.4 = (bf16[2,64,2560]{2,1,0:T(8,128)(2,1)}, bf16[2,64,2560]{2,1,0:T(8,128)(2,1)}, u32[]{:S(2)}, u32[]{:S(2)}) collective-permute-start(bf16[2,64,2560]{2,1,0:T(8,128)(2,1)} %get-tuple-element.59), channel_id=1, source_target_pairs={{1,0},{2,1},{3,2},{4,3},{5,4},{6,5},{7,6},{8,7},{9,8},{10,9},{11,1... | collective-permute-start | bytes 1966088 | tf_op jit(solution)/shard_map/ppermute | solution.py:597
  10.1 20.3 %collective-permute-start = (bf16[528,128]{1,0:T(8,128)(2,1)}, bf16[528,128]{1,0:T(8,128)(2,1)S(1)}, u32[]{:S(2)}, u32[]{:S(2)}) collective-permute-start(bf16[528,128]{1,0:T(8,128)(2,1)} %get-tuple-element.55), channel_id=1, source_target_pairs={{0,16},{16,32},{32,48},{48,0},{64,80},{80,96},{96,112},{112,64},{1... | collective-permute-start | bytes 405512 | tf_op jit(solution)/shard_map/ppermute | solution.py:579
  13.1 19.4 %collective-permute-start.1 = (bf16[528,128]{1,0:T(8,128)(2,1)}, bf16[528,128]{1,0:T(8,128)(2,1)S(1)}, u32[]{:S(2)}, u32[]{:S(2)}) collective-permute-start(bf16[528,128]{1,0:T(8,128)(2,1)} %get-tuple-element.56), channel_id=1, source_target_pairs={{0,32},{16,48},{32,0},{48,16},{64,96},{80,112},{96,64},{112,80},{1... | collective-permute-start | bytes 405512 | tf_op jit(solution)/shard_map/ppermute | solution.py:579
  17.4 15.2 %collective-permute-start.2 = (bf16[528,128]{1,0:T(8,128)(2,1)}, bf16[528,128]{1,0:T(8,128)(2,1)S(1)}, u32[]{:S(2)}, u32[]{:S(2)}) collective-permute-start(bf16[528,128]{1,0:T(8,128)(2,1)} %get-tuple-element.57), channel_id=1, source_target_pairs={{0,48},{16,0},{32,16},{48,32},{64,112},{80,64},{96,80},{112,96},{1... | collective-permute-start | bytes 405512 | tf_op jit(solution)/shard_map/ppermute | solution.py:579
  32.6 7.8 %copy-start = (bf16[528,128]{1,0:T(8,128)(2,1)S(1)}, bf16[528,128]{1,0:T(8,128)(2,1)}, u32[]{:S(2)}) copy-start(bf16[528,128]{1,0:T(8,128)(2,1)} %get-tuple-element.61.refs_0_) | copy-start | bytes 405508
  32.6 57.3 %all-to-all-start = ((bf16[16,528,128]{2,1,0:T(8,128)(2,1)}), bf16[16,528,128]{2,1,0:T(8,128)(2,1)}, u32[]{:S(2)}, u32[]{:S(2)}) async-start(bf16[16,528,128]{2,1,0:T(8,128)(2,1)} %pack_b.1), calls=%async_computation | async-start | bytes 4325376 | tf_op jit(solution)/shard_map/all_to_all | solution.py:600
  41.4 17.6 %collective-permute-start.5 = (bf16[4,208,128]{2,1,0:T(8,128)(2,1)}, bf16[4,208,128]{2,1,0:T(8,128)(2,1)S(1)}, u32[]{:S(2)}, u32[]{:S(2)}) collective-permute-start(bf16[4,208,128]{2,1,0:T(8,128)(2,1)} %get-tuple-element.66), channel_id=1, source_target_pairs={{0,64},{16,80},{32,96},{48,112},{64,128},{80,144},{96,160},{112,17... | collective-permute-start | bytes 638984 | tf_op jit(solution)/shard_map/ppermute | solution.py:579
  42.2 16.7 %collective-permute-start.6 = (bf16[4,208,128]{2,1,0:T(8,128)(2,1)}, bf16[4,208,128]{2,1,0:T(8,128)(2,1)S(1)}, u32[]{:S(2)}, u32[]{:S(2)}) collective-permute-start(bf16[4,208,128]{2,1,0:T(8,128)(2,1)} %get-tuple-element.67), channel_id=1, source_target_pairs={{0,128},{16,144},{32,160},{48,176},{64,192},{80,208},{96,224},{112... | collective-permute-start | bytes 638984 | tf_op jit(solution)/shard_map/ppermute | solution.py:579
  42.8 16.5 %collective-permute-start.7 = (bf16[4,208,128]{2,1,0:T(8,128)(2,1)}, bf16[4,208,128]{2,1,0:T(8,128)(2,1)S(1)}, u32[]{:S(2)}, u32[]{:S(2)}) collective-permute-start(bf16[4,208,128]{2,1,0:T(8,128)(2,1)} %get-tuple-element.68), channel_id=1, source_target_pairs={{0,192},{16,208},{32,224},{48,240},{64,0},{80,16},{96,32},{112,48}... | collective-permute-start | bytes 638984 | tf_op jit(solution)/shard_map/ppermute | solution.py:579
  61.4 36.5 %collective-permute-start.14 = (bf16[2,64,2560]{2,1,0:T(8,128)(2,1)}, bf16[2,64,2560]{2,1,0:T(8,128)(2,1)S(1)}, u32[]{:S(2)}, u32[]{:S(2)}) collective-permute-start(bf16[2,64,2560]{2,1,0:T(8,128)(2,1)} %get-tuple-element.96), channel_id=1, source_target_pairs={{0,1},{1,2},{2,3},{3,4},{4,5},{5,6},{6,7},{7,8},{8,9},{9,10},{10,1... | collective-permute-start | bytes 1966088 | tf_op jit(solution)/shard_map/ppermute | solution.py:611
  66.1 31.8 %collective-permute-start.15 = (bf16[2,64,2560]{2,1,0:T(8,128)(2,1)}, bf16[2,64,2560]{2,1,0:T(8,128)(2,1)S(1)}, u32[]{:S(2)}, u32[]{:S(2)}) collective-permute-start(bf16[2,64,2560]{2,1,0:T(8,128)(2,1)} %get-tuple-element.97), channel_id=1, source_target_pairs={{1,0},{2,1},{3,2},{4,3},{5,4},{6,5},{7,6},{8,7},{9,8},{10,9},{11,1... | collective-permute-start | bytes 1966088 | tf_op jit(solution)/shard_map/ppermute | solution.py:610
  68.0 6.3 %collective-permute-start.8 = (bf16[4,160,128]{2,1,0:T(8,128)(2,1)S(1)}, bf16[4,160,128]{2,1,0:T(8,128)(2,1)S(1)}, u32[]{:S(2)}, u32[]{:S(2)}) collective-permute-start(bf16[4,160,128]{2,1,0:T(8,128)(2,1)S(1)} %get-tuple-element.84), channel_id=1, source_target_pairs={{0,192},{16,208},{32,224},{48,240},{64,0},{80,16},{96,32},{112,48}... | collective-permute-start | bytes 491528 | tf_op jit(solution)/shard_map/ppermute | solution.py:579
  68.1 16.5 %collective-permute-start.9 = (bf16[4,160,128]{2,1,0:T(8,128)(2,1)S(1)}, bf16[4,160,128]{2,1,0:T(8,128)(2,1)S(1)}, u32[]{:S(2)}, u32[]{:S(2)}) collective-permute-start(bf16[4,160,128]{2,1,0:T(8,128)(2,1)S(1)} %get-tuple-element.85), channel_id=1, source_target_pairs={{0,128},{16,144},{32,160},{48,176},{64,192},{80,208},{96,224},{112... | collective-permute-start | bytes 491528 | tf_op jit(solution)/shard_map/ppermute | solution.py:579
  71.9 15.9 %collective-permute-start.10 = (bf16[4,160,128]{2,1,0:T(8,128)(2,1)S(1)}, bf16[4,160,128]{2,1,0:T(8,128)(2,1)S(1)}, u32[]{:S(2)}, u32[]{:S(2)}) collective-permute-start(bf16[4,160,128]{2,1,0:T(8,128)(2,1)S(1)} %get-tuple-element.86), channel_id=1, source_target_pairs={{0,64},{16,80},{32,96},{48,112},{64,128},{80,144},{96,160},{112,17... | collective-permute-start | bytes 491528 | tf_op jit(solution)/shard_map/ppermute | solution.py:579
  87.9 0.6 copy-start.1
  97.9 18.1 %copy-start.2 = (bf16[2,64,2560]{2,1,0:T(8,128)(2,1)}, bf16[2,64,2560]{2,1,0:T(8,128)(2,1)S(1)}, u32[]{:S(2)}) copy-start(bf16[2,64,2560]{2,1,0:T(8,128)(2,1)S(1)} %collective-permute-done.14.left_ref) | copy-start | bytes 1966084
  97.9 18.0 %copy-start.3 = (bf16[2,64,2560]{2,1,0:T(8,128)(2,1)}, bf16[2,64,2560]{2,1,0:T(8,128)(2,1)S(1)}, u32[]{:S(2)}) copy-start(bf16[2,64,2560]{2,1,0:T(8,128)(2,1)S(1)} %collective-permute-done.15.right_ref) | copy-start | bytes 1966084
  98.0 56.7 %all-to-all-start.1 = ((bf16[16,384,128]{2,1,0:T(8,128)(2,1)}), bf16[16,384,128]{2,1,0:T(8,128)(2,1)}, u32[]{:S(2)}, u32[]{:S(2)}) async-start(bf16[16,384,128]{2,1,0:T(8,128)(2,1)} %head.1), calls=%async_computation.1 | async-start | bytes 3145728 | tf_op jit(solution)/shard_map/all_to_all | solution.py:618
  108.5 43.9 %collective-permute-start.11 = (bf16[384,128]{1,0:T(8,128)(2,1)S(1)}, bf16[384,128]{1,0:T(8,128)(2,1)}, u32[]{:S(2)}, u32[]{:S(2)}) collective-permute-start(bf16[384,128]{1,0:T(8,128)(2,1)S(1)} %get-tuple-element.92), channel_id=1, source_target_pairs={{0,48},{16,0},{32,16},{48,32},{64,112},{80,64},{96,80},{112,96},{1... | collective-permute-start | bytes 294920 | tf_op jit(solution)/shard_map/ppermute | solution.py:579
  111.8 40.9 %collective-permute-start.12 = (bf16[384,128]{1,0:T(8,128)(2,1)S(1)}, bf16[384,128]{1,0:T(8,128)(2,1)}, u32[]{:S(2)}, u32[]{:S(2)}) collective-permute-start(bf16[384,128]{1,0:T(8,128)(2,1)S(1)} %get-tuple-element.93), channel_id=1, source_target_pairs={{0,32},{16,48},{32,0},{48,16},{64,96},{80,112},{96,64},{112,80},{1... | collective-permute-start | bytes 294920 | tf_op jit(solution)/shard_map/ppermute | solution.py:579
  113.9 40.8 %collective-permute-start.13 = (bf16[384,128]{1,0:T(8,128)(2,1)S(1)}, bf16[384,128]{1,0:T(8,128)(2,1)}, u32[]{:S(2)}, u32[]{:S(2)}) collective-permute-start(bf16[384,128]{1,0:T(8,128)(2,1)S(1)} %get-tuple-element.94), channel_id=1, source_target_pairs={{0,16},{16,32},{32,48},{48,0},{64,80},{80,96},{96,112},{112,64},{1... | collective-permute-start | bytes 294920 | tf_op jit(solution)/shard_map/ppermute | solution.py:579

commit v5 on v4

--- a/solution.py
+++ b/solution.py
@@ -222,7 +222,6 @@
 
 
 CHUNK = 512
-UNROLL = 2
 KEYS = GROUP * TILE
 
 
@@ -235,13 +234,11 @@
     kx_ref[:, 0:HEAD] = k
     kx_ref[:, HEAD:] = ((nt(spread, padded.astype(BF)) - 1.0) * BIG).astype(BF)
     kt_ref[...] = k.astype(F32).T.astype(BF)
-    dk_ref[...] = jnp.zeros_like(dk_ref)
-    dv_ref[...] = jnp.zeros_like(dv_ref)
     count = CHUNK // span
     query = lax.broadcasted_iota(jnp.int32, (CHUNK, HEAD), 0) // span
     column = lax.broadcasted_iota(jnp.int32, (CHUNK, HEAD), 1)
 
-    def one_chunk(c, carry):
+    for c in range(GROUP * span // CHUNK):
         frames = pl.ds(c * count, count)
         q, g = queries(frames)
         choose = (column == query + c * count).astype(F32).astype(BF)
@@ -252,12 +249,10 @@
         )
         p = jnp.exp2(nt(kx_ref[...], qx) * (SCALE * LOG2E) - lse * LOG2E)
         ds = (p * (nt(v, g) - delta)).astype(BF)
-        dv_ref[...] += nn(p.astype(BF), g)
-        dk_ref[...] += nn(ds, q)
+        dv, dk = nn(p.astype(BF), g), nn(ds, q)
+        dv_ref[...] = dv if c == 0 else dv_ref[...] + dv
+        dk_ref[...] = dk if c == 0 else dk_ref[...] + dk
         put_dq(frames, (nn(kt_ref[...], ds) * SCALE).T.astype(BF).reshape(count, span, HEAD))
-        return carry
-
-    lax.fori_loop(0, GROUP * span // CHUNK, one_chunk, 0, unroll=UNROLL)
 
 
 def added(stats, at):

time: 161 us -> 161 us (level)
  no operation moved by 1% of the time
where the time goes in v5:
time: 161 us; the launch traced here: 158 us
  waiting for transfers between devices  64.5 us (40%)
  starting transfers between devices  56.1 us (35%)
  Pallas kernels  35.9 us (22%)
    ppermute x12, waiting for transfers between devices, around(): lax.ppermute(shares[d], 'group', [(i, partner(i, step)) for i in range(GR...  63.2 us
    ppermute x12, starting transfers between devices, around(): lax.ppermute(shares[d], 'group', [(i, partner(i, step)) for i in range(GR...  25.2 us
    all_to_all x1, starting transfers between devices, body(): home_b = lax.all_to_all(back_b, 'group', 0, 0, tiled=True)  10.6 us
    pallas_call x1, Pallas kernels, own_call(): pl.pallas_call(functools.partial(own_kernel, inner), grid=(feature // WID...  8.91 us
    pallas_call x1, Pallas kernels, head_call(): pl.pallas_call(head_kernel, out_shape=shape(GROUP, BACK_B, HEAD), in_spec...  8.05 us
    all_to_all x1, starting transfers between devices, body(): got_b = lax.all_to_all(send_b, 'group', 0, 0, tiled=True)  7.82 us
    pallas_call x1, Pallas kernels, settle_call(): pl.pallas_call(settle_kernel, grid=(sums.shape[2] // WIDE,), out_shape=sh...  5.18 us
    ppermute x1, starting transfers between devices, body(): from_left = lax.ppermute(to_high, 'inner', up)  4.67 us
  transfers between devices with their start and end apart: 18, of which 11 were waited for; matrix products, arithmetic and copies ran while one was open for 0% of the time, Pallas kernels for 18%

profile of v5, /device:TPU:23, one launch (start us, length us, event | category | flops | bytes accessed | tf_op | source)
XLA Modules:
  0.0 158.1 jit_solution(720482079783583148)
XLA Ops:
  0.6 3.5 %pack_a.1 = (bf16[528,128]{1,0:T(8,128)(2,1)}, bf16[528,128]{1,0:T(8,128)(2,1)}, bf16[528,128]{1,0:T(8,128)(2,1)}, bf16[528,128]{1,0:T(8,128)(2,1)}, bf16[2,64,2...) custom-call(s32[1]{0:T(128)} %bitcast.group_ref, s32[2,11]{1,0:T(2,128)} %bitcast.31, s32[2,11]{1,0:T(2,128)} %bitcast.33, ...), custom_call_target="tpu_custom_call" | custom-call | bytes 9000000 | tf_op jit(solution)/shard_map/pack_a/pallas_call | solution.py:454
  4.1 4.0 %collective-permute-start.3 = (bf16[2,64,2560]{2,1,0:T(8,128)(2,1)}, bf16[2,64,2560]{2,1,0:T(8,128)(2,1)}, u32[]{:S(2)}, u32[]{:S(2)}) collective-permute-start(bf16[2,64,2560]{2,1,0:T(8,128)(2,1)} %get-tuple-element.58), channel_id=1, source_target_pairs={{0,1},{1,2},{2,3},{3,4},{4,5},{5,6},{6,7},{7,8},{8,9},{9,10},{10,1... | collective-permute-start | bytes 1966088 | tf_op jit(solution)/shard_map/ppermute | solution.py:591
  8.1 1.9 %collective-permute-start.4 = (bf16[2,64,2560]{2,1,0:T(8,128)(2,1)}, bf16[2,64,2560]{2,1,0:T(8,128)(2,1)}, u32[]{:S(2)}, u32[]{:S(2)}) collective-permute-start(bf16[2,64,2560]{2,1,0:T(8,128)(2,1)} %get-tuple-element.59), channel_id=1, source_target_pairs={{1,0},{2,1},{3,2},{4,3},{5,4},{6,5},{7,6},{8,7},{9,8},{10,9},{11,1... | collective-permute-start | bytes 1966088 | tf_op jit(solution)/shard_map/ppermute | solution.py:592
  10.1 3.1 %collective-permute-start = (bf16[528,128]{1,0:T(8,128)(2,1)}, bf16[528,128]{1,0:T(8,128)(2,1)S(1)}, u32[]{:S(2)}, u32[]{:S(2)}) collective-permute-start(bf16[528,128]{1,0:T(8,128)(2,1)} %get-tuple-element.55), channel_id=1, source_target_pairs={{0,16},{16,32},{32,48},{48,0},{64,80},{80,96},{96,112},{112,64},{1... | collective-permute-start | bytes 405512 | tf_op jit(solution)/shard_map/ppermute | solution.py:574
  13.1 4.2 %collective-permute-start.1 = (bf16[528,128]{1,0:T(8,128)(2,1)}, bf16[528,128]{1,0:T(8,128)(2,1)S(1)}, u32[]{:S(2)}, u32[]{:S(2)}) collective-permute-start(bf16[528,128]{1,0:T(8,128)(2,1)} %get-tuple-element.56), channel_id=1, source_target_pairs={{0,32},{16,48},{32,0},{48,16},{64,96},{80,112},{96,64},{112,80},{1... | collective-permute-start | bytes 405512 | tf_op jit(solution)/shard_map/ppermute | solution.py:574
  17.4 2.4 %collective-permute-start.2 = (bf16[528,128]{1,0:T(8,128)(2,1)}, bf16[528,128]{1,0:T(8,128)(2,1)S(1)}, u32[]{:S(2)}, u32[]{:S(2)}) collective-permute-start(bf16[528,128]{1,0:T(8,128)(2,1)} %get-tuple-element.57), channel_id=1, source_target_pairs={{0,48},{16,0},{32,16},{48,32},{64,112},{80,64},{96,80},{112,96},{1... | collective-permute-start | bytes 405512 | tf_op jit(solution)/shard_map/ppermute | solution.py:574
  19.7 3.8 %pack_b.1 = bf16[16,528,128]{2,1,0:T(8,128)(2,1)} custom-call(s32[1]{0:T(128)} %bitcast.group_ref, s32[2,11]{1,0:T(2,128)} %bitcast.32, s32[2,11]{1,0:T(2,128)} %bitcast.34, f32[20,1,128]{2,1,0:T(1,128)} %bitcast.29, bf16[128,2560]{1,0:T(8,128)(2,1)} %bitcast.14, bf16[128,2560]{1,0:T(8,128)(2,1)} %bitcast.17, bf16[128,2560]{1,0:T(8,128)(2,1)} %bitcast.20, ...), custom_call_target="tpu_custom_call" | custom-call | bytes 12000000 | tf_op jit(solution)/shard_map/pack_b/pallas_call | solution.py:473
  23.6 6.8 %collective-permute-done.refs_1_ = bf16[528,128]{1,0:T(8,128)(2,1)S(1)} collective-permute-done((bf16[528,128]{1,0:T(8,128)(2,1)}, bf16[528,128]{1,0:T(8,128)(2,1)S(1)}, u32[]{:S(2)}, u32[]{:S(2)}) %collective-permute-start) | collective-permute-done | bytes 135200 | tf_op jit(solution)/shard_map/ppermute | solution.py:574
  30.4 2.2 %collective-permute-done.1.refs_2_ = bf16[528,128]{1,0:T(8,128)(2,1)S(1)} collective-permute-done((bf16[528,128]{1,0:T(8,128)(2,1)}, bf16[528,128]{1,0:T(8,128)(2,1)S(1)}, u32[]{:S(2)}, u32[]{:S(2)}) %collective-permute-start.1) | collective-permute-done | bytes 135200 | tf_op jit(solution)/shard_map/ppermute | solution.py:574
  32.6 0.0 collective-permute-done.2.refs_3_
  32.6 0.0 collective-permute-done.3.before_ref
  32.6 0.0 collective-permute-done.4.after_ref
  32.6 0.0 copy-start
  32.6 7.8 %all-to-all-start = ((bf16[16,528,128]{2,1,0:T(8,128)(2,1)}), bf16[16,528,128]{2,1,0:T(8,128)(2,1)}, u32[]{:S(2)}, u32[]{:S(2)}) async-start(bf16[16,528,128]{2,1,0:T(8,128)(2,1)} %pack_b.1), calls=%async_computation | async-start | bytes 4325376 | tf_op jit(solution)/shard_map/all_to_all | solution.py:595
  40.4 0.9 split.1
  41.4 0.9 collective-permute-start.5
  42.2 0.6 collective-permute-start.6
  42.8 0.8 collective-permute-start.7
  43.6 8.9 %own.1 = (f32[3,128,2560]{2,1,0:T(8,128)}, bf16[2,64,2560]{2,1,0:T(8,128)(2,1)}, bf16[2,64,2560]{2,1,0:T(8,128)(2,1)}) custom-call(s32[1]{0:T(128)} %bitcast.9.at_ref, bf16[128,2560]{1,0:T(8,128)(2,1)} %bitcast.15, bf16[128,2560]{1,0:T(8,128)(2,1)} %bitcast.18, bf16[128,2560]{1,0:T(8,128)(2,1)} %bitcast.21, bf16[128,2560]{1,0:T(8,128)(2,1)} %bitcast.24, ...), custom_call_target="tpu_custom_call" | custom-call | bytes 27000000 | tf_op jit(solution)/shard_map/own/pallas_call | solution.py:554
  52.5 6.5 %collective-permute-done.5.refs_1_ = bf16[4,208,128]{2,1,0:T(8,128)(2,1)S(1)} collective-permute-done((bf16[4,208,128]{2,1,0:T(8,128)(2,1)}, bf16[4,208,128]{2,1,0:T(8,128)(2,1)S(1)}, u32[]{:S(2)}, u32[]{:S(2)}) %collective-permute-start.5) | collective-permute-done | bytes 213024 | tf_op jit(solution)/shard_map/ppermute | solution.py:574
  59.0 0.0 collective-permute-done.6.refs_2_
  59.0 0.3 collective-permute-done.7.refs_3_
  59.3 2.1 %quarter.1 = (bf16[4,160,128]{2,1,0:T(8,128)(2,1)S(1)}, bf16[4,160,128]{2,1,0:T(8,128)(2,1)S(1)}, bf16[4,160,128]{2,1,0:T(8,128)(2,1)S(1)}, bf16[4,160,128]{2,1,0:T(8,128)(2,1)S(1)}) custom-call(s32[1]{0:T(128)} %bitcast.group_ref, bf16[4,208,128]{2,1,0:T(8,128)(2,1)S(1)} %get-tuple-element.73.refs_0_, ...), custom_call_target="tpu_custom_call" | custom-call | bytes 9000000 | tf_op jit(solution)/shard_map/quarter/pallas_call | solution.py:487
  61.4 4.7 %collective-permute-start.14 = (bf16[2,64,2560]{2,1,0:T(8,128)(2,1)}, bf16[2,64,2560]{2,1,0:T(8,128)(2,1)S(1)}, u32[]{:S(2)}, u32[]{:S(2)}) collective-permute-start(bf16[2,64,2560]{2,1,0:T(8,128)(2,1)} %get-tuple-element.96), channel_id=1, source_target_pairs={{0,1},{1,2},{2,3},{3,4},{4,5},{5,6},{6,7},{7,8},{8,9},{9,10},{10,1... | collective-permute-start | bytes 1966088 | tf_op jit(solution)/shard_map/ppermute | solution.py:606
  66.1 1.9 %collective-permute-start.15 = (bf16[2,64,2560]{2,1,0:T(8,128)(2,1)}, bf16[2,64,2560]{2,1,0:T(8,128)(2,1)S(1)}, u32[]{:S(2)}, u32[]{:S(2)}) collective-permute-start(bf16[2,64,2560]{2,1,0:T(8,128)(2,1)} %get-tuple-element.97), channel_id=1, source_target_pairs={{1,0},{2,1},{3,2},{4,3},{5,4},{6,5},{7,6},{8,7},{9,8},{10,9},{11,1... | collective-permute-start | bytes 1966088 | tf_op jit(solution)/shard_map/ppermute | solution.py:605
  68.0 0.1 collective-permute-start.8
  68.1 3.8 %collective-permute-start.9 = (bf16[4,160,128]{2,1,0:T(8,128)(2,1)S(1)}, bf16[4,160,128]{2,1,0:T(8,128)(2,1)S(1)}, u32[]{:S(2)}, u32[]{:S(2)}) collective-permute-start(bf16[4,160,128]{2,1,0:T(8,128)(2,1)S(1)} %get-tuple-element.85), channel_id=1, source_target_pairs={{0,128},{16,144},{32,160},{48,176},{64,192},{80,208},{96,224},{112... | collective-permute-start | bytes 491528 | tf_op jit(solution)/shard_map/ppermute | solution.py:574
  71.9 2.0 %collective-permute-start.10 = (bf16[4,160,128]{2,1,0:T(8,128)(2,1)S(1)}, bf16[4,160,128]{2,1,0:T(8,128)(2,1)S(1)}, u32[]{:S(2)}, u32[]{:S(2)}) collective-permute-start(bf16[4,160,128]{2,1,0:T(8,128)(2,1)S(1)} %get-tuple-element.86), channel_id=1, source_target_pairs={{0,64},{16,80},{32,96},{48,112},{64,128},{80,144},{96,160},{112,17... | collective-permute-start | bytes 491528 | tf_op jit(solution)/shard_map/ppermute | solution.py:574
  73.9 0.5 collective-permute-done.8.refs_1_
  74.4 10.2 %collective-permute-done.9.refs_2_ = bf16[4,160,128]{2,1,0:T(8,128)(2,1)S(1)} collective-permute-done((bf16[4,160,128]{2,1,0:T(8,128)(2,1)S(1)}, bf16[4,160,128]{2,1,0:T(8,128)(2,1)S(1)}, u32[]{:S(2)}, u32[]{:S(2)}) %collective-permute-start.9) | collective-permute-done | bytes 163872 | tf_op jit(solution)/shard_map/ppermute | solution.py:574
  84.6 3.2 %collective-permute-done.10.refs_3_ = bf16[4,160,128]{2,1,0:T(8,128)(2,1)S(1)} collective-permute-done((bf16[4,160,128]{2,1,0:T(8,128)(2,1)S(1)}, bf16[4,160,128]{2,1,0:T(8,128)(2,1)S(1)}, u32[]{:S(2)}, u32[]{:S(2)}) %collective-permute-start.10) | collective-permute-done | bytes 163872 | tf_op jit(solution)/shard_map/ppermute | solution.py:574
  87.8 0.2 merge.1
  87.9 0.6 copy-done.1
  88.6 1.3 all-to-all-done.in_hbm
  89.8 8.0 %head.1 = bf16[16,384,128]{2,1,0:T(8,128)(2,1)} custom-call(bf16[16,528,128]{2,1,0:T(8,128)(2,1)} %all-to-all-done.in_hbm), custom_call_target="tpu_custom_call" | custom-call | bytes 24000000 | tf_op jit(solution)/shard_map/head/pallas_call | solution.py:500
  97.9 0.0 collective-permute-done.14.left_ref
  97.9 0.0 copy-start.2
  97.9 0.0 collective-permute-done.15.right_ref
  97.9 0.0 copy-start.3
  98.0 10.6 %all-to-all-start.1 = ((bf16[16,384,128]{2,1,0:T(8,128)(2,1)}), bf16[16,384,128]{2,1,0:T(8,128)(2,1)}, u32[]{:S(2)}, u32[]{:S(2)}) async-start(bf16[16,384,128]{2,1,0:T(8,128)(2,1)} %head.1), calls=%async_computation.1 | async-start | bytes 3145728 | tf_op jit(solution)/shard_map/all_to_all | solution.py:613
  108.5 3.3 %collective-permute-start.11 = (bf16[384,128]{1,0:T(8,128)(2,1)S(1)}, bf16[384,128]{1,0:T(8,128)(2,1)}, u32[]{:S(2)}, u32[]{:S(2)}) collective-permute-start(bf16[384,128]{1,0:T(8,128)(2,1)S(1)} %get-tuple-element.92), channel_id=1, source_target_pairs={{0,48},{16,0},{32,16},{48,32},{64,112},{80,64},{96,80},{112,96},{1... | collective-permute-start | bytes 294920 | tf_op jit(solution)/shard_map/ppermute | solution.py:574
  111.8 2.1 %collective-permute-start.12 = (bf16[384,128]{1,0:T(8,128)(2,1)S(1)}, bf16[384,128]{1,0:T(8,128)(2,1)}, u32[]{:S(2)}, u32[]{:S(2)}) collective-permute-start(bf16[384,128]{1,0:T(8,128)(2,1)S(1)} %get-tuple-element.93), channel_id=1, source_target_pairs={{0,32},{16,48},{32,0},{48,16},{64,96},{80,112},{96,64},{112,80},{1... | collective-permute-start | bytes 294920 | tf_op jit(solution)/shard_map/ppermute | solution.py:574
  113.9 2.1 %collective-permute-start.13 = (bf16[384,128]{1,0:T(8,128)(2,1)S(1)}, bf16[384,128]{1,0:T(8,128)(2,1)}, u32[]{:S(2)}, u32[]{:S(2)}) collective-permute-start(bf16[384,128]{1,0:T(8,128)(2,1)S(1)} %get-tuple-element.94), channel_id=1, source_target_pairs={{0,16},{16,32},{32,48},{48,0},{64,80},{80,96},{96,112},{112,64},{1... | collective-permute-start | bytes 294920 | tf_op jit(solution)/shard_map/ppermute | solution.py:574
  116.0 5.2 %settle.1.base_in = bf16[3,128,2560]{2,1,0:T(8,128)(2,1)} custom-call(f32[3,128,2560]{2,1,0:T(8,128)} %get-tuple-element.99.sums_ref, bf16[2,64,2560]{2,1,0:T(8,128)(2,1)} %copy-done.2, bf16[2,64,2560]{2,1,0:T(8,128)(2,1)} %copy-done.3), custom_call_target="tpu_custom_call" | custom-call | bytes 12000000 | tf_op jit(solution)/shard_map/settle/pallas_call | solution.py:520
  121.2 31.3 %collective-permute-done.11.z1_hbm = bf16[384,128]{1,0:T(8,128)(2,1)} collective-permute-done((bf16[384,128]{1,0:T(8,128)(2,1)S(1)}, bf16[384,128]{1,0:T(8,128)(2,1)}, u32[]{:S(2)}, u32[]{:S(2)}) %collective-permute-start.11) | collective-permute-done | bytes 98336 | tf_op jit(solution)/shard_map/ppermute | solution.py:574
  152.5 0.2 collective-permute-done.12.z2_hbm
  152.7 2.0 %collective-permute-done.13.z3_hbm = bf16[384,128]{1,0:T(8,128)(2,1)} collective-permute-done((bf16[384,128]{1,0:T(8,128)(2,1)S(1)}, bf16[384,128]{1,0:T(8,128)(2,1)}, u32[]{:S(2)}, u32[]{:S(2)}) %collective-permute-start.13) | collective-permute-done | bytes 98336 | tf_op jit(solution)/shard_map/ppermute | solution.py:574
  154.7 3.2 %join.1 = (bf16[128,2560]{1,0:T(8,128)(2,1)}, bf16[128,2560]{1,0:T(8,128)(2,1)}, bf16[128,2560]{1,0:T(8,128)(2,1)}) custom-call(s32[1]{0:T(128)} %bitcast.group_ref, bf16[384,128]{1,0:T(8,128)(2,1)} %copy-done.1, bf16[384,128]{1,0:T(8,128)(2,1)} %collective-permute-done.11.z1_hbm, bf16[384,128]{1,0:T(8,128)(2,1)} %collective-permute-done.12.z2_hbm, ...), custom_call_target="tpu_custom_call" | custom-call | bytes 12000000 | tf_op jit(solution)/shard_map/join/pallas_call | solution.py:534
  (5 shorter events, 0.0 us)
Async XLA Ops:
  4.1 28.4 %collective-permute-start.3 = (bf16[2,64,2560]{2,1,0:T(8,128)(2,1)}, bf16[2,64,2560]{2,1,0:T(8,128)(2,1)}, u32[]{:S(2)}, u32[]{:S(2)}) collective-permute-start(bf16[2,64,2560]{2,1,0:T(8,128)(2,1)} %get-tuple-element.58), channel_id=1, source_target_pairs={{0,1},{1,2},{2,3},{3,4},{4,5},{5,6},{6,7},{7,8},{8,9},{9,10},{10,1... | collective-permute-start | bytes 1966088 | tf_op jit(solution)/shard_map/ppermute | solution.py:591
  8.1 24.4 %collective-permute-start.4 = (bf16[2,64,2560]{2,1,0:T(8,128)(2,1)}, bf16[2,64,2560]{2,1,0:T(8,128)(2,1)}, u32[]{:S(2)}, u32[]{:S(2)}) collective-permute-start(bf16[2,64,2560]{2,1,0:T(8,128)(2,1)} %get-tuple-element.59), channel_id=1, source_target_pairs={{1,0},{2,1},{3,2},{4,3},{5,4},{6,5},{7,6},{8,7},{9,8},{10,9},{11,1... | collective-permute-start | bytes 1966088 | tf_op jit(solution)/shard_map/ppermute | solution.py:592
  10.1 20.3 %collective-permute-start = (bf16[528,128]{1,0:T(8,128)(2,1)}, bf16[528,128]{1,0:T(8,128)(2,1)S(1)}, u32[]{:S(2)}, u32[]{:S(2)}) collective-permute-start(bf16[528,128]{1,0:T(8,128)(2,1)} %get-tuple-element.55), channel_id=1, source_target_pairs={{0,16},{16,32},{32,48},{48,0},{64,80},{80,96},{96,112},{112,64},{1... | collective-permute-start | bytes 405512 | tf_op jit(solution)/shard_map/ppermute | solution.py:574
  13.1 19.4 %collective-permute-start.1 = (bf16[528,128]{1,0:T(8,128)(2,1)}, bf16[528,128]{1,0:T(8,128)(2,1)S(1)}, u32[]{:S(2)}, u32[]{:S(2)}) collective-permute-start(bf16[528,128]{1,0:T(8,128)(2,1)} %get-tuple-element.56), channel_id=1, source_target_pairs={{0,32},{16,48},{32,0},{48,16},{64,96},{80,112},{96,64},{112,80},{1... | collective-permute-start | bytes 405512 | tf_op jit(solution)/shard_map/ppermute | solution.py:574
  17.4 15.2 %collective-permute-start.2 = (bf16[528,128]{1,0:T(8,128)(2,1)}, bf16[528,128]{1,0:T(8,128)(2,1)S(1)}, u32[]{:S(2)}, u32[]{:S(2)}) collective-permute-start(bf16[528,128]{1,0:T(8,128)(2,1)} %get-tuple-element.57), channel_id=1, source_target_pairs={{0,48},{16,0},{32,16},{48,32},{64,112},{80,64},{96,80},{112,96},{1... | collective-permute-start | bytes 405512 | tf_op jit(solution)/shard_map/ppermute | solution.py:574
  32.6 7.8 %copy-start = (bf16[528,128]{1,0:T(8,128)(2,1)S(1)}, bf16[528,128]{1,0:T(8,128)(2,1)}, u32[]{:S(2)}) copy-start(bf16[528,128]{1,0:T(8,128)(2,1)} %get-tuple-element.61.refs_0_) | copy-start | bytes 405508
  32.6 57.3 %all-to-all-start = ((bf16[16,528,128]{2,1,0:T(8,128)(2,1)}), bf16[16,528,128]{2,1,0:T(8,128)(2,1)}, u32[]{:S(2)}, u32[]{:S(2)}) async-start(bf16[16,528,128]{2,1,0:T(8,128)(2,1)} %pack_b.1), calls=%async_computation | async-start | bytes 4325376 | tf_op jit(solution)/shard_map/all_to_all | solution.py:595
  41.4 17.6 %collective-permute-start.5 = (bf16[4,208,128]{2,1,0:T(8,128)(2,1)}, bf16[4,208,128]{2,1,0:T(8,128)(2,1)S(1)}, u32[]{:S(2)}, u32[]{:S(2)}) collective-permute-start(bf16[4,208,128]{2,1,0:T(8,128)(2,1)} %get-tuple-element.66), channel_id=1, source_target_pairs={{0,64},{16,80},{32,96},{48,112},{64,128},{80,144},{96,160},{112,17... | collective-permute-start | bytes 638984 | tf_op jit(solution)/shard_map/ppermute | solution.py:574
  42.2 16.7 %collective-permute-start.6 = (bf16[4,208,128]{2,1,0:T(8,128)(2,1)}, bf16[4,208,128]{2,1,0:T(8,128)(2,1)S(1)}, u32[]{:S(2)}, u32[]{:S(2)}) collective-permute-start(bf16[4,208,128]{2,1,0:T(8,128)(2,1)} %get-tuple-element.67), channel_id=1, source_target_pairs={{0,128},{16,144},{32,160},{48,176},{64,192},{80,208},{96,224},{112... | collective-permute-start | bytes 638984 | tf_op jit(solution)/shard_map/ppermute | solution.py:574
  42.8 16.5 %collective-permute-start.7 = (bf16[4,208,128]{2,1,0:T(8,128)(2,1)}, bf16[4,208,128]{2,1,0:T(8,128)(2,1)S(1)}, u32[]{:S(2)}, u32[]{:S(2)}) collective-permute-start(bf16[4,208,128]{2,1,0:T(8,128)(2,1)} %get-tuple-element.68), channel_id=1, source_target_pairs={{0,192},{16,208},{32,224},{48,240},{64,0},{80,16},{96,32},{112,48}... | collective-permute-start | bytes 638984 | tf_op jit(solution)/shard_map/ppermute | solution.py:574
  61.4 36.5 %collective-permute-start.14 = (bf16[2,64,2560]{2,1,0:T(8,128)(2,1)}, bf16[2,64,2560]{2,1,0:T(8,128)(2,1)S(1)}, u32[]{:S(2)}, u32[]{:S(2)}) collective-permute-start(bf16[2,64,2560]{2,1,0:T(8,128)(2,1)} %get-tuple-element.96), channel_id=1, source_target_pairs={{0,1},{1,2},{2,3},{3,4},{4,5},{5,6},{6,7},{7,8},{8,9},{9,10},{10,1... | collective-permute-start | bytes 1966088 | tf_op jit(solution)/shard_map/ppermute | solution.py:606
  66.1 31.8 %collective-permute-start.15 = (bf16[2,64,2560]{2,1,0:T(8,128)(2,1)}, bf16[2,64,2560]{2,1,0:T(8,128)(2,1)S(1)}, u32[]{:S(2)}, u32[]{:S(2)}) collective-permute-start(bf16[2,64,2560]{2,1,0:T(8,128)(2,1)} %get-tuple-element.97), channel_id=1, source_target_pairs={{1,0},{2,1},{3,2},{4,3},{5,4},{6,5},{7,6},{8,7},{9,8},{10,9},{11,1... | collective-permute-start | bytes 1966088 | tf_op jit(solution)/shard_map/ppermute | solution.py:605
  68.0 6.3 %collective-permute-start.8 = (bf16[4,160,128]{2,1,0:T(8,128)(2,1)S(1)}, bf16[4,160,128]{2,1,0:T(8,128)(2,1)S(1)}, u32[]{:S(2)}, u32[]{:S(2)}) collective-permute-start(bf16[4,160,128]{2,1,0:T(8,128)(2,1)S(1)} %get-tuple-element.84), channel_id=1, source_target_pairs={{0,192},{16,208},{32,224},{48,240},{64,0},{80,16},{96,32},{112,48}... | collective-permute-start | bytes 491528 | tf_op jit(solution)/shard_map/ppermute | solution.py:574
  68.1 16.5 %collective-permute-start.9 = (bf16[4,160,128]{2,1,0:T(8,128)(2,1)S(1)}, bf16[4,160,128]{2,1,0:T(8,128)(2,1)S(1)}, u32[]{:S(2)}, u32[]{:S(2)}) collective-permute-start(bf16[4,160,128]{2,1,0:T(8,128)(2,1)S(1)} %get-tuple-element.85), channel_id=1, source_target_pairs={{0,128},{16,144},{32,160},{48,176},{64,192},{80,208},{96,224},{112... | collective-permute-start | bytes 491528 | tf_op jit(solution)/shard_map/ppermute | solution.py:574
  71.9 15.9 %collective-permute-start.10 = (bf16[4,160,128]{2,1,0:T(8,128)(2,1)S(1)}, bf16[4,160,128]{2,1,0:T(8,128)(2,1)S(1)}, u32[]{:S(2)}, u32[]{:S(2)}) collective-permute-start(bf16[4,160,128]{2,1,0:T(8,128)(2,1)S(1)} %get-tuple-element.86), channel_id=1, source_target_pairs={{0,64},{16,80},{32,96},{48,112},{64,128},{80,144},{96,160},{112,17... | collective-permute-start | bytes 491528 | tf_op jit(solution)/shard_map/ppermute | solution.py:574
  87.9 0.6 copy-start.1
  97.9 18.1 %copy-start.2 = (bf16[2,64,2560]{2,1,0:T(8,128)(2,1)}, bf16[2,64,2560]{2,1,0:T(8,128)(2,1)S(1)}, u32[]{:S(2)}) copy-start(bf16[2,64,2560]{2,1,0:T(8,128)(2,1)S(1)} %collective-permute-done.14.left_ref) | copy-start | bytes 1966084
  97.9 18.0 %copy-start.3 = (bf16[2,64,2560]{2,1,0:T(8,128)(2,1)}, bf16[2,64,2560]{2,1,0:T(8,128)(2,1)S(1)}, u32[]{:S(2)}) copy-start(bf16[2,64,2560]{2,1,0:T(8,128)(2,1)S(1)} %collective-permute-done.15.right_ref) | copy-start | bytes 1966084
  98.0 56.7 %all-to-all-start.1 = ((bf16[16,384,128]{2,1,0:T(8,128)(2,1)}), bf16[16,384,128]{2,1,0:T(8,128)(2,1)}, u32[]{:S(2)}, u32[]{:S(2)}) async-start(bf16[16,384,128]{2,1,0:T(8,128)(2,1)} %head.1), calls=%async_computation.1 | async-start | bytes 3145728 | tf_op jit(solution)/shard_map/all_to_all | solution.py:613
  108.5 43.9 %collective-permute-start.11 = (bf16[384,128]{1,0:T(8,128)(2,1)S(1)}, bf16[384,128]{1,0:T(8,128)(2,1)}, u32[]{:S(2)}, u32[]{:S(2)}) collective-permute-start(bf16[384,128]{1,0:T(8,128)(2,1)S(1)} %get-tuple-element.92), channel_id=1, source_target_pairs={{0,48},{16,0},{32,16},{48,32},{64,112},{80,64},{96,80},{112,96},{1... | collective-permute-start | bytes 294920 | tf_op jit(solution)/shard_map/ppermute | solution.py:574
  111.8 40.9 %collective-permute-start.12 = (bf16[384,128]{1,0:T(8,128)(2,1)S(1)}, bf16[384,128]{1,0:T(8,128)(2,1)}, u32[]{:S(2)}, u32[]{:S(2)}) collective-permute-start(bf16[384,128]{1,0:T(8,128)(2,1)S(1)} %get-tuple-element.93), channel_id=1, source_target_pairs={{0,32},{16,48},{32,0},{48,16},{64,96},{80,112},{96,64},{112,80},{1... | collective-permute-start | bytes 294920 | tf_op jit(solution)/shard_map/ppermute | solution.py:574
  113.9 40.8 %collective-permute-start.13 = (bf16[384,128]{1,0:T(8,128)(2,1)S(1)}, bf16[384,128]{1,0:T(8,128)(2,1)}, u32[]{:S(2)}, u32[]{:S(2)}) collective-permute-start(bf16[384,128]{1,0:T(8,128)(2,1)S(1)} %get-tuple-element.94), channel_id=1, source_target_pairs={{0,16},{16,32},{32,48},{48,0},{64,80},{80,96},{96,112},{112,64},{1... | collective-permute-start | bytes 294920 | tf_op jit(solution)/shard_map/ppermute | solution.py:574
